TPU v7x, 32 devices: a whole 2x2x4 slice. The times are simulated.
32 devices in a mesh: dp: 2 (over core), context: 4 (over y, x), tensor: 4 (over z).
Axes of the slice: x: 2, y: 2, z: 4, core: 2. Of those that a mesh axis runs over, the one named last changes fastest.
Arguments:
- tokens_in: bfloat16 [8192, 768], P(('dp', 'context')), may hold values from -6 to 6
- query_weight: bfloat16 [768, 768], P(('dp', 'context'), 'tensor'), may hold values from -0.21875 to 0.21875
- key_weight: bfloat16 [768, 768], P(('dp', 'context'), 'tensor'), may hold values from -0.21875 to 0.21875
- value_weight: bfloat16 [768, 768], P(('dp', 'context'), 'tensor'), may hold values from -0.21875 to 0.21875
- output_weight: bfloat16 [768, 768], P('tensor', ('dp', 'context')), may hold values from -0.875 to 0.875
- bias_table: float32 [32, 12], P(None, 'tensor'), may hold values from -4 to 4
- attention_gain: bfloat16 [768], P(('dp', 'context')), may hold values from 0.5 to 1.5
- router_weight: bfloat16 [768, 8], P(('dp', 'context')), may hold values from -0.21875 to 0.21875
- expert_gain: bfloat16 [768], P(('dp', 'context')), may hold values from 0.5 to 1.5
- expert_in: bfloat16 [8, 768, 3072], P(('dp', 'context'), None, 'tensor'), may hold values from -0.21875 to 0.21875
- expert_out: bfloat16 [8, 3072, 768], P(('dp', 'context'), 'tensor'), may hold values from -0.15625 to 0.15625
- routes: int32 [8192, 2], P(('dp', 'context')), may hold values from 0 to 7, all different within a row
- pair_order: int32 [8, 2048], P(('dp', 'context')), may hold values from 0 to 2047, each once within a row
- seq_lengths: int32 [2, 2], P('dp'), may hold values from 1 to 4095, as said below
- cotangent: bfloat16 [8192, 768], P(('dp', 'context')), may hold values from -6 to 6
Outputs:
- layer_out: bfloat16 [8192, 768], P(('dp', 'context'))
- input_grad: float32 [8192, 768], P(('dp', 'context'))
- query_grad: float32 [768, 768], P(('dp', 'context'), 'tensor')
- key_grad: float32 [768, 768], P(('dp', 'context'), 'tensor')
- value_grad: float32 [768, 768], P(('dp', 'context'), 'tensor')
- output_grad: float32 [768, 768], P('tensor', ('dp', 'context'))
- table_grad: float32 [32, 12], P(None, 'tensor')
- attention_gain_grad: float32 [768], P(('dp', 'context'))
- router_grad: float32 [768, 8], P(('dp', 'context'))
- expert_gain_grad: float32 [768], P(('dp', 'context'))
- expert_in_grad: float32 [8, 768, 3072], P(('dp', 'context'), None, 'tensor')
- expert_out_grad: float32 [8, 3072, 768], P(('dp', 'context'), 'tensor')
Inputs may be any that keep to these rules, and one draw needn't show every extreme that they name: `pair_order`: row b lists the (2048) pairs of block b of tokens, pair 2 t + k for local token t and route k, in the order in which they take slots. `seq_lengths`: row g gives the lengths of the two sequences of token group g, packed from the group's first position, with padding after them; their sum is at most 4096; one of them (which one is drawn) is longer than (3) * 1024, the other at most 512.
All inputs are finite; a program needn't handle non-finite values.
Results may differ from a plain program's by a relative error of at most 0.014.
Values may be sent and summed in bfloat16 or wider, within the bound.
No kernel may reach another device: no remote copies, remote signals or barrier semaphores. Data moves between devices by JAX's collectives and lax.ppermute only.
A program may use at most 448 MiB of HBM per device.

v0:
```python
import functools
import jax
import jax.numpy as jnp
import numpy as np
from jax import lax
from jax.experimental import pallas as pl
from jax.experimental.pallas import tpu as pltpu
from jax.sharding import PartitionSpec as P

bf16 = jnp.bfloat16
f32 = jnp.float32
epsilon = 1e-06
masked_value = -1e30
tile = 256
VMEM = pl.BlockSpec(memory_space=pltpu.VMEM)
SMEM = pl.BlockSpec(memory_space=pltpu.SMEM)


def dot_nn(a, b):
    return lax.dot_general(a, b, (((1,), (0,)), ((), ())), preferred_element_type=f32)


def dot_nt(a, b):
    return lax.dot_general(a, b, (((1,), (1,)), ((), ())), preferred_element_type=f32)


def dot_tn(a, b):
    return lax.dot_general(a, b, (((0,), (0,)), ((), ())), preferred_element_type=f32)


def start_of(position, first_end, second_end):
    return jnp.where(
        position >= second_end, second_end, jnp.where(position >= first_end, first_end, 0)
    )


def aligned(value, size):
    return pl.multiple_of(value, size)


def attention_forward_kernel(
    heads, width, scalars, far_bias, offsets, query_ref, bias_ref, *rest
):
    piece_count = len(rest) - 9
    pieces = rest[:piece_count]
    packed_one, packed_two, lse_ref, keys_values = rest[piece_count : piece_count + 4]
    values_t, best, running, side_one, side_two = rest[piece_count + 4 :]
    rows = query_ref.shape[0]
    context, first_end, second_end = scalars[0], scalars[1], scalars[2]
    for index, piece in enumerate(pieces):
        size = piece.shape[0]
        keys_values[pl.ds(aligned(offsets[index], 128), size), :] = piece[...]
    lane_q = lax.broadcasted_iota(jnp.int32, (tile, 256), 1)

    def transpose_values(index, carry):
        start = aligned(index * tile, tile)
        upper = keys_values[pl.ds(start, tile), 256:384].astype(f32).T.astype(bf16)
        lower = keys_values[pl.ds(start, tile), 128:256].astype(f32).T.astype(bf16)
        values_t[0, 0:width, pl.ds(start, tile)] = upper[0:width]
        values_t[1, 0:width, pl.ds(start, tile)] = upper[width:]
        values_t[2, 0:width, pl.ds(start, tile)] = lower[width:]
        for head in range(heads):
            values_t[head, width:, pl.ds(start, tile)] = jnp.ones((16, tile), bf16)
        return carry

    lax.fori_loop(0, (context + 1) * (rows // tile), transpose_values, 0)

    def query_tile(index, carry):
        local = aligned(index * tile, tile)
        first = aligned(context * rows + local, tile)
        positions = first + lax.broadcasted_iota(jnp.int32, (1, tile), 1)
        row_start = start_of(positions, first_end, second_end)
        start_first = start_of(first, first_end, second_end)
        start_last = start_of(first + tile - 1, first_end, second_end)
        queries = query_ref[pl.ds(local, tile), :]
        masked_queries = [
            jnp.where(lane_q // width == head, queries, jnp.zeros_like(queries))
            for head in range(heads)
        ]

        def absorb(key_start, size, bias_index, masked, first_time):
            keys = keys_values[pl.ds(key_start, size), 0:256]
            if masked:
                key_positions = key_start + lax.broadcasted_iota(jnp.int32, (size, tile), 0)
                seen = key_positions >= row_start
                if bias_index == 0:
                    seen = seen & (key_positions <= positions)
            for head in range(heads):
                scores = dot_nt(keys, masked_queries[head])
                shift = 0.0
                if bias_index is None:
                    shift = far_bias[head]
                else:
                    scores = scores + bias_ref[bias_index, head]
                if masked:
                    scores = jnp.where(seen, scores, masked_value)
                top = jnp.max(scores, axis=0, keepdims=True) + shift
                values = values_t[head, :, pl.ds(key_start, size)]
                if first_time:
                    weights = jnp.exp(scores - top).astype(bf16)
                    running[head] = dot_nn(values, weights)
                    best[head] = jnp.broadcast_to(top, (8, tile))
                else:
                    old = best[head, 0:1]
                    new = jnp.maximum(old, top)
                    weights = jnp.exp(scores - (new - shift)).astype(bf16)
                    running[head] = running[head] * jnp.exp(old - new) + dot_nn(values, weights)
                    best[head] = jnp.broadcast_to(new, (8, tile))

        absorb(first, tile, 0, True, True)

        @pl.when(first > 0)
        def _():
            absorb(aligned(first - tile, tile), tile, 1, True, False)

        far_rows = jnp.maximum(first - tile, 0)
        big = 2 * tile
        big_count = far_rows // big
        low = jnp.minimum(start_first // big, big_count)
        middle = jnp.clip((start_last + big - 1) // big, low, big_count)

        def masked_step(step, carry):
            absorb(aligned(step * big, big), big, None, True, False)
            return carry

        def plain_step(step, carry):
            absorb(aligned(step * big, big), big, None, False, False)
            return carry

        lax.fori_loop(low, middle, masked_step, 0)
        lax.fori_loop(middle, big_count, plain_step, 0)

        @pl.when(far_rows > big_count * big)
        def _():
            absorb(aligned(big_count * big, tile), tile, None, True, False)

        outs = []
        for head in range(heads):
            total = running[head, width : width + 1]
            outs.append(running[head, 0:width] / total)
            lse_ref[pl.ds(head, 1), pl.ds(local, tile)] = best[head, 0:1] + jnp.log(total)
        side_one[pl.ds(local, tile), :] = jnp.concatenate([outs[0], outs[1]], axis=0).T
        side_two[pl.ds(local, tile), :] = jnp.concatenate([outs[2], outs[2]], axis=0).T
        return carry

    lax.fori_loop(0, rows // tile, query_tile, 0)
    half, quarter = rows // 2, rows // 4
    lane = lax.broadcasted_iota(jnp.int32, (quarter, 128), 1)
    for part, packed in enumerate((packed_one, packed_two)):
        near = slice(part * quarter, (part + 1) * quarter)
        later = slice(half + part * quarter, half + (part + 1) * quarter)
        packed[:, 0:128] = side_one[near, :].astype(bf16)
        packed[:, 128:256] = jnp.where(
            lane < width, side_two[near, :], side_two[later, :]
        ).astype(bf16)
        packed[:, 256:384] = side_one[later, :].astype(bf16)


def attention_forward(scalars, far_bias, offsets, queries, bias_tiles, pieces, group_rows, heads, width):
    rows = queries.shape[0]
    return pl.pallas_call(
        functools.partial(attention_forward_kernel, heads, width),
        out_shape=(
            jax.ShapeDtypeStruct((rows // 4, 384), bf16),
            jax.ShapeDtypeStruct((rows // 4, 384), bf16),
            jax.ShapeDtypeStruct((8, rows), f32),
            jax.ShapeDtypeStruct((group_rows, 384), bf16),
        ),
        in_specs=[SMEM, SMEM, SMEM, VMEM, VMEM] + [VMEM] * len(pieces),
        out_specs=(VMEM,) * 4,
        scratch_shapes=[
            pltpu.VMEM((heads, width + 16, group_rows), bf16),
            pltpu.VMEM((heads, 8, tile), f32),
            pltpu.VMEM((heads, width + 16, tile), f32),
            pltpu.VMEM((rows, 128), f32),
            pltpu.VMEM((rows, 128), f32),
        ],
        compiler_params=pltpu.CompilerParams(vmem_limit_bytes=56 * 2**20),
        cost_estimate=pl.CostEstimate(
            flops=4 * rows * group_rows * 256 * heads,
            bytes_accessed=10 * 2**20,
            transcendentals=rows * group_rows * heads,
        ),
        name="attention_forward",
    )(scalars, far_bias, offsets, queries, bias_tiles, *pieces)


def attention_backward_kernel(
    heads, width, piece_count, scalars, far_bias, offsets,
    query_ref, keys_values, bias_ref, lse_ref, packed_one, packed_two, output_ref, *rest
):
    pieces = rest[:piece_count]
    (
        dq_ref, own_ref, beside_one, beside_two, across_one, across_two, far_one, far_two, fold_ref
    ) = rest[piece_count : piece_count + 9]
    grad_branch, dout, masked_q, masked_o, keys_t, deltas, dq_t, dk, dv, dkv, band_ref = rest[
        piece_count + 9 :
    ]
    rows = query_ref.shape[0]
    half, quarter = rows // 2, rows // 4
    context, first_end, second_end = scalars[0], scalars[1], scalars[2]
    tiles_here = rows // tile
    for index, piece in enumerate(pieces):
        grad_branch[pl.ds(aligned(offsets[index], 128), piece.shape[0]), :] = piece[...]
    lane_low = lax.broadcasted_iota(jnp.int32, (output_ref.shape[0], 128), 1)
    last_head = jnp.where(lane_low < width, output_ref[:, 128:256].astype(f32), 0.0)
    ordered = jnp.concatenate(
        [pltpu.roll(last_head, width, 1).astype(bf16), output_ref[:, 0:128]], axis=1
    )
    dout[...] = dot_nn(grad_branch[...], ordered).astype(bf16)
    head_row = lax.broadcasted_iota(jnp.int32, (16, 256), 0)
    head_lane = lax.broadcasted_iota(jnp.int32, (16, 256), 1) // width
    head_hot = (head_row == jnp.where(head_lane == 1, 2, head_lane - 2)).astype(bf16)
    for part in range(4):
        span = slice(part * quarter, (part + 1) * quarter)
        packed = packed_one if part % 2 == 0 else packed_two
        lower = packed[:, 128:256].astype(f32)
        if part < 2:
            upper, lower = packed[:, 0:128], pltpu.roll(lower, width, 1)
        else:
            upper = packed[:, 256:384]
        product = dout[span, :].astype(f32) * jnp.concatenate([lower, upper.astype(f32)], axis=1)
        high = product.astype(bf16)
        rest_part = (product - high.astype(f32)).astype(bf16)
        deltas[:, span] = dot_nt(head_hot, high) + dot_nt(head_hot, rest_part)
    lane = lax.broadcasted_iota(jnp.int32, (rows, 256), 1) // width
    for head in range(heads):
        masked_q[head] = jnp.where(lane == head, query_ref[...], jnp.zeros((rows, 256), bf16))
        slot = 1 if head == 2 else head + 2
        masked_o[head] = jnp.where(lane == slot, dout[...], jnp.zeros((rows, 256), bf16))

    def transpose_keys(index, carry):
        start = aligned(index * tile, tile)
        lower = keys_values[pl.ds(start, tile), 0:128].astype(f32).T.astype(bf16)
        upper = keys_values[pl.ds(start, tile), 128:256].astype(f32).T.astype(bf16)
        keys_t[0, :, pl.ds(start, tile)] = lower[0:width]
        keys_t[1, :, pl.ds(start, tile)] = lower[width:]
        keys_t[2, :, pl.ds(start, tile)] = upper[0:width]
        return carry

    lax.fori_loop(0, (context + 1) * tiles_here, transpose_keys, 0)
    dq_t[...] = jnp.zeros_like(dq_t)
    dkv[...] = jnp.zeros_like(dkv)
    band_ref[...] = jnp.zeros_like(band_ref)
    first = context * rows
    all_positions = first + lax.broadcasted_iota(jnp.int32, (1, rows), 1)
    all_starts = start_of(all_positions, first_end, second_end)
    start_first = start_of(first, first_end, second_end)
    start_last = start_of(first + rows - 1, first_end, second_end)

    def block(key_start, query_start, size, bias_index, masked, near):
        keys = keys_values[pl.ds(key_start, tile), 0:256]
        values = keys_values[pl.ds(key_start, tile), 128:384]
        key_sum, value_sum = None, None
        if masked:
            key_positions = key_start + lax.broadcasted_iota(jnp.int32, (tile, size), 0)
            if near:
                positions = (
                    first + query_start + lax.broadcasted_iota(jnp.int32, (1, size), 1)
                )
                seen = (key_positions >= start_of(positions, first_end, second_end)) & (
                    key_positions <= positions
                )
            else:
                seen = key_positions >= all_starts
        span = pl.ds(query_start, size)
        for head in range(heads):
            queries = masked_q[head, span, :]
            grads = masked_o[head, span, :]
            scores = dot_nt(keys, queries)
            lse = lse_ref[pl.ds(head, 1), span]
            if near:
                scores = scores + bias_ref[bias_index, head]
            else:
                lse = lse - far_bias[head]
            probs = jnp.exp(scores - lse)
            if masked:
                probs = jnp.where(seen, probs, 0.0)
            grad_probs = dot_nt(values, grads)
            grad_scores = probs * (grad_probs - deltas[pl.ds(head, 1), span])
            if near:

                @pl.when(bias_index < 2)
                def _():
                    band_ref[bias_index, head] += grad_scores

            low_scores = grad_scores.astype(bf16)
            value_part = dot_nn(probs.astype(bf16), grads)
            key_part = dot_nn(low_scores, queries)
            dq_t[head, :, span] += dot_nn(keys_t[head, :, pl.ds(key_start, tile)], low_scores)
            key_sum = key_part if key_sum is None else key_sum + key_part
            value_sum = value_part if value_sum is None else value_sum + value_part
        return key_sum, value_sum

    lane_tile = lax.broadcasted_iota(jnp.int32, (tile, 128), 1)

    def write(key_start, key_sum, value_sum):
        span = pl.ds(key_start, tile)
        dkv[span, 0:128] = key_sum[:, 0:128].astype(bf16)
        dkv[span, 128:256] = jnp.where(
            lane_tile < width, key_sum[:, 128:256], value_sum[:, 0:128]
        ).astype(bf16)
        dkv[span, 256:384] = value_sum[:, 128:256].astype(bf16)

    far_count = jnp.maximum(context * tiles_here - 1, 0)
    low = jnp.minimum(start_first // tile, far_count)
    middle = jnp.clip((start_last + tile - 1) // tile, low, far_count)

    def masked_step(index, carry):
        start = aligned(index * tile, tile)
        write(start, *block(start, 0, rows, None, True, False))
        return carry

    def plain_step(index, carry):
        start = aligned(index * tile, tile)
        write(start, *block(start, 0, rows, None, False, False))
        return carry

    lax.fori_loop(low, middle, masked_step, 0)
    lax.fori_loop(middle, far_count, plain_step, 0)

    def near_keys(index, carry):
        start = aligned(index * tile, tile)
        lag = index - context * tiles_here
        dk[...] = jnp.zeros_like(dk)
        dv[...] = jnp.zeros_like(dv)

        def near_queries(query, inner):
            bias_index = jnp.minimum(query - lag, 2)
            key_sum, value_sum = block(
                start, aligned(query * tile, tile), tile, bias_index, True, True
            )
            dk[...] += key_sum
            dv[...] += value_sum
            return inner

        lax.fori_loop(jnp.maximum(lag, 0), tiles_here, near_queries, 0)
        write(start, dk[...], dv[...])
        return carry

    lax.fori_loop(far_count, (context + 1) * tiles_here, near_keys, 0)

    def block_rows(which):
        return pl.ds(aligned(which * rows, rows), rows)

    own_ref[...] = dkv[block_rows(context), :]
    for which, first_half, second_half in (
        (1, beside_one, beside_two), (2, across_one, across_two), (3, far_one, far_two)
    ):
        start = (context ^ which) * rows
        first_half[...] = dkv[pl.ds(aligned(start, half), half), :]
        second_half[...] = dkv[pl.ds(aligned(start + half, half), half), :]
    key_index = lax.broadcasted_iota(jnp.int32, (tile, tile), 0)
    query_index = lax.broadcasted_iota(jnp.int32, (tile, tile), 1)
    fold_ref[...] = jnp.zeros_like(fold_ref)
    for head in range(heads):
        both = jnp.where(key_index > query_index, band_ref[1, head], band_ref[0, head])
        by_row = both[0:8]
        for first_row in range(8, tile, 8):
            by_row = by_row + pltpu.roll(both[first_row : first_row + 8], tile - first_row, 1)
        folded = by_row[0:1]
        for row in range(1, 8):
            folded = folded + pltpu.roll(by_row, tile - row, 1)[row : row + 1]
        fold_ref[head : head + 1, :] = folded
    upper = jnp.concatenate([dq_t[0], dq_t[1]], axis=0)
    lower = jnp.concatenate([dq_t[2], jnp.zeros((width, rows), f32)], axis=0)
    scale = width ** (-0.5)
    dq_ref[:, 0:128] = (upper.T * scale).astype(bf16)
    dq_ref[:, 128:256] = (lower.T * scale).astype(bf16)


def attention_backward(
    scalars, far_bias, offsets, queries, keys_values, bias_tiles, lse, packed, output_part, pieces, heads, width
):
    rows = queries.shape[0]
    half = rows // 2
    group_rows = keys_values.shape[0]
    model = output_part.shape[0]
    shape = jax.ShapeDtypeStruct
    return pl.pallas_call(
        functools.partial(attention_backward_kernel, heads, width, len(pieces)),
        out_shape=(
            shape((rows, 256), bf16),
            shape((rows, 384), bf16),
        )
        + (shape((half, 384), bf16),) * 6
        + (shape((8, tile), f32),),
        in_specs=[SMEM, SMEM, SMEM] + [VMEM] * (7 + len(pieces)),
        out_specs=(VMEM,) * 9,
        scratch_shapes=[
            pltpu.VMEM((rows, model), bf16),
            pltpu.VMEM((rows, 256), bf16),
            pltpu.VMEM((heads, rows, 256), bf16),
            pltpu.VMEM((heads, rows, 256), bf16),
            pltpu.VMEM((heads, width, group_rows), bf16),
            pltpu.VMEM((16, rows), f32),
            pltpu.VMEM((heads, width, rows), f32),
            pltpu.VMEM((tile, 256), f32),
            pltpu.VMEM((tile, 256), f32),
            pltpu.VMEM((group_rows, 384), bf16),
            pltpu.VMEM((2, heads, tile, tile), f32),
        ],
        compiler_params=pltpu.CompilerParams(vmem_limit_bytes=60 * 2**20),
        cost_estimate=pl.CostEstimate(
            flops=10 * rows * group_rows * 256 * heads,
            bytes_accessed=16 * 2**20,
            transcendentals=rows * group_rows * heads,
        ),
        name="attention_backward",
    )(scalars, far_bias, offsets, queries, keys_values, bias_tiles, lse, *packed, output_part, *pieces)


bucket_edges = np.array(
    [19, 21, 24, 27, 31, 35, 40, 46, 52, 59, 67, 77, 87, 99, 113], dtype=np.int32
)


def bucket_tiles():
    key = np.arange(tile)[None, :, None]
    query = np.arange(tile)[None, None, :]
    lag = np.arange(3)[:, None, None] * tile + query - key
    clipped = np.maximum(lag, 0)
    counted = (clipped[..., None] >= bucket_edges).sum(-1)
    return np.where(clipped < 16, clipped, 16 + counted).astype(np.int32)


def bias_of(table, buckets):
    out = jnp.broadcast_to(table[0][None, :, None, None], (buckets.shape[0], table.shape[1]) + buckets.shape[1:])
    for b in range(1, table.shape[0]):
        out = jnp.where(buckets[:, None] >= b, table[b][None, :, None, None], out)
    return out


def shape(dims, dtype):
    return jax.ShapeDtypeStruct(dims, dtype)


def params(mebibytes):
    return pltpu.CompilerParams(vmem_limit_bytes=mebibytes * 2**20)


def cost(flops, bytes_accessed):
    return pl.CostEstimate(flops=flops, bytes_accessed=bytes_accessed, transcendentals=0)


def gelu_constants():
    return 0.7978845608028654, 0.044715


def place_kernel(capacity, scalars, route_ref, order_ref, rows_ref, columns_ref, ranks, hot_ref, tall):
    pair_count = order_ref.shape[1]
    rows = pair_count // 2
    expert_pad = hot_ref.shape[0]
    step = 256
    live_end = scalars[2] - scalars[0] * rows
    order = order_ref[...]
    index_row = lax.broadcasted_iota(jnp.int32, (pair_count, 128), 0)
    index_lane = lax.broadcasted_iota(jnp.int32, (pair_count, 128), 1)
    digits = jnp.where(
        index_lane == 0, index_row // 64, jnp.where(index_lane == 1, index_row % 64, 0)
    ).astype(f32).astype(bf16)

    def rank_step(index, carry):
        start = aligned(index * step, step)
        pair = start + lax.broadcasted_iota(jnp.int32, (step, pair_count), 0)
        hit = (pair == order).astype(f32).astype(bf16)
        found = dot_nn(hit, digits)
        rank = found[:, 0:1] * 64.0 + found[:, 1:2]
        ranks[pl.ds(start, step), :] = jnp.broadcast_to(rank, (step, 128))
        return carry

    lax.fori_loop(0, pair_count // step, rank_step, 0)
    rank_row = ranks[...].T[0:1, :]
    position = lax.broadcasted_iota(jnp.int32, (1, rows), 1)
    live = position < live_end
    expert_row = jnp.concatenate([route_ref[0:1, :], route_ref[1:2, :]], axis=1)
    live_row = jnp.concatenate([live, live], axis=1)
    expert_index = lax.broadcasted_iota(jnp.int32, (expert_pad, pair_count), 0)
    hot = ((expert_index == expert_row) & live_row).astype(f32)
    hot_ref[...] = hot.astype(bf16)

    def count_step(index, counts):
        start = aligned(index * step, step)
        earlier = (ranks[pl.ds(start, step), 0:1] < rank_row).astype(f32).astype(bf16)
        return counts + dot_nn(hot_ref[:, pl.ds(start, step)], earlier)

    counts = lax.fori_loop(
        0, pair_count // step, count_step, jnp.zeros((expert_pad, pair_count), f32)
    )
    slot = jnp.sum(counts * hot, axis=0, keepdims=True).astype(jnp.int32)
    place = jnp.where(live_row & (slot < capacity), expert_row * capacity + slot, -1)
    rows_ref[...] = jnp.full_like(rows_ref, -1)
    rows_ref[0:1, :] = place[:, 0:rows]
    rows_ref[1:2, :] = place[:, rows:]
    tall[...] = jnp.full_like(tall, -1.0)
    tall[0:1, :] = place[:, 0:rows].astype(f32)
    tall[1:2, :] = place[:, rows:].astype(f32)
    columns_ref[...] = tall[...].T.astype(jnp.int32)


def find_places(scalars, route_rows, order_row, expert_count, capacity):
    rows = route_rows.shape[1]
    expert_pad = max(16, expert_count)
    return pl.pallas_call(
        functools.partial(place_kernel, capacity),
        out_shape=(shape((8, rows), jnp.int32), shape((rows, 128), jnp.int32)),
        in_specs=[SMEM, VMEM, VMEM],
        out_specs=(VMEM, VMEM),
        scratch_shapes=[
            pltpu.VMEM((2 * rows, 128), f32),
            pltpu.VMEM((expert_pad, 2 * rows), bf16),
            pltpu.VMEM((128, rows), f32),
        ],
        compiler_params=params(40),
        cost_estimate=cost(4 * 4 * rows * rows * 128, 2**20),
        name="find_places",
    )(scalars, route_rows, order_row)


def project_kernel(piece_count, offsets, token_ref, *rest):
    pieces = rest[:piece_count]
    hidden_ref, query_ref, kv_one, kv_two, weight_ref, gain_ref = rest[piece_count:]
    for index, piece in enumerate(pieces):
        weight_ref[pl.ds(aligned(offsets[index], 16), piece.shape[0]), :] = piece[...]
    rows = token_ref.shape[0]
    half = rows // 2
    gains = weight_ref[:, 128:256].astype(f32).T
    gain_ref[0:1, :] = gains[64:65, :]
    gain_ref[1:2, :] = gains[65:66, :]
    step = 256
    lane = lax.broadcasted_iota(jnp.int32, (step, 256), 1)
    for start in range(0, rows, step):
        inputs = token_ref[start : start + step, :].astype(f32)
        scale = lax.rsqrt(jnp.mean(inputs * inputs, axis=-1, keepdims=True) + epsilon)
        hidden = (inputs * scale * gain_ref[0:1, :]).astype(bf16)
        hidden_ref[start : start + step, :] = hidden
        queries = dot_nn(hidden, weight_ref[:, 0:256]).astype(bf16)
        query_ref[start : start + step, :] = jnp.where(
            lane < 192, queries * bf16(0.125), jnp.zeros_like(queries)
        )
        target, base = (kv_one, 0) if start < half else (kv_two, half)
        target[start - base : start - base + step, :] = dot_nn(
            hidden, weight_ref[:, 256:640]
        ).astype(bf16)


def project(offsets, tokens, pieces):
    rows, model = tokens.shape
    return pl.pallas_call(
        functools.partial(project_kernel, len(pieces)),
        out_shape=(
            shape((rows, model), bf16),
            shape((rows, 256), bf16),
            shape((rows // 2, 384), bf16),
            shape((rows // 2, 384), bf16),
            shape((model, 640), bf16),
            shape((8, model), f32),
        ),
        in_specs=[SMEM, VMEM] + [VMEM] * len(pieces),
        out_specs=(VMEM,) * 6,
        compiler_params=params(40),
        cost_estimate=cost(2 * rows * model * 640, 6 * 2**20),
        name="project",
    )(offsets, tokens, *pieces)


def assemble_kernel(piece_count, offsets, *rest):
    pieces = rest[:piece_count]
    out_ref = rest[piece_count]
    for index, piece in enumerate(pieces):
        size = piece.shape[0]
        out_ref[pl.ds(aligned(offsets[index], 16), size), :] = piece[...].astype(out_ref.dtype)


def assemble(offsets, pieces, dtype):
    total = sum(piece.shape[0] for piece in pieces)
    width = pieces[0].shape[1]
    return pl.pallas_call(
        functools.partial(assemble_kernel, len(pieces)),
        out_shape=shape((total, width), dtype),
        in_specs=[SMEM] + [VMEM] * len(pieces),
        out_specs=VMEM,
        compiler_params=params(40),
        cost_estimate=cost(0, 6 * total * width),
        name="assemble",
    )(offsets, *pieces)


def dispatch_kernel(
    heads, width, capacity, expert_count, chunk_count, scalars, starts,
    token_ref, gain_ref, route_ref, row_place, *rest
):
    attended = rest[0:8]
    weights = rest[8:12]
    residual_ref, hidden_ref, info_ref = rest[12:15]
    chunks = rest[15 : 15 + chunk_count]
    packed, joined, column = rest[15 + chunk_count :]
    rows, model = token_ref.shape
    quarter = rows // 4
    lane_low = lax.broadcasted_iota(jnp.int32, (quarter, 128), 1)
    for source in range(4):
        for part in range(2):
            piece = attended[2 * source + part]
            span = slice(part * quarter, (part + 1) * quarter)
            middle = piece[:, 128:256].astype(f32)
            packed[source, span, 0:128] = piece[:, 0:128]
            packed[source, span, 128:256] = jnp.where(lane_low < width, middle, 0.0).astype(bf16)
            span = slice((part + 2) * quarter, (part + 3) * quarter)
            packed[source, span, 0:128] = piece[:, 256:384]
            packed[source, span, 128:256] = jnp.where(
                lane_low < width, pltpu.roll(middle, 64, 1), 0.0
            ).astype(bf16)
    step = 256
    lane = lax.broadcasted_iota(jnp.int32, (step, 128), 1)
    valid = (lane >= 64) & (lane < 64 + expert_count)

    def token_step(index, carry):
        start = aligned(index * step, step)
        span = pl.ds(start, step)
        residual = token_ref[span, :].astype(f32)
        for source in range(4):
            residual = residual + dot_nt(packed[source, span, :], weights[source][...])
        joined[span, :] = residual
        scale = lax.rsqrt(jnp.mean(residual * residual, axis=-1, keepdims=True) + epsilon)
        hidden = (residual * scale * gain_ref[1:2, :]).astype(bf16)
        hidden_ref[span, :] = hidden
        logits = dot_nn(hidden, weights[0][:, 128:256])
        logits = jnp.where(valid, logits, masked_value)
        powers = jnp.where(valid, jnp.exp(logits - jnp.max(logits, axis=-1, keepdims=True)), 0.0)
        probs = powers / jnp.sum(powers, axis=-1, keepdims=True)
        first = jnp.sum(
            jnp.where(lane == route_ref[span, 0:1] + 64, probs, 0.0), axis=-1, keepdims=True
        )
        second = jnp.sum(
            jnp.where(lane == route_ref[span, 1:2] + 64, probs, 0.0), axis=-1, keepdims=True
        )
        total = first + second
        info_ref[span, :] = jnp.where(
            lane == 0,
            first / total,
            jnp.where(lane == 1, second / total, jnp.where(lane == 2, total, probs)),
        )
        return carry

    lax.fori_loop(0, rows // step, token_step, 0)
    residual_ref[...] = joined[pl.ds(aligned(scalars[3] * quarter, quarter), quarter), :]
    gates = info_ref[...].T
    gate_one, gate_two = gates[0:1, :], gates[1:2, :]
    place_one, place_two = row_place[0:1, :], row_place[1:2, :]
    slot = lax.broadcasted_iota(jnp.int32, (capacity, rows), 0)
    column[...] = jnp.zeros_like(column)

    def fill(chunk, entry, expert):
        base = expert * capacity
        hit_one = slot == place_one - base
        hit_two = slot == place_two - base
        picked = jnp.where(hit_one | hit_two, 1.0, 0.0).astype(bf16)
        chunk[entry, 16:, :] = dot_nn(picked, hidden_ref[...]).astype(bf16)
        gate = jnp.where(hit_one, gate_one, 0.0) + jnp.where(hit_two, gate_two, 0.0)
        gate = jnp.sum(gate, axis=-1, keepdims=True)
        column[0:capacity, :] = jnp.broadcast_to(gate, (capacity, 128))
        write_head(chunk, entry, column[...].T[0:1, :])

    for chunk_index, chunk in enumerate(chunks):
        if chunk.shape[0] == 1:
            fill(chunk, 0, starts[chunk_index])
        else:

            def one(entry, carry):
                fill(chunk, entry, starts[chunk_index] + entry)
                return carry

            lax.fori_loop(0, chunk.shape[0], one, 0)


def write_head(chunk, entry, row):
    high = row.astype(bf16)
    left = row - high.astype(f32)
    middle = left.astype(bf16)
    low = (left - middle.astype(f32)).astype(bf16)
    size = row.shape[1]
    index = lax.broadcasted_iota(jnp.int32, (16, size), 0)
    block = jnp.where(
        index == 0,
        high.astype(f32),
        jnp.where(index == 1, middle.astype(f32), jnp.where(index == 2, low.astype(f32), 0.0)),
    )
    chunk[entry, 0:16, :] = jnp.zeros((16, chunk.shape[2]), bf16)
    chunk[entry, 0:16, 0:size] = block.astype(bf16)


def dispatch(
    scalars, starts, tokens, gains, routes, row_place, attended, weights, chunk_shapes,
    heads, width, capacity, expert_count
):
    rows, model = tokens.shape
    pad = (capacity + 127) // 128 * 128
    return pl.pallas_call(
        functools.partial(
            dispatch_kernel, heads, width, capacity, expert_count, len(chunk_shapes)
        ),
        out_shape=(
            shape((rows // 4, model), f32),
            shape((rows, model), bf16),
            shape((rows, 128), f32),
        )
        + tuple(shape((per, capacity + 16, model), bf16) for per in chunk_shapes),
        in_specs=[SMEM, SMEM] + [VMEM] * 16,
        out_specs=(VMEM,) * (3 + len(chunk_shapes)),
        scratch_shapes=[
            pltpu.VMEM((4, rows, 256), bf16),
            pltpu.VMEM((rows, model), f32),
            pltpu.VMEM((pad, 128), f32),
        ],
        compiler_params=params(56),
        cost_estimate=cost(2 * rows * model * (1024 + 2304), 16 * 2**20),
        name="dispatch",
    )(scalars, starts, tokens, gains, routes, row_place, *attended, *weights)


def scatter_kernel(capacity, chunk_count, starts, value_ref, row_place, *chunks):
    rows = value_ref.shape[0]
    place_one, place_two = row_place[0:1, :], row_place[1:2, :]
    slot = lax.broadcasted_iota(jnp.int32, (capacity, rows), 0)

    def fill(chunk, entry, expert):
        base = expert * capacity
        hit = (slot == place_one - base) | (slot == place_two - base)
        picked = jnp.where(hit, 1.0, 0.0).astype(bf16)
        chunk[entry] = dot_nn(picked, value_ref[...]).astype(bf16)

    for chunk_index, chunk in enumerate(chunks):
        if chunk.shape[0] == 1:
            fill(chunk, 0, starts[chunk_index])
        else:

            def one(entry, carry):
                fill(chunk, entry, starts[chunk_index] + entry)
                return carry

            lax.fori_loop(0, chunk.shape[0], one, 0)


def scatter_rows(starts, values, row_place, chunk_shapes, capacity):
    rows, model = values.shape
    return pl.pallas_call(
        functools.partial(scatter_kernel, capacity, len(chunk_shapes)),
        out_shape=tuple(shape((per, capacity, model), bf16) for per in chunk_shapes),
        in_specs=[SMEM, VMEM, VMEM],
        out_specs=(VMEM,) * len(chunk_shapes),
        compiler_params=params(40),
        cost_estimate=cost(2 * rows * model * 2304, 6 * 2**20),
        name="scatter_rows",
    )(starts, values, row_place)


def expert_kernel(chunk_count, in_ref, out_ref, *rest):
    row_chunks = rest[:chunk_count]
    grad_chunks = rest[chunk_count : 2 * chunk_count]
    rows_all, grads_all, acted_all, pre_all = rest[2 * chunk_count : 2 * chunk_count + 4]
    returns = rest[2 * chunk_count + 4 : 3 * chunk_count + 4]
    held, column = rest[3 * chunk_count + 4 :]
    source_count, capacity, model = rows_all.shape
    root, cubic = gelu_constants()
    at = 0
    for chunk, grads in zip(row_chunks, grad_chunks):
        per = chunk.shape[0]
        rows_all[at : at + per] = chunk[:, 16:, :]
        grads_all[at : at + per] = grads[...]
        at += per
    column[...] = jnp.zeros_like(column)

    def one(source, carry):
        pre = dot_nn(rows_all[source], in_ref[0])
        square = pre * pre
        bent = jnp.tanh(root * pre * (1.0 + cubic * square))
        acted = (0.5 * pre * (1.0 + bent)).astype(bf16)
        slope = 0.5 * (1.0 + bent) + 0.5 * pre * (1.0 - bent * bent) * root * (
            1.0 + 3.0 * cubic * square
        )
        grad_acted = dot_nt(grads_all[source], out_ref[0])
        acted_all[source] = acted
        gate_grad = jnp.sum(grad_acted * acted.astype(f32), axis=-1, keepdims=True)
        column[0:capacity, :] = jnp.broadcast_to(gate_grad, (capacity, 128))
        grad_pre = (grad_acted * slope).astype(bf16)
        pre_all[source] = grad_pre
        held[source, 16:, :] = dot_nt(grad_pre, in_ref[0]).astype(bf16)
        write_head(held, source, column[...].T[0:1, :])
        return carry

    lax.fori_loop(0, source_count, one, 0)
    at = 0
    for returned in returns:
        per = returned.shape[0]
        returned[...] = held[at : at + per]
        at += per


def expert_step(weight_in, weight_out, row_chunks, grad_chunks):
    count = len(row_chunks)
    sources = sum(chunk.shape[0] for chunk in row_chunks)
    _, capacity, model = grad_chunks[0].shape
    hidden = weight_in.shape[2]
    pad = (capacity + 127) // 128 * 128
    return pl.pallas_call(
        functools.partial(expert_kernel, count),
        out_shape=(
            shape((sources, capacity, model), bf16),
            shape((sources, capacity, model), bf16),
            shape((sources, capacity, hidden), bf16),
            shape((sources, capacity, hidden), bf16),
        )
        + tuple(shape(chunk.shape, bf16) for chunk in row_chunks),
        in_specs=[VMEM] * (2 + 2 * count),
        out_specs=(VMEM,) * (4 + count),
        scratch_shapes=[
            pltpu.VMEM((sources, capacity + 16, model), bf16),
            pltpu.VMEM((pad, 128), f32),
        ],
        compiler_params=params(60),
        cost_estimate=cost(6 * sources * capacity * model * hidden, 30 * 2**20),
        name="expert_step",
    )(weight_in, weight_out, *row_chunks, *grad_chunks)


def expert_out_kernel(acted_all, out_ref, *rest):
    chunks, held = rest[:-1], rest[-1]

    def one(source, carry):
        held[source] = dot_nn(acted_all[source], out_ref[0]).astype(bf16)
        return carry

    lax.fori_loop(0, held.shape[0], one, 0)
    at = 0
    for chunk in chunks:
        per = chunk.shape[0]
        chunk[...] = held[at : at + per]
        at += per


def expert_outputs(acted_all, weight_out, chunk_shapes):
    sources, capacity, hidden = acted_all.shape
    model = weight_out.shape[2]
    return pl.pallas_call(
        expert_out_kernel,
        out_shape=tuple(shape((per, capacity, model), bf16) for per in chunk_shapes),
        in_specs=[VMEM, VMEM],
        out_specs=(VMEM,) * len(chunk_shapes),
        scratch_shapes=[pltpu.VMEM((sources, capacity, model), bf16)],
        compiler_params=params(40),
        cost_estimate=cost(2 * sources * capacity * model * hidden, 10 * 2**20),
        name="expert_outputs",
    )(acted_all, weight_out)


def gather_rows(chunks, head, starts, place, info, capacity):
    tokens = place.shape[0]
    slot = lax.broadcasted_iota(jnp.int32, (tokens, capacity), 1)
    gate_one, gate_two = info[:, 0:1], info[:, 1:2]
    place_one, place_two = place[:, 0:1], place[:, 1:2]
    total, grad_one, grad_two = None, None, None

    def one(chunk, entry, expert):
        base = expert * capacity
        hit_one = slot == place_one - base
        hit_two = slot == place_two - base
        weights = jnp.where(hit_one, gate_one, jnp.where(hit_two, gate_two, 0.0)).astype(bf16)
        out = dot_nn(weights, chunk[entry, head:, :])
        if head == 0:
            return (out,)
        row = jnp.sum(chunk[entry, 0:16, 0:capacity].astype(f32), axis=0, keepdims=True)
        first = jnp.sum(jnp.where(hit_one, row, 0.0), axis=-1, keepdims=True)
        second = jnp.sum(jnp.where(hit_two, row, 0.0), axis=-1, keepdims=True)
        return out, first, second

    sums = None
    for index, chunk in enumerate(chunks):
        if chunk.shape[0] == 1:
            parts = one(chunk, 0, starts[index])
        else:

            def step(entry, carry, chunk=chunk, index=index):
                found = one(chunk, entry, starts[index] + entry)
                return tuple(a + b for a, b in zip(carry, found))

            zero = (jnp.zeros((tokens, chunk.shape[2]), f32),)
            if head:
                zero = zero + (jnp.zeros((tokens, 1), f32),) * 2
            parts = lax.fori_loop(0, chunk.shape[0], step, zero)
        sums = parts if sums is None else tuple(a + b for a, b in zip(sums, parts))
    return sums


def write_ring(scalars, joined, own, next_one, next_two, last_one, last_two, far_one, far_two):
    quarter = own.shape[0]
    eighth = quarter // 2
    rank = scalars[3]

    def rows_of(which):
        return aligned(lax.rem(rank + which, 4) * quarter, quarter)

    own[...] = joined[pl.ds(rows_of(0), quarter), :]
    for which, one, two in ((1, next_one, next_two), (3, last_one, last_two), (2, far_one, far_two)):
        start = rows_of(which)
        one[...] = joined[pl.ds(start, eighth), :].astype(bf16)
        two[...] = joined[pl.ds(aligned(start + eighth, eighth), eighth), :].astype(bf16)


def ring_shapes(rows, model):
    return (shape((rows // 4, model), f32),) + (shape((rows // 8, model), bf16),) * 6


def combine_grads_kernel(
    capacity, expert_count, chunk_count, scalars, starts, place_ref, info_ref, route_ref, router_ref, *rest
):
    chunks = rest[:chunk_count]
    logit_ref = rest[chunk_count]
    ring = rest[chunk_count + 1 : chunk_count + 8]
    joined = rest[chunk_count + 8]
    rows = place_ref.shape[0]
    step = 256
    lane = lax.broadcasted_iota(jnp.int32, (step, 128), 1)

    def token_step(index, carry):
        start = aligned(index * step, step)
        span = pl.ds(start, step)
        info = info_ref[span, :]
        total, first, second = gather_rows(
            chunks, 16, starts, place_ref[span, :], info, capacity
        )
        mix = first * info[:, 0:1] + second * info[:, 1:2]
        pair_total = info[:, 2:3]
        picked = jnp.where(
            lane == route_ref[span, 0:1] + 64,
            (first - mix) / pair_total,
            jnp.where(lane == route_ref[span, 1:2] + 64, (second - mix) / pair_total, 0.0),
        )
        probs = jnp.where((lane >= 64) & (lane < 64 + expert_count), info, 0.0)
        grads = probs * (picked - jnp.sum(probs * picked, axis=-1, keepdims=True))
        grads = grads.astype(bf16)
        logit_ref[span, :] = grads
        joined[span, :] = total + dot_nt(grads, router_ref[:, 128:256])
        return carry

    lax.fori_loop(0, rows // step, token_step, 0)
    write_ring(scalars, joined, *ring)


def combine_grads(scalars, starts, place, info, routes, router, chunks, capacity, expert_count):
    rows = place.shape[0]
    model = router.shape[0]
    return pl.pallas_call(
        functools.partial(combine_grads_kernel, capacity, expert_count, len(chunks)),
        out_shape=(shape((rows, 128), bf16),) + ring_shapes(rows, model),
        in_specs=[SMEM, SMEM] + [VMEM] * (4 + len(chunks)),
        out_specs=(VMEM,) * 8,
        scratch_shapes=[pltpu.VMEM((rows, model), f32)],
        compiler_params=params(56),
        cost_estimate=cost(2 * rows * model * 2304, 10 * 2**20),
        name="combine_grads",
    )(scalars, starts, place, info, routes, router, *chunks)


def combine_outs_kernel(capacity, chunk_count, scalars, starts, place_ref, info_ref, *rest):
    chunks = rest[:chunk_count]
    ring = rest[chunk_count : chunk_count + 7]
    joined = rest[chunk_count + 7]
    rows = place_ref.shape[0]
    step = 256

    def token_step(index, carry):
        span = pl.ds(aligned(index * step, step), step)
        (total,) = gather_rows(
            chunks, 0, starts, place_ref[span, :], info_ref[span, :], capacity
        )
        joined[span, :] = total
        return carry

    lax.fori_loop(0, rows // step, token_step, 0)
    write_ring(scalars, joined, *ring)


def combine_outs(scalars, starts, place, info, chunks, capacity):
    rows = place.shape[0]
    model = chunks[0].shape[2]
    return pl.pallas_call(
        functools.partial(combine_outs_kernel, capacity, len(chunks)),
        out_shape=ring_shapes(rows, model),
        in_specs=[SMEM, SMEM] + [VMEM] * (2 + len(chunks)),
        out_specs=(VMEM,) * 7,
        scratch_shapes=[pltpu.VMEM((rows, model), f32)],
        compiler_params=params(56),
        cost_estimate=cost(2 * rows * model * 2304, 10 * 2**20),
        name="combine_outs",
    )(scalars, starts, place, info, *chunks)


def received(own, next_one, next_two, last_one, last_two):
    eighth = next_one.shape[0]
    first = own[0:eighth, :] + next_one[...].astype(f32) + last_one[...].astype(f32)
    second = own[eighth:, :] + next_two[...].astype(f32) + last_two[...].astype(f32)
    return jnp.concatenate([first, second], axis=0)


def norm_back_kernel(gain_index, has_bypass_rows, scalars, value_ref, gain_ref, bypass_ref, *rest):
    grads = received(*rest[:5])
    full_ref, one_ref, two_ref, gain_grad = rest[5:]
    quarter = grads.shape[0]
    eighth = quarter // 2
    here = pl.ds(aligned(scalars[3] * quarter, quarter), quarter)
    values = (value_ref[here, :] if gain_index == 0 else value_ref[...]).astype(f32)
    bypass = (bypass_ref[here, :] if has_bypass_rows else bypass_ref[...]).astype(f32)
    scale = lax.rsqrt(jnp.mean(values * values, axis=-1, keepdims=True) + epsilon)
    normed = values * scale
    scaled = grads * gain_ref[gain_index : gain_index + 1, :]
    gain_grad[...] = jnp.broadcast_to(
        jnp.sum(grads * normed, axis=0, keepdims=True), gain_grad.shape
    )
    out = bypass + scale * (scaled - normed * jnp.mean(scaled * normed, axis=-1, keepdims=True))
    full_ref[...] = out
    one_ref[...] = out[0:eighth].astype(bf16)
    two_ref[...] = out[eighth:].astype(bf16)


def norm_back(gain_index, has_bypass_rows, scalars, values, gains, bypass, parts):
    quarter, model = parts[0].shape
    return pl.pallas_call(
        functools.partial(norm_back_kernel, gain_index, has_bypass_rows),
        out_shape=(
            shape((quarter, model), f32),
            shape((quarter // 2, model), bf16),
            shape((quarter // 2, model), bf16),
            shape((8, model), f32),
        ),
        in_specs=[SMEM] + [VMEM] * 8,
        out_specs=(VMEM,) * 4,
        compiler_params=params(40),
        cost_estimate=cost(quarter * model * 16, 6 * 2**20),
        name="norm_back",
    )(scalars, values, gains, bypass, *parts)


def finish_kernel(residual_ref, *rest):
    total = residual_ref[...] + received(*rest[:5])
    one_ref, two_ref = rest[5:]
    eighth = one_ref.shape[0]
    one_ref[...] = total[0:eighth].astype(bf16)
    two_ref[...] = total[eighth:].astype(bf16)


def finish(residual, parts):
    quarter, model = residual.shape
    return pl.pallas_call(
        finish_kernel,
        out_shape=(shape((quarter // 2, model), bf16),) * 2,
        in_specs=[VMEM] * 6,
        out_specs=(VMEM,) * 2,
        compiler_params=params(40),
        cost_estimate=cost(quarter * model * 4, 4 * 2**20),
        name="finish",
    )(residual, *parts)


def hidden_grad_kernel(scalars, dq_ref, weight_ref, own, from_one, from_two, dkv_ref, *rest):
    ring, joined = rest[:7], rest[7]
    half = own.shape[0] // 2
    for part in range(2):
        span = slice(part * half, (part + 1) * half)
        total = (
            own[span, :].astype(f32)
            + from_one[part][...].astype(f32)
            + from_two[part][...].astype(f32)
        ).astype(bf16)
        dkv_ref[span, :] = total
        joined[span, :] = dot_nt(dq_ref[span, :], weight_ref[:, 0:256]) + dot_nt(
            total, weight_ref[:, 256:640]
        )
    write_ring(scalars, joined, *ring)


def hidden_grad(scalars, dq, weights, own, from_one, from_two):
    rows = dq.shape[0]
    model = weights.shape[0]

    def kernel(scal, dq_ref, weight_ref, own_ref, a, b, c, d, *rest):
        hidden_grad_kernel(scal, dq_ref, weight_ref, own_ref, (a, b), (c, d), *rest)

    return pl.pallas_call(
        kernel,
        out_shape=(shape((rows, 384), bf16),) + ring_shapes(rows, model),
        in_specs=[SMEM] + [VMEM] * 7,
        out_specs=(VMEM,) * 8,
        scratch_shapes=[pltpu.VMEM((rows, model), f32)],
        compiler_params=params(40),
        cost_estimate=cost(2 * rows * model * 640, 8 * 2**20),
        name="hidden_grad",
    )(scalars, dq, weights, own, *from_one, *from_two)


def shift(value, amount):
    size = lax.axis_size("tensor")
    return lax.ppermute(value, "tensor", [(i, (i + amount) % size) for i in range(size)])


def cross(value, mask):
    size = lax.axis_size("context")
    return lax.ppermute(value, "context", [(i, i ^ mask) for i in range(size)])


def ring_gather(one, two):
    last_one, next_two = shift(one, 1), shift(two, -1)
    last_two, next_one = shift(two, 1), shift(one, -1)
    far_one, far_two = shift(last_one, 1), shift(next_two, -1)
    return (one, two, last_one, last_two, next_one, next_two, far_one, far_two)


def ring_ranks(rank):
    return [lax.rem(rank + step, 4) for step in (0, 3, 1, 2)]


def added(first, second):
    return (first.astype(f32) + second.astype(f32)).astype(bf16)


def ring_reduce(own, next_one, next_two, last_one, last_two, far_one, far_two):
    arrived_one, arrived_two = shift(far_one, 1), shift(far_two, -1)
    from_last_two, from_next_one = shift(next_two, 1), shift(last_one, -1)
    from_last_one = shift(added(next_one, arrived_one), 1)
    from_next_two = shift(added(last_two, arrived_two), -1)
    return (own, from_last_one, from_last_two, from_next_one, from_next_two)


def square_gather(one, two):
    beside_one, across_two = cross(one, 1), cross(two, 2)
    beside_two, across_one = cross(two, 1), cross(one, 2)
    far_one, far_two = cross(beside_one, 2), cross(across_two, 1)
    return (one, two, beside_one, beside_two, across_one, across_two, far_one, far_two)


def square_reduce(beside_one, beside_two, across_one, across_two, far_one, far_two):
    arrived_one, arrived_two = cross(far_one, 1), cross(far_two, 2)
    from_beside_one, from_across_two = cross(beside_one, 1), cross(across_two, 2)
    from_across_one = cross(added(across_one, arrived_one), 2)
    from_beside_two = cross(added(beside_two, arrived_two), 1)
    return (from_beside_one, from_beside_two), (from_across_one, from_across_two)


ALL_ROWS = ("dp", "context")


def exchange(chunks):
    count = lax.axis_size("dp") * lax.axis_size("context")
    if len(chunks) == 1:
        return [lax.all_to_all(chunks[0], ALL_ROWS, split_axis=0, concat_axis=0, tiled=True)]
    return [
        chunk if j == 0 else lax.ppermute(chunk, ALL_ROWS, [(d, d ^ j) for d in range(count)])
        for j, chunk in enumerate(chunks)
    ]


def gather_weights(block, here, small):
    count = lax.axis_size("dp") * lax.axis_size("context")
    size = block.shape[0]
    if not small:
        whole = lax.all_gather(block, ALL_ROWS, axis=0, tiled=True)
        return [whole], jnp.zeros((1,), jnp.int32)
    pieces = [
        block if j == 0 else lax.ppermute(block, ALL_ROWS, [(d, d ^ j) for d in range(count)])
        for j in range(count)
    ]
    return pieces, jnp.stack([(here ^ j) * size for j in range(count)])


def scatter_weights(whole, small):
    if not small:
        return lax.psum_scatter(whole, ALL_ROWS, scatter_dimension=0, tiled=True)
    side, context = lax.axis_index("dp"), lax.axis_index("context")
    halves = whole.reshape((2, whole.shape[0] // 2) + whole.shape[1:])
    mine = lax.dynamic_index_in_dim(halves, side, 0, keepdims=False)
    other = lax.dynamic_index_in_dim(halves, 1 - side, 0, keepdims=False)
    mine = mine + lax.ppermute(other, "dp", [(0, 1), (1, 0)])
    blocks = mine.reshape((4, mine.shape[0] // 4) + mine.shape[1:])
    total = lax.dynamic_index_in_dim(blocks, context, 0, keepdims=False)
    for mask in (1, 2, 3):
        part = lax.dynamic_index_in_dim(blocks, context ^ mask, 0, keepdims=False)
        total = total + cross(part, mask)
    return total


def on_device(
    tokens_in, query_weight, key_weight, value_weight, output_weight, bias_table, attention_gain,
    router_weight, expert_gain, expert_in, expert_out, routes, pair_order, seq_lengths, cotangent,
):
    rows, model = tokens_in.shape
    heads = bias_table.shape[1]
    width = query_weight.shape[1] // heads
    group_rows = rows * lax.axis_size("context")
    expert_count = router_weight.shape[1]
    capacity = (9 * rows + 4 * expert_count - 1) // (4 * expert_count)
    count = lax.axis_size("dp") * lax.axis_size("context")
    small = count == 8
    context, rank = lax.axis_index("context"), lax.axis_index("tensor")
    here = lax.axis_index("dp") * lax.axis_size("context") + context
    first_end = seq_lengths[0, 0]
    second_end = first_end + seq_lengths[0, 1]
    scalars = jnp.stack([context, first_end, second_end, rank]).astype(jnp.int32)
    chunk_shapes = [1] * count if small else [expert_count]
    starts = jnp.stack([here ^ j for j in range(count)]) if small else jnp.zeros((1,), jnp.int32)
    starts = starts.astype(jnp.int32)
    shard = query_weight.shape[0]
    first_block = jnp.concatenate(
        [
            query_weight,
            attention_gain[:, None],
            expert_gain[:, None],
            jnp.zeros((shard, 62), bf16),
            key_weight,
            value_weight[:, 2 * width :],
            value_weight[:, : 2 * width],
        ],
        axis=1,
    )
    second_block = jnp.concatenate(
        [output_weight.T, router_weight, jnp.zeros((shard, 64 - expert_count), bf16)], axis=1
    )
    first_pieces, first_offsets = gather_weights(first_block, here, small)
    buckets = jnp.asarray(bucket_tiles())
    bias_tiles = bias_of(bias_table, buckets)
    far_bias = bias_table[-1]
    order_row = (pair_order & 1) * rows + (pair_order >> 1)
    row_place, column_place = find_places(scalars, routes.T, order_row, expert_count, capacity)
    hidden_one, queries, kv_one, kv_two, weights, gains = project(
        first_offsets, tokens_in, first_pieces
    )
    kv_pieces = square_gather(kv_one, kv_two)
    second_pieces, second_offsets = gather_weights(second_block, here, small)
    output_own = assemble(second_offsets, second_pieces, bf16)
    output_parts = [output_own] + [shift(output_own, step) for step in (1, -1, 2)]
    cotangent_chunks = exchange(
        scatter_rows(starts, cotangent, row_place, chunk_shapes, capacity)
    )
    half = rows // 2
    kv_offsets = jnp.stack(
        [(context ^ mask) * rows + part * half for mask in range(4) for part in range(2)]
    )
    packed_one, packed_two, lse, keys_values = attention_forward(
        scalars, far_bias, kv_offsets, queries, bias_tiles, kv_pieces, group_rows, heads, width
    )
    attended = ring_gather(packed_one, packed_two)
    residual, hidden_two, info, *row_chunks = dispatch(
        scalars, starts, tokens_in, gains, routes, row_place, attended, output_parts, chunk_shapes,
        heads, width, capacity, expert_count,
    )
    row_chunks = exchange(row_chunks)
    rows_all, grads_all, acted_all, pre_all, *returns = expert_step(
        expert_in, expert_out, row_chunks, cotangent_chunks
    )
    returns = exchange(returns)
    grad_logits, *ring = combine_grads(
        scalars, starts, column_place, info, routes, output_own, returns, capacity, expert_count
    )
    grad_one, branch_one, branch_two, gain_two_grad = norm_back(
        1, True, scalars, residual, gains, cotangent, ring_reduce(*ring)
    )
    branch_pieces = ring_gather(branch_one, branch_two)
    eighth = rows // 8
    token_offsets = jnp.stack(
        [which * 2 * eighth + part * eighth for which in ring_ranks(rank) for part in range(2)]
    )
    dq, own, *sent, fold = attention_backward(
        scalars, far_bias, token_offsets, queries, keys_values, bias_tiles, lse,
        (packed_one, packed_two), output_own, branch_pieces, heads, width,
    )
    dkv, *ring = hidden_grad(scalars, dq, weights, own, *square_reduce(*sent))
    input_full, input_one, input_two, gain_one_grad = norm_back(
        0, False, scalars, tokens_in, gains, grad_one, ring_reduce(*ring)
    )
    input_grad = assemble(token_offsets, ring_gather(input_one, input_two), f32)
    out_chunks = exchange(expert_outputs(acted_all, expert_out, chunk_shapes))
    ring = combine_outs(scalars, starts, column_place, info, out_chunks, capacity)
    layer_one, layer_two = finish(residual, ring_reduce(*ring))
    layer_out = assemble(token_offsets, ring_gather(layer_one, layer_two), bf16)
    gate_rows = jnp.concatenate([chunk[:, 0:16, 0:capacity] for chunk in row_chunks], axis=0)
    gates = jnp.sum(gate_rows.astype(f32), axis=1).reshape(-1, 1)
    total_rows = gates.shape[0]
    acted_flat = acted_all.reshape(total_rows, -1)
    pre_flat = pre_all.reshape(total_rows, -1)
    expert_out_grad = dot_tn(
        (acted_flat.astype(f32) * gates).astype(bf16), grads_all.reshape(total_rows, -1)
    )[None]
    expert_in_grad = dot_tn(
        rows_all.reshape(total_rows, -1), (pre_flat.astype(f32) * gates).astype(bf16)
    )[None]
    grad_branch = assemble(token_offsets, branch_pieces, bf16)
    quarter = rows // 4
    attended_own = jnp.concatenate(
        [
            jnp.concatenate([packed_one[:, :192], packed_two[:, :192]], axis=0),
            jnp.concatenate(
                [
                    jnp.concatenate([packed_one[:, 256:], packed_one[:, 192:256]], axis=1),
                    jnp.concatenate([packed_two[:, 256:], packed_two[:, 192:256]], axis=1),
                ],
                axis=0,
            ),
        ],
        axis=0,
    )
    output_grad = scatter_weights(dot_tn(grad_branch, attended_own), small).T
    projected = jnp.concatenate([dot_tn(hidden_one, dq), dot_tn(hidden_one, dkv)], axis=1)
    projected = scatter_weights(projected, small)
    router_grad = dot_tn(hidden_two, grad_logits)[:, 64 : 64 + expert_count]
    vectors = jnp.concatenate([router_grad, gain_two_grad[0][:, None]], axis=1)
    vectors = lax.psum(vectors, ("dp", "context", "tensor"))
    vectors = lax.dynamic_slice_in_dim(vectors, here * shard, shard, 0)
    gain_one_grad = lax.psum(gain_one_grad[0], ("dp", "context", "tensor"))
    gain_one_grad = lax.dynamic_slice_in_dim(gain_one_grad, here * shard, shard, 0)
    bucket_row = jnp.asarray(bucket_tiles()[0, 0])
    bucket_hot = (bucket_row[None, :] == jnp.arange(bias_table.shape[0] - 1)[:, None]).astype(f32)
    near_grad = jnp.sum(bucket_hot[:, None, :] * fold[None, :heads, :], axis=-1)
    table_grad = jnp.concatenate([near_grad, -jnp.sum(near_grad, axis=0, keepdims=True)], axis=0)
    table_grad = lax.psum(table_grad, ALL_ROWS)
    return (
        layer_out,
        input_grad,
        projected[:, :192],
        projected[:, 256:448],
        jnp.concatenate([projected[:, 512:], projected[:, 448:512]], axis=1),
        output_grad,
        table_grad,
        gain_one_grad,
        vectors[:, :expert_count],
        vectors[:, expert_count],
        expert_in_grad,
        expert_out_grad,
    )


def solution(mesh):
    rows = P(("dp", "context"), None)
    return jax.shard_map(
        on_device,
        mesh=mesh,
        in_specs=(
            rows,
            P(("dp", "context"), "tensor"),
            P(("dp", "context"), "tensor"),
            P(("dp", "context"), "tensor"),
            P("tensor", ("dp", "context")),
            P(None, "tensor"),
            P(("dp", "context")),
            rows,
            P(("dp", "context")),
            P(("dp", "context"), None, "tensor"),
            P(("dp", "context"), "tensor", None),
            rows,
            rows,
            P("dp", None),
            rows,
        ),
        out_specs=(
            rows,
            rows,
            P(("dp", "context"), "tensor"),
            P(("dp", "context"), "tensor"),
            P(("dp", "context"), "tensor"),
            P("tensor", ("dp", "context")),
            P(None, "tensor"),
            P(("dp", "context")),
            rows,
            P(("dp", "context")),
            P(("dp", "context"), None, "tensor"),
            P(("dp", "context"), "tensor", None),
        ),
        check_vma=False,
    )
```

profile of v0, /device:TPU:0, one launch (start us, length us, event | category | flops | bytes accessed | tf_op | source)
XLA Modules:
  0.0 716.0 jit_solution(14481320040509478466)
XLA Ops:
  65.9 12.3 %select_select_fusion.bias_ref = f32[3,3,256,256]{3,2,1,0:T(8,128)} fusion(f32[3]{0:T(128)S(1)} %get-tuple-element.228, f32[3]{0:T(128)S(1)} %get-tuple-element.229, f32[3]{0:T(128)S(1)} %get-tuple-element.199, f32[3]{0:T(128)S(1)} %get-tuple-element.200, f32[3]{0:T(128)S(1)} %get-tuple-element.201, f32[3]{0:T(128)S(1)} %get-tuple-element.202, ...), kind=kLoop, calls=%fused_computation.6 | loop fusion | flops 18284544 | bytes 8454528 | tf_op jit(solution)/shard_map/jit(_where)/select_n | solution.py:430
  86.9 15.1 %collective-permute-done.24.rest_6_ = bf16[96,256]{1,0:T(8,128)(2,1)S(1)} collective-permute-done((bf16[96,256]{1,0:T(8,128)(2,1)S(1)}, bf16[96,256]{1,0:T(8,128)(2,1)S(1)}, u32[]{:S(2)}, u32[]{:S(2)}) %collective-permute-start.24) | collective-permute-done | bytes 49184 | tf_op jit(solution)/shard_map/ppermute | solution.py:1168
  115.0 11.6 %attention_forward.1 = (bf16[256,384]{1,0:T(8,128)(2,1)}, bf16[256,384]{1,0:T(8,128)(2,1)}, f32[8,1024]{1,0:T(8,128)}, bf16[4096,384]{1,0:T(8,128)(2,1)}) custom-call(s32[4]{0:T(128)} %pad_add_fusion.scalars.scal, f32[3]{0:T(128)} %copy-done.124, s32[8]{0:T(128)} %stack.168.offsets, bf16[1024,256]{1,0:T(8,128)(2,1)} %copy-done.73, ...), custom_call_target="tpu_custom_call" | custom-call | flops 12884901888 | bytes 10485760 | tf_op jit(solution)/shard_map/attention_forward/pallas_call | solution.py:161
  130.4 8.6 %find_places.1 = (s32[8,1024]{1,0:T(8,128)S(1)}, s32[1024,128]{1,0:T(8,128)S(1)}) custom-call(s32[4]{0:T(128)S(1)} %copy-done.49, s32[2,1024]{1,0:T(2,128)S(1)} %bitcast.93, s32[1,2048]{1,0:T(1,128)S(1)} %copy-done.52), custom_call_target="tpu_custom_call" | custom-call | flops 2147483648 | bytes 1048576 | tf_op jit(solution)/shard_map/find_places/pallas_call | solution.py:504
  145.4 15.5 %collective-permute-start.17 = (bf16[256,384]{1,0:T(8,128)(2,1)}, bf16[256,384]{1,0:T(8,128)(2,1)S(1)}, u32[]{:S(2)}, u32[]{:S(2)}) collective-permute-start(bf16[256,384]{1,0:T(8,128)(2,1)} %collective-permute-done.13.rest_2_), channel_id=1, source_target_pairs={{0,1},{1,2},{2,3},{3,0},{4,5},{5,6},{6,7},{7,4},{8,9},{9,10},{10,1... | collective-permute-start | bytes 589832 | tf_op jit(solution)/shard_map/ppermute | solution.py:1102
  168.2 15.6 %collective-permute-start.37 = (bf16[1,288,768]{2,1,0:T(8,128)(2,1)S(1)}, bf16[1,288,768]{2,1,0:T(8,128)(2,1)S(1)}, u32[]{:S(2)}, u32[]{:S(2)}) collective-permute-start(bf16[1,288,768]{2,1,0:T(8,128)(2,1)S(1)} %get-tuple-element.124), channel_id=1, source_target_pairs={{0,8},{4,12},{8,0},{12,4},{16,24},{20,28},{24,16},{28,20},{1,9},{5... | collective-permute-start | bytes 1327112 | tf_op jit(solution)/shard_map/ppermute | solution.py:1156
  185.5 17.1 %dispatch.1 = (f32[256,768]{1,0:T(8,128)}, bf16[1024,768]{1,0:T(8,128)(2,1)}, f32[1024,128]{1,0:T(8,128)}, bf16[1,304,768]{2,1,0:T(8,128)(2,1)}, bf16[1,304,768]...) custom-call(s32[4]{0:T(128)} %pad_add_fusion.scalars.scal, ...), custom_call_target="tpu_custom_call" | custom-call | flops 5234491392 | bytes 16777216 | tf_op jit(solution)/shard_map/dispatch/pallas_call | solution.py:698
  209.9 14.8 %collective-permute-done.40.rest_13_ = bf16[1,288,768]{2,1,0:T(8,128)(2,1)S(1)} collective-permute-done((bf16[1,288,768]{2,1,0:T(8,128)(2,1)S(1)}, bf16[1,288,768]{2,1,0:T(8,128)(2,1)S(1)}, u32[]{:S(2)}, u32[]{:S(2)}) %collective-permute-start.40) | collective-permute-done | bytes 442400 | tf_op jit(solution)/shard_map/ppermute | solution.py:1156
  228.1 18.5 %collective-permute-done.41.rest_14_ = bf16[1,288,768]{2,1,0:T(8,128)(2,1)S(1)} collective-permute-done((bf16[1,288,768]{2,1,0:T(8,128)(2,1)S(1)}, bf16[1,288,768]{2,1,0:T(8,128)(2,1)S(1)}, u32[]{:S(2)}, u32[]{:S(2)}) %collective-permute-start.41) | collective-permute-done | bytes 442400 | tf_op jit(solution)/shard_map/ppermute | solution.py:1156
  254.0 6.6 collective-permute-done.33.rest_5_
  260.5 10.0 %collective-permute-done.34.rest_6_ = bf16[1,304,768]{2,1,0:T(8,128)(2,1)} collective-permute-done((bf16[1,304,768]{2,1,0:T(8,128)(2,1)}, bf16[1,304,768]{2,1,0:T(8,128)(2,1)}, u32[]{:S(2)}, u32[]{:S(2)}) %collective-permute-start.34) | collective-permute-done | bytes 466976 | tf_op jit(solution)/shard_map/ppermute | solution.py:1156
  271.5 20.5 %expert_step.1 = (bf16[8,288,768]{2,1,0:T(8,128)(2,1)}, bf16[8,288,768]{2,1,0:T(8,128)(2,1)}, bf16[8,288,768]{2,1,0:T(8,128)(2,1)}, bf16[8,288,768]{2,1,0:T(8,12...) custom-call(bf16[1,768,768]{2,1,0:T(8,128)(2,1)} %in_ref.1, ...), custom_call_target="tpu_custom_call" | custom-call | flops 8153726976 | bytes 31457280 | tf_op jit(solution)/shard_map/expert_step/pallas_call | solution.py:805
  307.6 7.7 %collective-permute-done.43.rest_1_ = bf16[1,288,768]{2,1,0:T(8,128)(2,1)S(1)} collective-permute-done((bf16[1,288,768]{2,1,0:T(8,128)(2,1)S(1)}, bf16[1,288,768]{2,1,0:T(8,128)(2,1)S(1)}, u32[]{:S(2)}, u32[]{:S(2)}) %collective-permute-start.43) | collective-permute-done | bytes 442400 | tf_op jit(solution)/shard_map/ppermute | solution.py:1156
  316.6 8.9 %collective-permute-done.45.rest_3_ = bf16[1,288,768]{2,1,0:T(8,128)(2,1)S(1)} collective-permute-done((bf16[1,288,768]{2,1,0:T(8,128)(2,1)S(1)}, bf16[1,288,768]{2,1,0:T(8,128)(2,1)S(1)}, u32[]{:S(2)}, u32[]{:S(2)}) %collective-permute-start.45) | collective-permute-done | bytes 442400 | tf_op jit(solution)/shard_map/ppermute | solution.py:1156
  334.8 28.8 %collective-permute-done.48.rest_6_ = bf16[1,288,768]{2,1,0:T(8,128)(2,1)S(1)} collective-permute-done((bf16[1,288,768]{2,1,0:T(8,128)(2,1)S(1)}, bf16[1,288,768]{2,1,0:T(8,128)(2,1)S(1)}, u32[]{:S(2)}, u32[]{:S(2)}) %collective-permute-start.48) | collective-permute-done | bytes 442400 | tf_op jit(solution)/shard_map/ppermute | solution.py:1156
  371.8 11.8 %combine_outs.1 = (f32[256,768]{1,0:T(8,128)}, bf16[128,768]{1,0:T(8,128)(2,1)}, bf16[128,768]{1,0:T(8,128)(2,1)}, bf16[128,768]{1,0:T(8,128)(2,1)}, bf16[128,76...) custom-call(s32[4]{0:T(128)} %pad_add_fusion.scalars.scal, s32[8]{0:T(128)} %copy-done.55, ...), custom_call_target="tpu_custom_call" | custom-call | flops 3623878656 | bytes 10485760 | tf_op jit(solution)/shard_map/combine_outs/pallas_call | solution.py:986
  389.6 14.9 %combine_grads.1 = (bf16[1024,128]{1,0:T(8,128)(2,1)}, f32[256,768]{1,0:T(8,128)}, bf16[128,768]{1,0:T(8,128)(2,1)}, bf16[128,768]{1,0:T(8,128)(2,1)}, bf16[128,...) custom-call(s32[4]{0:T(128)} %pad_add_fusion.scalars.scal, ...), custom_call_target="tpu_custom_call" | custom-call | flops 3623878656 | bytes 10485760 | tf_op jit(solution)/shard_map/combine_grads/pallas_call | solution.py:952
  406.8 11.9 %collective-permute-done.73 = bf16[128,768]{1,0:T(8,128)(2,1)S(1)} collective-permute-done((bf16[128,768]{1,0:T(8,128)(2,1)}, bf16[128,768]{1,0:T(8,128)(2,1)S(1)}, u32[]{:S(2)}, u32[]{:S(2)}) %collective-permute-start.73) | collective-permute-done | bytes 196640 | tf_op jit(solution)/shard_map/ppermute | solution.py:1102
  431.1 5.6 collective-permute-start.56
  437.2 7.6 %fusion.5 = f32[1,768,768]{2,1,0:T(8,128)} fusion(bf16[8,288,768]{2,1,0:T(8,128)(2,1)} %get-tuple-element.193, bf16[8,288,768]{2,1,0:T(8,128)(2,1)} %get-tuple-element.194, f32[8,288]{1,0:T(8,128)S(1)} %convert_reduce_fusion), kind=kOutput, calls=%fused_computation.9 | convolution fusion | flops 2723217408 | bytes 9446400 | tf_op jit(solution)/shard_map/dot_general | solution.py:28
  459.1 5.2 collective-permute-done.58.rest_4_
  464.4 4.9 collective-permute-start.61
  469.3 6.6 collective-permute-done.78.rest_5_
  480.3 8.0 %collective-permute-done.61.rest_7_ = bf16[128,768]{1,0:T(8,128)(2,1)S(1)} collective-permute-done((bf16[128,768]{1,0:T(8,128)(2,1)S(1)}, bf16[128,768]{1,0:T(8,128)(2,1)S(1)}, u32[]{:S(2)}, u32[]{:S(2)}) %collective-permute-start.61) | collective-permute-done | bytes 196640 | tf_op jit(solution)/shard_map/ppermute | solution.py:1102
  491.7 21.7 %attention_backward.1 = (bf16[1024,256]{1,0:T(8,128)(2,1)}, bf16[1024,384]{1,0:T(8,128)(2,1)}, bf16[512,384]{1,0:T(8,128)(2,1)}, bf16[512,384]{1,0:T(8,128)(2,1)...) custom-call(s32[4]{0:T(128)} %pad_add_fusion.scalars.scal, ...), custom_call_target="tpu_custom_call" | custom-call | flops 32212254720 | bytes 16777216 | tf_op jit(solution)/shard_map/attention_backward/pallas_call | solution.py:380
  513.4 13.3 %collective-permute-start.84 = (bf16[512,384]{1,0:T(8,128)(2,1)}, bf16[512,384]{1,0:T(8,128)(2,1)}, u32[]{:S(2)}, u32[]{:S(2)}) collective-permute-start(bf16[512,384]{1,0:T(8,128)(2,1)} %get-tuple-element.175), channel_id=1, source_target_pairs={{0,4},{4,0},{8,12},{12,8},{1,5},{5,1},{9,13},{13,9},{2,6},{6,2},{1... | collective-permute-start | bytes 1179656 | tf_op jit(solution)/shard_map/ppermute | solution.py:1107
  526.8 22.7 %collective-permute-start.82 = (bf16[512,384]{1,0:T(8,128)(2,1)}, bf16[512,384]{1,0:T(8,128)(2,1)}, u32[]{:S(2)}, u32[]{:S(2)}) collective-permute-start(bf16[512,384]{1,0:T(8,128)(2,1)} %get-tuple-element.173), channel_id=1, source_target_pairs={{0,8},{4,12},{8,0},{12,4},{1,9},{5,13},{9,1},{13,5},{2,10},{6,14},... | collective-permute-start | bytes 1179656 | tf_op jit(solution)/shard_map/ppermute | solution.py:1107
  569.3 19.1 %psum.21 = f32[32,3]{0,1:T(4,128)} all-reduce(f32[32,3]{0,1:T(4,128)S(1)} %pad_maximum_fusion.3), channel_id=1, replica_groups=mesh['dp'=2,'context'=4,'tensor'=4] {'dp','context'}, use_global_device_ids=true, to_apply=%region_2.3 | all-reduce | flops 96 | bytes 768 | tf_op jit(solution)/shard_map/psum | solution.py:1322
  611.5 7.1 collective-permute-done.87
  633.4 5.5 collective-permute-done.88.rest_1_
  648.5 6.7 collective-permute-done.93.rest_2_
  657.3 43.4 %all-reduce = (f32[768]{0:T(1024)S(1)}, f32[768,9]{0,1:T(8,128)S(1)}) all-reduce(f32[768]{0:T(1024)S(1)} %slice_reduce_fusion, f32[768,9]{0,1:T(8,128)S(1)} %copy-done.116), channel_id=1, replica_groups=mesh['dp'=2,'context'=4,'tensor'=4] {'dp','context','tensor'}, use_global_device_ids=true, to_apply=%region_3.4 | all-reduce | flops 7680 | bytes 61440 | tf_op jit(solution)/shard_map/psum | solution.py:1316
  (624 shorter events, 284.8 us)
Async XLA Ops:
  9.4 35.4 %collective-permute-start.2 = (bf16[96,640]{1,0:T(8,128)(2,1)S(1)}, bf16[96,640]{1,0:T(8,128)(2,1)S(1)}, u32[]{:S(2)}, u32[]{:S(2)}) collective-permute-start(bf16[96,640]{1,0:T(8,128)(2,1)S(1)} %concatenate.30.rest_0_), channel_id=1, source_target_pairs={{0,12},{4,8},{8,4},{12,0},{16,28},{20,24},{24,20},{28,16},{1,13},{... | collective-permute-start | bytes 368648 | tf_op jit(solution)/shard_map/ppermute | solution.py:1168
  9.4 37.4 %collective-permute-start.3 = (bf16[96,640]{1,0:T(8,128)(2,1)S(1)}, bf16[96,640]{1,0:T(8,128)(2,1)S(1)}, u32[]{:S(2)}, u32[]{:S(2)}) collective-permute-start(bf16[96,640]{1,0:T(8,128)(2,1)S(1)} %concatenate.30.rest_0_), channel_id=1, source_target_pairs={{0,16},{4,20},{8,24},{12,28},{16,0},{20,4},{24,8},{28,12},{1,17},{... | collective-permute-start | bytes 368648 | tf_op jit(solution)/shard_map/ppermute | solution.py:1168
  9.4 39.6 %collective-permute-start.4 = (bf16[96,640]{1,0:T(8,128)(2,1)S(1)}, bf16[96,640]{1,0:T(8,128)(2,1)S(1)}, u32[]{:S(2)}, u32[]{:S(2)}) collective-permute-start(bf16[96,640]{1,0:T(8,128)(2,1)S(1)} %concatenate.30.rest_0_), channel_id=1, source_target_pairs={{0,20},{4,16},{8,28},{12,24},{16,4},{20,0},{24,12},{28,8},{1,21},{... | collective-permute-start | bytes 368648 | tf_op jit(solution)/shard_map/ppermute | solution.py:1168
  13.3 36.9 %collective-permute-start.5 = (bf16[96,640]{1,0:T(8,128)(2,1)S(1)}, bf16[96,640]{1,0:T(8,128)(2,1)S(1)}, u32[]{:S(2)}, u32[]{:S(2)}) collective-permute-start(bf16[96,640]{1,0:T(8,128)(2,1)S(1)} %concatenate.30.rest_0_), channel_id=1, source_target_pairs={{0,24},{4,28},{8,16},{12,20},{16,8},{20,12},{24,0},{28,4},{1,25},{... | collective-permute-start | bytes 368648 | tf_op jit(solution)/shard_map/ppermute | solution.py:1168
  14.5 36.7 %collective-permute-start.6 = (bf16[96,640]{1,0:T(8,128)(2,1)S(1)}, bf16[96,640]{1,0:T(8,128)(2,1)S(1)}, u32[]{:S(2)}, u32[]{:S(2)}) collective-permute-start(bf16[96,640]{1,0:T(8,128)(2,1)S(1)} %concatenate.30.rest_0_), channel_id=1, source_target_pairs={{0,28},{4,24},{8,20},{12,16},{16,12},{20,8},{24,4},{28,0},{1,29},{... | collective-permute-start | bytes 368648 | tf_op jit(solution)/shard_map/ppermute | solution.py:1168
  114.1 52.0 %collective-permute-start.28 = (bf16[768,256]{1,0:T(8,128)(2,1)S(1)}, bf16[768,256]{1,0:T(8,128)(2,1)}, u32[]{:S(2)}, u32[]{:S(2)}) collective-permute-start(bf16[768,256]{1,0:T(8,128)(2,1)S(1)} %assemble.4.rest_8_.router_ref.output_ref), channel_id=1, source_target_pairs={{0,2},{1,3},{2,0},{3,1},{4,6},{5,7},{6,4},{7,5},{8,10},{9,11},{10,... | collective-permute-start | bytes 1179656 | tf_op jit(solution)/shard_map/ppermute | solution.py:1102
  141.6 42.2 %collective-permute-start.15 = (bf16[256,384]{1,0:T(8,128)(2,1)}, bf16[256,384]{1,0:T(8,128)(2,1)S(1)}, u32[]{:S(2)}, u32[]{:S(2)}) collective-permute-start(bf16[256,384]{1,0:T(8,128)(2,1)} %get-tuple-element.109.rest_0_.packed_one), channel_id=1, source_target_pairs={{0,3},{1,0},{2,1},{3,2},{4,7},{5,4},{6,5},{7,6},{8,11},{9,8},{10,9... | collective-permute-start | bytes 589832 | tf_op jit(solution)/shard_map/ppermute | solution.py:1102
  145.4 38.7 %collective-permute-start.17 = (bf16[256,384]{1,0:T(8,128)(2,1)}, bf16[256,384]{1,0:T(8,128)(2,1)S(1)}, u32[]{:S(2)}, u32[]{:S(2)}) collective-permute-start(bf16[256,384]{1,0:T(8,128)(2,1)} %collective-permute-done.13.rest_2_), channel_id=1, source_target_pairs={{0,1},{1,2},{2,3},{3,0},{4,5},{5,6},{6,7},{7,4},{8,9},{9,10},{10,1... | collective-permute-start | bytes 589832 | tf_op jit(solution)/shard_map/ppermute | solution.py:1102
  166.1 37.8 %collective-permute-start.36 = (bf16[1,288,768]{2,1,0:T(8,128)(2,1)S(1)}, bf16[1,288,768]{2,1,0:T(8,128)(2,1)S(1)}, u32[]{:S(2)}, u32[]{:S(2)}) collective-permute-start(bf16[1,288,768]{2,1,0:T(8,128)(2,1)S(1)} %get-tuple-element.123), channel_id=1, source_target_pairs={{0,4},{4,0},{8,12},{12,8},{16,20},{20,16},{24,28},{28,24},{1,5},{5... | collective-permute-start | bytes 1327112 | tf_op jit(solution)/shard_map/ppermute | solution.py:1156
  168.2 39.7 %collective-permute-start.37 = (bf16[1,288,768]{2,1,0:T(8,128)(2,1)S(1)}, bf16[1,288,768]{2,1,0:T(8,128)(2,1)S(1)}, u32[]{:S(2)}, u32[]{:S(2)}) collective-permute-start(bf16[1,288,768]{2,1,0:T(8,128)(2,1)S(1)} %get-tuple-element.124), channel_id=1, source_target_pairs={{0,8},{4,12},{8,0},{12,4},{16,24},{20,28},{24,16},{28,20},{1,9},{5... | collective-permute-start | bytes 1327112 | tf_op jit(solution)/shard_map/ppermute | solution.py:1156
  202.7 44.8 %collective-permute-start.29 = (bf16[1,304,768]{2,1,0:T(8,128)(2,1)}, bf16[1,304,768]{2,1,0:T(8,128)(2,1)}, u32[]{:S(2)}, u32[]{:S(2)}) collective-permute-start(bf16[1,304,768]{2,1,0:T(8,128)(2,1)} %get-tuple-element.115), channel_id=1, source_target_pairs={{0,4},{4,0},{8,12},{12,8},{16,20},{20,16},{24,28},{28,24},{1,5},{5... | collective-permute-start | bytes 1400840 | tf_op jit(solution)/shard_map/ppermute | solution.py:1156
  203.9 45.5 %collective-permute-start.30 = (bf16[1,304,768]{2,1,0:T(8,128)(2,1)}, bf16[1,304,768]{2,1,0:T(8,128)(2,1)}, u32[]{:S(2)}, u32[]{:S(2)}) collective-permute-start(bf16[1,304,768]{2,1,0:T(8,128)(2,1)} %get-tuple-element.116), channel_id=1, source_target_pairs={{0,8},{4,12},{8,0},{12,4},{16,24},{20,28},{24,16},{28,20},{1,9},{5... | collective-permute-start | bytes 1400840 | tf_op jit(solution)/shard_map/ppermute | solution.py:1156
  207.9 38.7 %collective-permute-start.41 = (bf16[1,288,768]{2,1,0:T(8,128)(2,1)S(1)}, bf16[1,288,768]{2,1,0:T(8,128)(2,1)S(1)}, u32[]{:S(2)}, u32[]{:S(2)}) collective-permute-start(bf16[1,288,768]{2,1,0:T(8,128)(2,1)S(1)} %get-tuple-element.128), channel_id=1, source_target_pairs={{0,24},{4,28},{8,16},{12,20},{16,8},{20,12},{24,0},{28,4},{1,25},{... | collective-permute-start | bytes 1327112 | tf_op jit(solution)/shard_map/ppermute | solution.py:1156
  208.0 39.3 %collective-permute-start.42 = (bf16[1,288,768]{2,1,0:T(8,128)(2,1)S(1)}, bf16[1,288,768]{2,1,0:T(8,128)(2,1)S(1)}, u32[]{:S(2)}, u32[]{:S(2)}) collective-permute-start(bf16[1,288,768]{2,1,0:T(8,128)(2,1)S(1)} %get-tuple-element.129), channel_id=1, source_target_pairs={{0,28},{4,24},{8,20},{12,16},{16,12},{20,8},{24,4},{28,0},{1,29},{... | collective-permute-start | bytes 1327112 | tf_op jit(solution)/shard_map/ppermute | solution.py:1156
  292.1 72.7 %collective-permute-start.62 = (bf16[1,304,768]{2,1,0:T(8,128)(2,1)}, bf16[1,304,768]{2,1,0:T(8,128)(2,1)S(1)}, u32[]{:S(2)}, u32[]{:S(2)}) collective-permute-start(bf16[1,304,768]{2,1,0:T(8,128)(2,1)} %get-tuple-element.149), channel_id=1, source_target_pairs={{0,4},{4,0},{8,12},{12,8},{16,20},{20,16},{24,28},{28,24},{1,5},{5... | collective-permute-start | bytes 1400840 | tf_op jit(solution)/shard_map/ppermute | solution.py:1156
  315.4 49.6 %collective-permute-start.63 = (bf16[1,304,768]{2,1,0:T(8,128)(2,1)S(1)}, bf16[1,304,768]{2,1,0:T(8,128)(2,1)S(1)}, u32[]{:S(2)}, u32[]{:S(2)}) collective-permute-start(bf16[1,304,768]{2,1,0:T(8,128)(2,1)S(1)} %copy-done.134), channel_id=1, source_target_pairs={{0,8},{4,12},{8,0},{12,4},{16,24},{20,28},{24,16},{28,20},{1,9},{5... | collective-permute-start | bytes 1400840 | tf_op jit(solution)/shard_map/ppermute | solution.py:1156
  325.5 38.0 %collective-permute-start.48 = (bf16[1,288,768]{2,1,0:T(8,128)(2,1)S(1)}, bf16[1,288,768]{2,1,0:T(8,128)(2,1)S(1)}, u32[]{:S(2)}, u32[]{:S(2)}) collective-permute-start(bf16[1,288,768]{2,1,0:T(8,128)(2,1)S(1)} %get-tuple-element.137), channel_id=1, source_target_pairs={{0,24},{4,28},{8,16},{12,20},{16,8},{20,12},{24,0},{28,4},{1,25},{... | collective-permute-start | bytes 1327112 | tf_op jit(solution)/shard_map/ppermute | solution.py:1156
  325.5 38.1 %collective-permute-start.49 = (bf16[1,288,768]{2,1,0:T(8,128)(2,1)S(1)}, bf16[1,288,768]{2,1,0:T(8,128)(2,1)S(1)}, u32[]{:S(2)}, u32[]{:S(2)}) collective-permute-start(bf16[1,288,768]{2,1,0:T(8,128)(2,1)S(1)} %get-tuple-element.138), channel_id=1, source_target_pairs={{0,28},{4,24},{8,20},{12,16},{16,12},{20,8},{24,4},{28,0},{1,29},{... | collective-permute-start | bytes 1327112 | tf_op jit(solution)/shard_map/ppermute | solution.py:1156
  332.7 50.9 %collective-permute-start.64 = (bf16[1,304,768]{2,1,0:T(8,128)(2,1)S(1)}, bf16[1,304,768]{2,1,0:T(8,128)(2,1)S(1)}, u32[]{:S(2)}, u32[]{:S(2)}) collective-permute-start(bf16[1,304,768]{2,1,0:T(8,128)(2,1)S(1)} %copy-done.132), channel_id=1, source_target_pairs={{0,12},{4,8},{8,4},{12,0},{16,28},{20,24},{24,20},{28,16},{1,13},{... | collective-permute-start | bytes 1400840 | tf_op jit(solution)/shard_map/ppermute | solution.py:1156
  385.7 37.0 %collective-permute-start.52 = (bf16[128,768]{1,0:T(8,128)(2,1)}, bf16[128,768]{1,0:T(8,128)(2,1)S(1)}, u32[]{:S(2)}, u32[]{:S(2)}) collective-permute-start(bf16[128,768]{1,0:T(8,128)(2,1)} %get-tuple-element.142), channel_id=1, source_target_pairs={{0,1},{1,2},{2,3},{3,0},{4,5},{5,6},{6,7},{7,4},{8,9},{9,10},{10,1... | collective-permute-start | bytes 589832 | tf_op jit(solution)/shard_map/ppermute | solution.py:1102
  387.6 37.0 %collective-permute-start.53 = (bf16[128,768]{1,0:T(8,128)(2,1)}, bf16[128,768]{1,0:T(8,128)(2,1)S(1)}, u32[]{:S(2)}, u32[]{:S(2)}) collective-permute-start(bf16[128,768]{1,0:T(8,128)(2,1)} %get-tuple-element.143), channel_id=1, source_target_pairs={{0,3},{1,0},{2,1},{3,2},{4,7},{5,4},{6,5},{7,6},{8,11},{9,8},{10,9... | collective-permute-start | bytes 589832 | tf_op jit(solution)/shard_map/ppermute | solution.py:1102
  513.4 48.1 %collective-permute-start.84 = (bf16[512,384]{1,0:T(8,128)(2,1)}, bf16[512,384]{1,0:T(8,128)(2,1)}, u32[]{:S(2)}, u32[]{:S(2)}) collective-permute-start(bf16[512,384]{1,0:T(8,128)(2,1)} %get-tuple-element.175), channel_id=1, source_target_pairs={{0,4},{4,0},{8,12},{12,8},{1,5},{5,1},{9,13},{13,9},{2,6},{6,2},{1... | collective-permute-start | bytes 1179656 | tf_op jit(solution)/shard_map/ppermute | solution.py:1107
  526.8 38.7 %collective-permute-start.82 = (bf16[512,384]{1,0:T(8,128)(2,1)}, bf16[512,384]{1,0:T(8,128)(2,1)}, u32[]{:S(2)}, u32[]{:S(2)}) collective-permute-start(bf16[512,384]{1,0:T(8,128)(2,1)} %get-tuple-element.173), channel_id=1, source_target_pairs={{0,8},{4,12},{8,0},{12,4},{1,9},{5,13},{9,1},{13,5},{2,10},{6,14},... | collective-permute-start | bytes 1179656 | tf_op jit(solution)/shard_map/ppermute | solution.py:1107
  549.5 39.6 %collective-permute-start.81 = (bf16[512,384]{1,0:T(8,128)(2,1)}, bf16[512,384]{1,0:T(8,128)(2,1)S(1)}, u32[]{:S(2)}, u32[]{:S(2)}) collective-permute-start(bf16[512,384]{1,0:T(8,128)(2,1)} %get-tuple-element.171), channel_id=1, source_target_pairs={{0,4},{4,0},{8,12},{12,8},{1,5},{5,1},{9,13},{13,9},{2,6},{6,2},{1... | collective-permute-start | bytes 1179656 | tf_op jit(solution)/shard_map/ppermute | solution.py:1107
  549.6 39.5 %collective-permute-start.86 = (bf16[512,384]{1,0:T(8,128)(2,1)}, bf16[512,384]{1,0:T(8,128)(2,1)}, u32[]{:S(2)}, u32[]{:S(2)}) collective-permute-start(bf16[512,384]{1,0:T(8,128)(2,1)} %get-tuple-element.176), channel_id=1, source_target_pairs={{0,8},{4,12},{8,0},{12,4},{1,9},{5,13},{9,1},{13,5},{2,10},{6,14},... | collective-permute-start | bytes 1179656 | tf_op jit(solution)/shard_map/ppermute | solution.py:1107
  561.5 39.1 %collective-permute-start.103 = (f32[384,192]{0,1:T(8,128)}, f32[384,192]{0,1:T(8,128)}, u32[]{:S(2)}, u32[]{:S(2)}) collective-permute-start(f32[384,192]{0,1:T(8,128)} %bitcast.92), channel_id=1, source_target_pairs={{0,16},{16,0},{1,17},{17,1},{2,18},{18,2},{3,19},{19,3},{4,20},{20... | collective-permute-start | bytes 884744 | tf_op jit(solution)/shard_map/ppermute | solution.py:1181
  600.3 46.5 %collective-permute-start.99 = (f32[384,640]{1,0:T(8,128)}, f32[384,640]{1,0:T(8,128)}, u32[]{:S(2)}, u32[]{:S(2)}) collective-permute-start(f32[384,640]{1,0:T(8,128)} %dynamic-slice_bitcast_fusion), channel_id=1, source_target_pairs={{0,16},{16,0},{1,17},{17,1},{2,18},{18,2},{3,19},{19,3},{4,20},{20... | collective-permute-start | bytes 2949128 | tf_op jit(solution)/shard_map/ppermute | solution.py:1181
  640.9 60.3 %collective-permute-start.94 = (bf16[128,768]{1,0:T(8,128)(2,1)S(1)}, bf16[128,768]{1,0:T(8,128)(2,1)S(1)}, u32[]{:S(2)}, u32[]{:S(2)}) collective-permute-start(bf16[128,768]{1,0:T(8,128)(2,1)S(1)} %get-tuple-element.185.rest_1_), channel_id=1, source_target_pairs={{0,1},{1,2},{2,3},{3,0},{4,5},{5,6},{6,7},{7,4},{8,9},{9,10},{10,1... | collective-permute-start | bytes 589832 | tf_op jit(solution)/shard_map/ppermute | solution.py:1102
  643.0 58.3 %collective-permute-start.95 = (bf16[128,768]{1,0:T(8,128)(2,1)S(1)}, bf16[128,768]{1,0:T(8,128)(2,1)S(1)}, u32[]{:S(2)}, u32[]{:S(2)}) collective-permute-start(bf16[128,768]{1,0:T(8,128)(2,1)S(1)} %get-tuple-element.184.rest_0_), channel_id=1, source_target_pairs={{0,3},{1,0},{2,1},{3,2},{4,7},{5,4},{6,5},{7,6},{8,11},{9,8},{10,9... | collective-permute-start | bytes 589832 | tf_op jit(solution)/shard_map/ppermute | solution.py:1102
  648.2 65.6 %collective-permute-start.100 = (f32[96,640]{1,0:T(8,128)S(1)}, f32[96,640]{1,0:T(8,128)}, u32[]{:S(2)}, u32[]{:S(2)}) collective-permute-start(f32[96,640]{1,0:T(8,128)S(1)} %get-tuple-element.232), channel_id=1, source_target_pairs={{0,4},{4,0},{8,12},{12,8},{1,5},{5,1},{9,13},{13,9},{2,6},{6,2},{1... | collective-permute-start | bytes 737288 | tf_op jit(solution)/shard_map/ppermute | solution.py:1107
  655.3 58.5 %collective-permute-start.101 = (f32[96,640]{1,0:T(8,128)S(1)}, f32[96,640]{1,0:T(8,128)}, u32[]{:S(2)}, u32[]{:S(2)}) collective-permute-start(f32[96,640]{1,0:T(8,128)S(1)} %get-tuple-element.234), channel_id=1, source_target_pairs={{0,8},{4,12},{8,0},{12,4},{1,9},{5,13},{9,1},{13,5},{2,10},{6,14},... | collective-permute-start | bytes 737288 | tf_op jit(solution)/shard_map/ppermute | solution.py:1107
  656.7 57.1 %collective-permute-start.102 = (f32[96,640]{1,0:T(8,128)S(1)}, f32[96,640]{1,0:T(8,128)}, u32[]{:S(2)}, u32[]{:S(2)}) collective-permute-start(f32[96,640]{1,0:T(8,128)S(1)} %get-tuple-element.233), channel_id=1, source_target_pairs={{0,12},{4,8},{8,4},{12,0},{1,13},{5,9},{9,5},{13,1},{2,14},{6,10},... | collective-permute-start | bytes 737288 | tf_op jit(solution)/shard_map/ppermute | solution.py:1107
  (231 other events, 4775.8 us)
where the time goes:
time: 730 us; the launch traced here: 716 us
  starting transfers between devices  194 us (27%)
  waiting for transfers between devices  190 us (26%)
  Pallas kernels  130 us (18%)
  local copies, waits for them, and re-layouts  91.5 us (13%)
  blocking collectives  62.5 us (9%)
  other arithmetic  28 us (4%)
  matrix products  15.5 us (2%)
    ppermute x28, waiting for transfers between devices, exchange(): lax.ppermute(chunk, ALL_ROWS, [(d, d ^ j) for d in range(count)])  102 us
    ppermute x45, starting transfers between devices, shift(): lax.ppermute(value, 'tensor', [(i, (i + amount) % size) for i in range(si...  83.4 us
    ppermute x45, waiting for transfers between devices, shift(): lax.ppermute(value, 'tensor', [(i, (i + amount) % size) for i in range(si...  71.7 us
    unnamed x354, local copies, waits for them, and re-layouts  66.9 us
    ppermute x18, starting transfers between devices, cross(): return lax.ppermute(value, 'context', [(i, i ^ mask) for i in range(size)])  52.6 us
    ppermute x28, starting transfers between devices, exchange(): lax.ppermute(chunk, ALL_ROWS, [(d, d ^ j) for d in range(count)])  44.2 us
    psum x1, blocking collectives, on_device(): gain_one_grad = lax.psum(gain_one_grad[0], ('dp', 'context', 'tensor'))  43.4 us
    pallas_call x1, Pallas kernels, attention_backward(): pl.pallas_call(functools.partial(attention_backward_kernel, heads, width,...  21.7 us
  transfers between devices with their start and end apart: 107, of which 27 were waited for; matrix products, arithmetic and copies ran while one was open for 14% of the time, Pallas kernels for 12%

commit v1 on v0

--- a/solution.py
+++ b/solution.py
@@ -187,13 +187,13 @@
 
 def attention_backward_kernel(
     heads, width, piece_count, scalars, far_bias, offsets,
-    query_ref, keys_values, bias_ref, lse_ref, packed_one, packed_two, output_ref, *rest
+    query_ref, keys_values, bias_ref, lse_ref, packed_one, packed_two, *rest
 ):
     pieces = rest[:piece_count]
     (
         dq_ref, own_ref, beside_one, beside_two, across_one, across_two, far_one, far_two, fold_ref
     ) = rest[piece_count : piece_count + 9]
-    grad_branch, dout, masked_q, masked_o, keys_t, deltas, dq_t, dk, dv, dkv, band_ref = rest[
+    dout, masked_q, masked_o, keys_t, deltas, dq_t, dk, dv, dkv, band_ref = rest[
         piece_count + 9 :
     ]
     rows = query_ref.shape[0]
@@ -201,13 +201,9 @@
     context, first_end, second_end = scalars[0], scalars[1], scalars[2]
     tiles_here = rows // tile
     for index, piece in enumerate(pieces):
-        grad_branch[pl.ds(aligned(offsets[index], 128), piece.shape[0]), :] = piece[...]
-    lane_low = lax.broadcasted_iota(jnp.int32, (output_ref.shape[0], 128), 1)
-    last_head = jnp.where(lane_low < width, output_ref[:, 128:256].astype(f32), 0.0)
-    ordered = jnp.concatenate(
-        [pltpu.roll(last_head, width, 1).astype(bf16), output_ref[:, 0:128]], axis=1
-    )
-    dout[...] = dot_nn(grad_branch[...], ordered).astype(bf16)
+        span = pl.ds(aligned(offsets[index], 128), piece.shape[0])
+        dout[span, 0:128] = pltpu.roll(piece[:, 128:256].astype(f32), width, 1).astype(bf16)
+        dout[span, 128:256] = piece[:, 0:128]
     head_row = lax.broadcasted_iota(jnp.int32, (16, 256), 0)
     head_lane = lax.broadcasted_iota(jnp.int32, (16, 256), 1) // width
     head_hot = (head_row == jnp.where(head_lane == 1, 2, head_lane - 2)).astype(bf16)
@@ -370,12 +366,11 @@
 
 
 def attention_backward(
-    scalars, far_bias, offsets, queries, keys_values, bias_tiles, lse, packed, output_part, pieces, heads, width
+    scalars, far_bias, offsets, queries, keys_values, bias_tiles, lse, packed, pieces, heads, width
 ):
     rows = queries.shape[0]
     half = rows // 2
     group_rows = keys_values.shape[0]
-    model = output_part.shape[0]
     shape = jax.ShapeDtypeStruct
     return pl.pallas_call(
         functools.partial(attention_backward_kernel, heads, width, len(pieces)),
@@ -385,10 +380,9 @@
         )
         + (shape((half, 384), bf16),) * 6
         + (shape((8, tile), f32),),
-        in_specs=[SMEM, SMEM, SMEM] + [VMEM] * (7 + len(pieces)),
+        in_specs=[SMEM, SMEM, SMEM] + [VMEM] * (6 + len(pieces)),
         out_specs=(VMEM,) * 9,
         scratch_shapes=[
-            pltpu.VMEM((rows, model), bf16),
             pltpu.VMEM((rows, 256), bf16),
             pltpu.VMEM((heads, rows, 256), bf16),
             pltpu.VMEM((heads, rows, 256), bf16),
@@ -407,7 +401,7 @@
             transcendentals=rows * group_rows * heads,
         ),
         name="attention_backward",
-    )(scalars, far_bias, offsets, queries, keys_values, bias_tiles, lse, *packed, output_part, *pieces)
+    )(scalars, far_bias, offsets, queries, keys_values, bias_tiles, lse, *packed, *pieces)
 
 
 bucket_edges = np.array(
@@ -424,13 +418,6 @@
     return np.where(clipped < 16, clipped, 16 + counted).astype(np.int32)
 
 
-def bias_of(table, buckets):
-    out = jnp.broadcast_to(table[0][None, :, None, None], (buckets.shape[0], table.shape[1]) + buckets.shape[1:])
-    for b in range(1, table.shape[0]):
-        out = jnp.where(buckets[:, None] >= b, table[b][None, :, None, None], out)
-    return out
-
-
 def shape(dims, dtype):
     return jax.ShapeDtypeStruct(dims, dtype)
 
@@ -447,7 +434,10 @@
     return 0.7978845608028654, 0.044715
 
 
-def place_kernel(capacity, scalars, route_ref, order_ref, rows_ref, columns_ref, ranks, hot_ref, tall):
+def prepare_kernel(
+    capacity, padded, scalars, table, route_ref, order_ref, rows_ref, columns_ref,
+    bias_ref, ranks, hot_ref, tall,
+):
     pair_count = order_ref.shape[1]
     rows = pair_count // 2
     expert_pad = hot_ref.shape[0]
@@ -465,8 +455,8 @@
         pair = start + lax.broadcasted_iota(jnp.int32, (step, pair_count), 0)
         hit = (pair == order).astype(f32).astype(bf16)
         found = dot_nn(hit, digits)
-        rank = found[:, 0:1] * 64.0 + found[:, 1:2]
-        ranks[pl.ds(start, step), :] = jnp.broadcast_to(rank, (step, 128))
+        position = found[:, 0:1] * 64.0 + found[:, 1:2]
+        ranks[pl.ds(start, step), :] = jnp.broadcast_to(position, (step, 128))
         return carry
 
     lax.fori_loop(0, pair_count // step, rank_step, 0)
@@ -488,7 +478,7 @@
         0, pair_count // step, count_step, jnp.zeros((expert_pad, pair_count), f32)
     )
     slot = jnp.sum(counts * hot, axis=0, keepdims=True).astype(jnp.int32)
-    place = jnp.where(live_row & (slot < capacity), expert_row * capacity + slot, -1)
+    place = jnp.where(live_row & (slot < capacity), expert_row * padded + slot, -1)
     rows_ref[...] = jnp.full_like(rows_ref, -1)
     rows_ref[0:1, :] = place[:, 0:rows]
     rows_ref[1:2, :] = place[:, rows:]
@@ -496,25 +486,51 @@
     tall[0:1, :] = place[:, 0:rows].astype(f32)
     tall[1:2, :] = place[:, rows:].astype(f32)
     columns_ref[...] = tall[...].T.astype(jnp.int32)
-
-
-def find_places(scalars, route_rows, order_row, expert_count, capacity):
+    key = lax.broadcasted_iota(jnp.int32, (8, tile), 0)
+    query = lax.broadcasted_iota(jnp.int32, (8, tile), 1)
+    heads = bias_ref.shape[1]
+    for head in range(heads):
+        bias_ref[2, head] = jnp.full((tile, tile), table[31, head], f32)
+
+    def bias_step(index, carry):
+        start = aligned(index * 8, 8)
+        for band in range(2):
+            lag = band * tile + query - key - start
+            found = [jnp.full((8, tile), table[0, head], f32) for head in range(heads)]
+            for bucket, edge in enumerate(list(range(1, 17)) + list(bucket_edges), start=1):
+                beyond = lag >= int(edge)
+                found = [
+                    jnp.where(beyond, table[bucket, head], found[head]) for head in range(heads)
+                ]
+            for head in range(heads):
+                bias_ref[band, head, pl.ds(start, 8), :] = found[head]
+        return carry
+
+    lax.fori_loop(0, tile // 8, bias_step, 0)
+
+
+def prepare(scalars, table, route_rows, order_row, expert_count, capacity, padded):
     rows = route_rows.shape[1]
+    heads = table.shape[1]
     expert_pad = max(16, expert_count)
     return pl.pallas_call(
-        functools.partial(place_kernel, capacity),
-        out_shape=(shape((8, rows), jnp.int32), shape((rows, 128), jnp.int32)),
-        in_specs=[SMEM, VMEM, VMEM],
-        out_specs=(VMEM, VMEM),
+        functools.partial(prepare_kernel, capacity, padded),
+        out_shape=(
+            shape((8, rows), jnp.int32),
+            shape((rows, 128), jnp.int32),
+            shape((3, heads, tile, tile), f32),
+        ),
+        in_specs=[SMEM, SMEM, VMEM, VMEM],
+        out_specs=(VMEM,) * 3,
         scratch_shapes=[
             pltpu.VMEM((2 * rows, 128), f32),
             pltpu.VMEM((expert_pad, 2 * rows), bf16),
             pltpu.VMEM((128, rows), f32),
         ],
         compiler_params=params(40),
-        cost_estimate=cost(4 * 4 * rows * rows * 128, 2**20),
-        name="find_places",
-    )(scalars, route_rows, order_row)
+        cost_estimate=cost(10 * 10**9, 3 * 2**20),
+        name="prepare",
+    )(scalars, table, route_rows, order_row)
 
 
 def project_kernel(piece_count, offsets, token_ref, *rest):
@@ -587,14 +603,23 @@
 
 
 def dispatch_kernel(
-    heads, width, capacity, expert_count, chunk_count, scalars, starts,
+    heads, width, expert_count, padded, piece_count, scalars, offsets,
     token_ref, gain_ref, route_ref, row_place, *rest
 ):
     attended = rest[0:8]
-    weights = rest[8:12]
-    residual_ref, hidden_ref, info_ref = rest[12:15]
-    chunks = rest[15 : 15 + chunk_count]
-    packed, joined, column = rest[15 + chunk_count :]
+    pieces = rest[8 : 8 + piece_count]
+    rest = rest[8 + piece_count :]
+    residual_ref, hidden_ref, info_ref, output_own, output_all, sent = rest[0:6]
+    packed, joined, weights, column = rest[6:]
+    for index, piece in enumerate(pieces):
+        weights[:, pl.ds(aligned(offsets[index], 16), piece.shape[1]), :] = piece[...]
+    output_own[...] = weights[0]
+    lane_weight = lax.broadcasted_iota(jnp.int32, (weights.shape[1], 128), 1)
+    for source in range(4):
+        output_all[source, :, 0:128] = weights[source, :, 0:128]
+        output_all[source, :, 128:256] = jnp.where(
+            lane_weight < width, weights[source, :, 128:256], jnp.zeros_like(lane_weight, bf16)
+        )
     rows, model = token_ref.shape
     quarter = rows // 4
     lane_low = lax.broadcasted_iota(jnp.int32, (quarter, 128), 1)
@@ -619,12 +644,12 @@
         span = pl.ds(start, step)
         residual = token_ref[span, :].astype(f32)
         for source in range(4):
-            residual = residual + dot_nt(packed[source, span, :], weights[source][...])
+            residual = residual + dot_nt(packed[source, span, :], weights[source])
         joined[span, :] = residual
         scale = lax.rsqrt(jnp.mean(residual * residual, axis=-1, keepdims=True) + epsilon)
         hidden = (residual * scale * gain_ref[1:2, :]).astype(bf16)
         hidden_ref[span, :] = hidden
-        logits = dot_nn(hidden, weights[0][:, 128:256])
+        logits = dot_nn(hidden, weights[0, :, 128:256])
         logits = jnp.where(valid, logits, masked_value)
         powers = jnp.where(valid, jnp.exp(logits - jnp.max(logits, axis=-1, keepdims=True)), 0.0)
         probs = powers / jnp.sum(powers, axis=-1, keepdims=True)
@@ -647,248 +672,164 @@
     gates = info_ref[...].T
     gate_one, gate_two = gates[0:1, :], gates[1:2, :]
     place_one, place_two = row_place[0:1, :], row_place[1:2, :]
-    slot = lax.broadcasted_iota(jnp.int32, (capacity, rows), 0)
     column[...] = jnp.zeros_like(column)
 
-    def fill(chunk, entry, expert):
-        base = expert * capacity
-        hit_one = slot == place_one - base
-        hit_two = slot == place_two - base
+    def expert_rows(index, carry):
+        start = aligned(index * padded, 16)
+        slot = start + lax.broadcasted_iota(jnp.int32, (padded, rows), 0)
+        hit_one, hit_two = slot == place_one, slot == place_two
         picked = jnp.where(hit_one | hit_two, 1.0, 0.0).astype(bf16)
-        chunk[entry, 16:, :] = dot_nn(picked, hidden_ref[...]).astype(bf16)
+        sent[pl.ds(start, padded), :] = dot_nn(picked, hidden_ref[...]).astype(bf16)
         gate = jnp.where(hit_one, gate_one, 0.0) + jnp.where(hit_two, gate_two, 0.0)
-        gate = jnp.sum(gate, axis=-1, keepdims=True)
-        column[0:capacity, :] = jnp.broadcast_to(gate, (capacity, 128))
-        write_head(chunk, entry, column[...].T[0:1, :])
-
-    for chunk_index, chunk in enumerate(chunks):
-        if chunk.shape[0] == 1:
-            fill(chunk, 0, starts[chunk_index])
-        else:
-
-            def one(entry, carry):
-                fill(chunk, entry, starts[chunk_index] + entry)
-                return carry
-
-            lax.fori_loop(0, chunk.shape[0], one, 0)
-
-
-def write_head(chunk, entry, row):
-    high = row.astype(bf16)
-    left = row - high.astype(f32)
-    middle = left.astype(bf16)
-    low = (left - middle.astype(f32)).astype(bf16)
+        write_digits(sent, column, start, padded, jnp.sum(gate, axis=-1, keepdims=True))
+        return carry
+
+    lax.fori_loop(0, expert_count, expert_rows, 0)
+
+
+def write_digits(rows_ref, column, start, padded, values):
+    column[0:padded, :] = jnp.broadcast_to(values, (padded, 128))
+    row = column[...].T[0:1, :]
+    high = row.astype(bf16).astype(f32)
+    middle = (row - high).astype(bf16).astype(f32)
+    low = row - high - middle
     size = row.shape[1]
     index = lax.broadcasted_iota(jnp.int32, (16, size), 0)
     block = jnp.where(
-        index == 0,
-        high.astype(f32),
-        jnp.where(index == 1, middle.astype(f32), jnp.where(index == 2, low.astype(f32), 0.0)),
-    )
-    chunk[entry, 0:16, :] = jnp.zeros((16, chunk.shape[2]), bf16)
-    chunk[entry, 0:16, 0:size] = block.astype(bf16)
+        index == 0, high, jnp.where(index == 1, middle, jnp.where(index == 2, low, 0.0))
+    )
+    span = pl.ds(aligned(start + padded - 16, 16), 16)
+    rows_ref[span, 0:size] = block.astype(bf16)
+    rows_ref[span, size:] = jnp.zeros((16, rows_ref.shape[1] - size), bf16)
+
+
+def read_digits(rows_ref, start, padded):
+    wide = (padded + 127) // 128 * 128
+    span = pl.ds(aligned(start + padded - 16, 16), 16)
+    return jnp.sum(rows_ref[span, 0:wide].astype(f32), axis=0, keepdims=True)
 
 
 def dispatch(
-    scalars, starts, tokens, gains, routes, row_place, attended, weights, chunk_shapes,
-    heads, width, capacity, expert_count
+    scalars, offsets, tokens, gains, routes, row_place, attended, pieces,
+    heads, width, expert_count, padded
 ):
     rows, model = tokens.shape
-    pad = (capacity + 127) // 128 * 128
-    return pl.pallas_call(
-        functools.partial(
-            dispatch_kernel, heads, width, capacity, expert_count, len(chunk_shapes)
-        ),
+    slots = expert_count * padded
+    wide = (padded + 127) // 128 * 128
+    return pl.pallas_call(
+        functools.partial(dispatch_kernel, heads, width, expert_count, padded, len(pieces)),
         out_shape=(
             shape((rows // 4, model), f32),
             shape((rows, model), bf16),
             shape((rows, 128), f32),
-        )
-        + tuple(shape((per, capacity + 16, model), bf16) for per in chunk_shapes),
-        in_specs=[SMEM, SMEM] + [VMEM] * 16,
-        out_specs=(VMEM,) * (3 + len(chunk_shapes)),
+            shape((model, 256), bf16),
+            shape((4, model, 256), bf16),
+            shape((slots, model), bf16),
+        ),
+        in_specs=[SMEM, SMEM] + [VMEM] * (12 + len(pieces)),
+        out_specs=(VMEM,) * 6,
         scratch_shapes=[
             pltpu.VMEM((4, rows, 256), bf16),
             pltpu.VMEM((rows, model), f32),
-            pltpu.VMEM((pad, 128), f32),
+            pltpu.VMEM((4, model, 256), bf16),
+            pltpu.VMEM((wide, 128), f32),
         ],
         compiler_params=params(56),
-        cost_estimate=cost(2 * rows * model * (1024 + 2304), 16 * 2**20),
+        cost_estimate=cost(2 * rows * model * (1024 + slots), 16 * 2**20),
         name="dispatch",
-    )(scalars, starts, tokens, gains, routes, row_place, *attended, *weights)
-
-
-def scatter_kernel(capacity, chunk_count, starts, value_ref, row_place, *chunks):
+    )(scalars, offsets, tokens, gains, routes, row_place, *attended, *pieces)
+
+
+def scatter_kernel(value_ref, row_place, sent):
     rows = value_ref.shape[0]
     place_one, place_two = row_place[0:1, :], row_place[1:2, :]
-    slot = lax.broadcasted_iota(jnp.int32, (capacity, rows), 0)
-
-    def fill(chunk, entry, expert):
-        base = expert * capacity
-        hit = (slot == place_one - base) | (slot == place_two - base)
-        picked = jnp.where(hit, 1.0, 0.0).astype(bf16)
-        chunk[entry] = dot_nn(picked, value_ref[...]).astype(bf16)
-
-    for chunk_index, chunk in enumerate(chunks):
-        if chunk.shape[0] == 1:
-            fill(chunk, 0, starts[chunk_index])
-        else:
-
-            def one(entry, carry):
-                fill(chunk, entry, starts[chunk_index] + entry)
-                return carry
-
-            lax.fori_loop(0, chunk.shape[0], one, 0)
-
-
-def scatter_rows(starts, values, row_place, chunk_shapes, capacity):
+    fill = 128
+
+    def slot_step(index, carry):
+        start = aligned(index * fill, fill)
+        slot = start + lax.broadcasted_iota(jnp.int32, (fill, rows), 0)
+        picked = jnp.where((slot == place_one) | (slot == place_two), 1.0, 0.0).astype(bf16)
+        sent[pl.ds(start, fill), :] = dot_nn(picked, value_ref[...]).astype(bf16)
+        return carry
+
+    lax.fori_loop(0, sent.shape[0] // fill, slot_step, 0)
+
+
+def scatter_rows(values, row_place, slots):
     rows, model = values.shape
     return pl.pallas_call(
-        functools.partial(scatter_kernel, capacity, len(chunk_shapes)),
-        out_shape=tuple(shape((per, capacity, model), bf16) for per in chunk_shapes),
-        in_specs=[SMEM, VMEM, VMEM],
-        out_specs=(VMEM,) * len(chunk_shapes),
+        scatter_kernel,
+        out_shape=shape((slots, model), bf16),
+        in_specs=[VMEM, VMEM],
+        out_specs=VMEM,
         compiler_params=params(40),
-        cost_estimate=cost(2 * rows * model * 2304, 6 * 2**20),
+        cost_estimate=cost(2 * rows * model * slots, 6 * 2**20),
         name="scatter_rows",
-    )(starts, values, row_place)
-
-
-def expert_kernel(chunk_count, in_ref, out_ref, *rest):
-    row_chunks = rest[:chunk_count]
-    grad_chunks = rest[chunk_count : 2 * chunk_count]
-    rows_all, grads_all, acted_all, pre_all = rest[2 * chunk_count : 2 * chunk_count + 4]
-    returns = rest[2 * chunk_count + 4 : 3 * chunk_count + 4]
-    held, column = rest[3 * chunk_count + 4 :]
-    source_count, capacity, model = rows_all.shape
+    )(values, row_place)
+
+
+def expert_kernel(padded, in_ref, out_ref, rows_ref, grads_ref, acted_ref, pre_ref, gate_ref, back_ref, held, column):
+    model = rows_ref.shape[1]
+    hidden = in_ref.shape[2]
     root, cubic = gelu_constants()
-    at = 0
-    for chunk, grads in zip(row_chunks, grad_chunks):
-        per = chunk.shape[0]
-        rows_all[at : at + per] = chunk[:, 16:, :]
-        grads_all[at : at + per] = grads[...]
-        at += per
+    wide = column.shape[0]
     column[...] = jnp.zeros_like(column)
 
-    def one(source, carry):
-        pre = dot_nn(rows_all[source], in_ref[0])
-        square = pre * pre
-        bent = jnp.tanh(root * pre * (1.0 + cubic * square))
-        acted = (0.5 * pre * (1.0 + bent)).astype(bf16)
-        slope = 0.5 * (1.0 + bent) + 0.5 * pre * (1.0 - bent * bent) * root * (
-            1.0 + 3.0 * cubic * square
-        )
-        grad_acted = dot_nt(grads_all[source], out_ref[0])
-        acted_all[source] = acted
-        gate_grad = jnp.sum(grad_acted * acted.astype(f32), axis=-1, keepdims=True)
-        column[0:capacity, :] = jnp.broadcast_to(gate_grad, (capacity, 128))
-        grad_pre = (grad_acted * slope).astype(bf16)
-        pre_all[source] = grad_pre
-        held[source, 16:, :] = dot_nt(grad_pre, in_ref[0]).astype(bf16)
-        write_head(held, source, column[...].T[0:1, :])
+    def one(index, carry):
+        start = aligned(index * padded, 16)
+        span = pl.ds(start, padded)
+        gate_part = None
+        for first in range(0, hidden, 256):
+            part = slice(first, first + 256)
+            pre = dot_nn(rows_ref[span, :], in_ref[0, :, part])
+            grad_acted = dot_nt(grads_ref[span, :], out_ref[0, part, :])
+            square = pre * pre
+            bent = jnp.tanh(root * pre * (1.0 + cubic * square))
+            acted = (0.5 * pre * (1.0 + bent)).astype(bf16)
+            slope = 0.5 * (1.0 + bent) + 0.5 * pre * (1.0 - bent * bent) * root * (
+                1.0 + 3.0 * cubic * square
+            )
+            acted_ref[span, part] = acted
+            product = grad_acted * acted.astype(f32)
+            folded = product[:, 0:128] + product[:, 128:256]
+            gate_part = folded if gate_part is None else gate_part + folded
+            held[:, part] = (grad_acted * slope).astype(bf16)
+        pre_ref[span, :] = held[...]
+        back_ref[span, :] = dot_nt(held[...], in_ref[0]).astype(bf16)
+        write_digits(back_ref, column, start, padded, jnp.sum(gate_part, axis=-1, keepdims=True))
+        gates = jnp.broadcast_to(read_digits(rows_ref, start, padded), (128, wide))
+        gate_ref[span, :] = gates.T[0:padded, :]
         return carry
 
-    lax.fori_loop(0, source_count, one, 0)
-    at = 0
-    for returned in returns:
-        per = returned.shape[0]
-        returned[...] = held[at : at + per]
-        at += per
-
-
-def expert_step(weight_in, weight_out, row_chunks, grad_chunks):
-    count = len(row_chunks)
-    sources = sum(chunk.shape[0] for chunk in row_chunks)
-    _, capacity, model = grad_chunks[0].shape
+    lax.fori_loop(0, rows_ref.shape[0] // padded, one, 0)
+
+
+def expert_step(weight_in, weight_out, rows_in, grads_in, padded):
+    slots, model = rows_in.shape
     hidden = weight_in.shape[2]
-    pad = (capacity + 127) // 128 * 128
-    return pl.pallas_call(
-        functools.partial(expert_kernel, count),
+    wide = (padded + 127) // 128 * 128
+    return pl.pallas_call(
+        functools.partial(expert_kernel, padded),
         out_shape=(
-            shape((sources, capacity, model), bf16),
-            shape((sources, capacity, model), bf16),
-            shape((sources, capacity, hidden), bf16),
-            shape((sources, capacity, hidden), bf16),
-        )
-        + tuple(shape(chunk.shape, bf16) for chunk in row_chunks),
-        in_specs=[VMEM] * (2 + 2 * count),
-        out_specs=(VMEM,) * (4 + count),
-        scratch_shapes=[
-            pltpu.VMEM((sources, capacity + 16, model), bf16),
-            pltpu.VMEM((pad, 128), f32),
-        ],
+            shape((slots, hidden), bf16),
+            shape((slots, hidden), bf16),
+            shape((slots, 128), f32),
+            shape((slots, model), bf16),
+        ),
+        in_specs=[VMEM] * 4,
+        out_specs=(VMEM,) * 4,
+        scratch_shapes=[pltpu.VMEM((padded, hidden), bf16), pltpu.VMEM((wide, 128), f32)],
         compiler_params=params(60),
-        cost_estimate=cost(6 * sources * capacity * model * hidden, 30 * 2**20),
+        cost_estimate=cost(6 * slots * model * hidden, 24 * 2**20),
         name="expert_step",
-    )(weight_in, weight_out, *row_chunks, *grad_chunks)
-
-
-def expert_out_kernel(acted_all, out_ref, *rest):
-    chunks, held = rest[:-1], rest[-1]
-
-    def one(source, carry):
-        held[source] = dot_nn(acted_all[source], out_ref[0]).astype(bf16)
-        return carry
-
-    lax.fori_loop(0, held.shape[0], one, 0)
-    at = 0
-    for chunk in chunks:
-        per = chunk.shape[0]
-        chunk[...] = held[at : at + per]
-        at += per
-
-
-def expert_outputs(acted_all, weight_out, chunk_shapes):
-    sources, capacity, hidden = acted_all.shape
-    model = weight_out.shape[2]
-    return pl.pallas_call(
-        expert_out_kernel,
-        out_shape=tuple(shape((per, capacity, model), bf16) for per in chunk_shapes),
-        in_specs=[VMEM, VMEM],
-        out_specs=(VMEM,) * len(chunk_shapes),
-        scratch_shapes=[pltpu.VMEM((sources, capacity, model), bf16)],
-        compiler_params=params(40),
-        cost_estimate=cost(2 * sources * capacity * model * hidden, 10 * 2**20),
-        name="expert_outputs",
-    )(acted_all, weight_out)
-
-
-def gather_rows(chunks, head, starts, place, info, capacity):
-    tokens = place.shape[0]
-    slot = lax.broadcasted_iota(jnp.int32, (tokens, capacity), 1)
-    gate_one, gate_two = info[:, 0:1], info[:, 1:2]
-    place_one, place_two = place[:, 0:1], place[:, 1:2]
-    total, grad_one, grad_two = None, None, None
-
-    def one(chunk, entry, expert):
-        base = expert * capacity
-        hit_one = slot == place_one - base
-        hit_two = slot == place_two - base
-        weights = jnp.where(hit_one, gate_one, jnp.where(hit_two, gate_two, 0.0)).astype(bf16)
-        out = dot_nn(weights, chunk[entry, head:, :])
-        if head == 0:
-            return (out,)
-        row = jnp.sum(chunk[entry, 0:16, 0:capacity].astype(f32), axis=0, keepdims=True)
-        first = jnp.sum(jnp.where(hit_one, row, 0.0), axis=-1, keepdims=True)
-        second = jnp.sum(jnp.where(hit_two, row, 0.0), axis=-1, keepdims=True)
-        return out, first, second
-
-    sums = None
-    for index, chunk in enumerate(chunks):
-        if chunk.shape[0] == 1:
-            parts = one(chunk, 0, starts[index])
-        else:
-
-            def step(entry, carry, chunk=chunk, index=index):
-                found = one(chunk, entry, starts[index] + entry)
-                return tuple(a + b for a, b in zip(carry, found))
-
-            zero = (jnp.zeros((tokens, chunk.shape[2]), f32),)
-            if head:
-                zero = zero + (jnp.zeros((tokens, 1), f32),) * 2
-            parts = lax.fori_loop(0, chunk.shape[0], step, zero)
-        sums = parts if sums is None else tuple(a + b for a, b in zip(sums, parts))
-    return sums
+    )(weight_in, weight_out, rows_in, grads_in)
+
+
+def weights_of(place, info, slots):
+    slot = lax.broadcasted_iota(jnp.int32, (place.shape[0], slots), 1)
+    hit_one, hit_two = slot == place[:, 0:1], slot == place[:, 1:2]
+    weights = jnp.where(hit_one, info[:, 0:1], jnp.where(hit_two, info[:, 1:2], 0.0))
+    return hit_one, hit_two, weights.astype(bf16)
 
 
 def write_ring(scalars, joined, own, next_one, next_two, last_one, last_two, far_one, far_two):
@@ -911,29 +852,45 @@
 
 
 def combine_grads_kernel(
-    capacity, expert_count, chunk_count, scalars, starts, place_ref, info_ref, route_ref, router_ref, *rest
+    expert_count, padded, scalars, place_ref, info_ref, route_ref, router_ref, back_ref,
+    logit_ref, *rest
 ):
-    chunks = rest[:chunk_count]
-    logit_ref = rest[chunk_count]
-    ring = rest[chunk_count + 1 : chunk_count + 8]
-    joined = rest[chunk_count + 8]
+    ring, joined, digits = rest[:7], rest[7], rest[8]
     rows = place_ref.shape[0]
+    slots = back_ref.shape[0]
+    wide = (padded + 127) // 128 * 128
+    lane_digit = lax.broadcasted_iota(jnp.int32, (padded, 128), 1)
+
+    def column_step(expert, carry):
+        start = aligned(expert * padded, 16)
+        row = jnp.broadcast_to(read_digits(back_ref, start, padded), (128, wide))
+        column = row.T[0:padded, :]
+        high = column.astype(bf16).astype(f32)
+        middle = (column - high).astype(bf16).astype(f32)
+        digits[pl.ds(start, padded), :] = jnp.where(
+            lane_digit == 0,
+            high,
+            jnp.where(lane_digit == 1, middle, jnp.where(lane_digit == 2, column - high - middle, 0.0)),
+        ).astype(bf16)
+        return carry
+
+    lax.fori_loop(0, expert_count, column_step, 0)
     step = 256
     lane = lax.broadcasted_iota(jnp.int32, (step, 128), 1)
+    slot = lax.broadcasted_iota(jnp.int32, (step, slots), 1)
 
     def token_step(index, carry):
-        start = aligned(index * step, step)
-        span = pl.ds(start, step)
-        info = info_ref[span, :]
-        total, first, second = gather_rows(
-            chunks, 16, starts, place_ref[span, :], info, capacity
-        )
-        mix = first * info[:, 0:1] + second * info[:, 1:2]
-        pair_total = info[:, 2:3]
+        span = pl.ds(aligned(index * step, step), step)
+        info, place = info_ref[span, :], place_ref[span, :]
+        hit_one, hit_two = slot == place[:, 0:1], slot == place[:, 1:2]
+        weights = jnp.where(hit_one, info[:, 0:1], jnp.where(hit_two, info[:, 1:2], 0.0))
+        total = dot_nn(weights.astype(bf16), back_ref[...])
+        signs = jnp.where(hit_one, 1.0, jnp.where(hit_two, -1.0, 0.0)).astype(bf16)
+        difference = jnp.sum(dot_nn(signs, digits[...]), axis=-1, keepdims=True) / info[:, 2:3]
         picked = jnp.where(
             lane == route_ref[span, 0:1] + 64,
-            (first - mix) / pair_total,
-            jnp.where(lane == route_ref[span, 1:2] + 64, (second - mix) / pair_total, 0.0),
+            info[:, 1:2] * difference,
+            jnp.where(lane == route_ref[span, 1:2] + 64, -info[:, 0:1] * difference, 0.0),
         )
         probs = jnp.where((lane >= 64) & (lane < 64 + expert_count), info, 0.0)
         grads = probs * (picked - jnp.sum(probs * picked, axis=-1, keepdims=True))
@@ -946,53 +903,46 @@
     write_ring(scalars, joined, *ring)
 
 
-def combine_grads(scalars, starts, place, info, routes, router, chunks, capacity, expert_count):
+def combine_grads(scalars, place, info, routes, router, back, expert_count, padded):
     rows = place.shape[0]
     model = router.shape[0]
-    return pl.pallas_call(
-        functools.partial(combine_grads_kernel, capacity, expert_count, len(chunks)),
+    slots = back.shape[0]
+    return pl.pallas_call(
+        functools.partial(combine_grads_kernel, expert_count, padded),
         out_shape=(shape((rows, 128), bf16),) + ring_shapes(rows, model),
-        in_specs=[SMEM, SMEM] + [VMEM] * (4 + len(chunks)),
+        in_specs=[SMEM] + [VMEM] * 5,
         out_specs=(VMEM,) * 8,
-        scratch_shapes=[pltpu.VMEM((rows, model), f32)],
+        scratch_shapes=[pltpu.VMEM((rows, model), f32), pltpu.VMEM((slots, 128), bf16)],
         compiler_params=params(56),
-        cost_estimate=cost(2 * rows * model * 2304, 10 * 2**20),
+        cost_estimate=cost(2 * rows * model * slots, 8 * 2**20),
         name="combine_grads",
-    )(scalars, starts, place, info, routes, router, *chunks)
-
-
-def combine_outs_kernel(capacity, chunk_count, scalars, starts, place_ref, info_ref, *rest):
-    chunks = rest[:chunk_count]
-    ring = rest[chunk_count : chunk_count + 7]
-    joined = rest[chunk_count + 7]
-    rows = place_ref.shape[0]
+    )(scalars, place, info, routes, router, back)
+
+
+def combine_outs_kernel(place_ref, info_ref, rows_ref, out_ref):
     step = 256
 
     def token_step(index, carry):
         span = pl.ds(aligned(index * step, step), step)
-        (total,) = gather_rows(
-            chunks, 0, starts, place_ref[span, :], info_ref[span, :], capacity
-        )
-        joined[span, :] = total
+        weights = weights_of(place_ref[span, :], info_ref[span, :], rows_ref.shape[0])[2]
+        out_ref[span, :] = dot_nn(weights, rows_ref[...]).astype(bf16)
         return carry
 
-    lax.fori_loop(0, rows // step, token_step, 0)
-    write_ring(scalars, joined, *ring)
-
-
-def combine_outs(scalars, starts, place, info, chunks, capacity):
+    lax.fori_loop(0, out_ref.shape[0] // step, token_step, 0)
+
+
+def combine_outs(place, info, rows_in):
     rows = place.shape[0]
-    model = chunks[0].shape[2]
-    return pl.pallas_call(
-        functools.partial(combine_outs_kernel, capacity, len(chunks)),
-        out_shape=ring_shapes(rows, model),
-        in_specs=[SMEM, SMEM] + [VMEM] * (2 + len(chunks)),
-        out_specs=(VMEM,) * 7,
-        scratch_shapes=[pltpu.VMEM((rows, model), f32)],
+    slots, model = rows_in.shape
+    return pl.pallas_call(
+        combine_outs_kernel,
+        out_shape=shape((rows, model), bf16),
+        in_specs=[VMEM] * 3,
+        out_specs=VMEM,
         compiler_params=params(56),
-        cost_estimate=cost(2 * rows * model * 2304, 10 * 2**20),
+        cost_estimate=cost(2 * rows * model * slots, 8 * 2**20),
         name="combine_outs",
-    )(scalars, starts, place, info, *chunks)
+    )(place, info, rows_in)
 
 
 def received(own, next_one, next_two, last_one, last_two):
@@ -1004,7 +954,10 @@
 
 def norm_back_kernel(gain_index, has_bypass_rows, scalars, value_ref, gain_ref, bypass_ref, *rest):
     grads = received(*rest[:5])
-    full_ref, one_ref, two_ref, gain_grad = rest[5:]
+    rest = rest[5:]
+    if gain_index == 1:
+        weight_ref, rest = rest[0], rest[1:]
+    full_ref, one_ref, two_ref, gain_grad = rest[0:4]
     quarter = grads.shape[0]
     eighth = quarter // 2
     here = pl.ds(aligned(scalars[3] * quarter, quarter), quarter)
@@ -1018,12 +971,16 @@
     )
     out = bypass + scale * (scaled - normed * jnp.mean(scaled * normed, axis=-1, keepdims=True))
     full_ref[...] = out
-    one_ref[...] = out[0:eighth].astype(bf16)
-    two_ref[...] = out[eighth:].astype(bf16)
-
-
-def norm_back(gain_index, has_bypass_rows, scalars, values, gains, bypass, parts):
+    low = out.astype(bf16)
+    one_ref[...] = low[0:eighth]
+    two_ref[...] = low[eighth:]
+    for source, target in enumerate(rest[4:]):
+        target[...] = dot_nn(low, weight_ref[source]).astype(bf16)
+
+
+def norm_back(gain_index, has_bypass_rows, scalars, values, gains, bypass, parts, weights=None):
     quarter, model = parts[0].shape
+    extra = () if weights is None else (weights,)
     return pl.pallas_call(
         functools.partial(norm_back_kernel, gain_index, has_bypass_rows),
         out_shape=(
@@ -1031,34 +988,37 @@
             shape((quarter // 2, model), bf16),
             shape((quarter // 2, model), bf16),
             shape((8, model), f32),
-        ),
-        in_specs=[SMEM] + [VMEM] * 8,
-        out_specs=(VMEM,) * 4,
+        )
+        + (shape((quarter, 256), bf16),) * (4 * len(extra)),
+        in_specs=[SMEM] + [VMEM] * (8 + len(extra)),
+        out_specs=(VMEM,) * (4 + 4 * len(extra)),
         compiler_params=params(40),
         cost_estimate=cost(quarter * model * 16, 6 * 2**20),
         name="norm_back",
-    )(scalars, values, gains, bypass, *parts)
-
-
-def finish_kernel(residual_ref, *rest):
-    total = residual_ref[...] + received(*rest[:5])
-    one_ref, two_ref = rest[5:]
-    eighth = one_ref.shape[0]
-    one_ref[...] = total[0:eighth].astype(bf16)
-    two_ref[...] = total[eighth:].astype(bf16)
+    )(scalars, values, gains, bypass, *parts, *extra)
+
+
+def finish_kernel(residual_ref, part_ref, out_ref):
+    total = residual_ref[...]
+    quarter = total.shape[0]
+    for source in range(4):
+        total = total + part_ref[source * quarter : (source + 1) * quarter, :].astype(f32)
+    low = total.astype(bf16)
+    for target in range(4):
+        out_ref[target * quarter : (target + 1) * quarter, :] = low
 
 
 def finish(residual, parts):
     quarter, model = residual.shape
     return pl.pallas_call(
         finish_kernel,
-        out_shape=(shape((quarter // 2, model), bf16),) * 2,
-        in_specs=[VMEM] * 6,
-        out_specs=(VMEM,) * 2,
+        out_shape=shape((4 * quarter, model), bf16),
+        in_specs=[VMEM] * 2,
+        out_specs=VMEM,
         compiler_params=params(40),
         cost_estimate=cost(quarter * model * 4, 4 * 2**20),
         name="finish",
-    )(residual, *parts)
+    )(residual, parts)
 
 
 def hidden_grad_kernel(scalars, dq_ref, weight_ref, own, from_one, from_two, dkv_ref, *rest):
@@ -1097,6 +1057,108 @@
     )(scalars, dq, weights, own, *from_one, *from_two)
 
 
+def split_by_side(scalars, whole, mine, other):
+    half = mine.shape[0]
+    side = scalars[5]
+    mine[...] = whole[pl.ds(aligned(side * half, 16), half), :]
+    other[...] = whole[pl.ds(aligned((1 - side) * half, 16), half), :]
+
+
+def output_grad_kernel(
+    piece_count, width, scalars, offsets, hidden_ref, logit_ref, packed_one, packed_two, *rest
+):
+    pieces = rest[:piece_count]
+    outs = rest[piece_count:-3]
+    grads, attended, whole = rest[-3:]
+    quarter = packed_one.shape[0]
+    for index, piece in enumerate(pieces):
+        grads[pl.ds(aligned(offsets[index], 16), piece.shape[0]), :] = piece[...]
+    lane = lax.broadcasted_iota(jnp.int32, (quarter, 128), 1)
+    for part, packed in enumerate((packed_one, packed_two)):
+        span = slice(part * quarter, (part + 1) * quarter)
+        middle = packed[:, 128:256].astype(f32)
+        attended[span, 0:128] = packed[:, 0:128]
+        attended[span, 128:256] = jnp.where(lane < width, middle, 0.0).astype(bf16)
+        span = slice((part + 2) * quarter, (part + 3) * quarter)
+        attended[span, 0:128] = packed[:, 256:384]
+        attended[span, 128:256] = jnp.where(lane < width, pltpu.roll(middle, 64, 1), 0.0).astype(bf16)
+    whole[...] = dot_tn(grads[...], attended[...])
+    whole[:, 128:256] += dot_tn(hidden_ref[...], logit_ref[...])
+    if len(outs) == 2:
+        split_by_side(scalars, whole, *outs)
+    else:
+        outs[0][...] = whole[...]
+
+
+def output_grads(scalars, offsets, hidden, grad_logits, packed, pieces, width, small):
+    rows, model = hidden.shape
+    outs = (shape((model // 2, 256), f32),) * 2 if small else (shape((model, 256), f32),)
+    return pl.pallas_call(
+        functools.partial(output_grad_kernel, len(pieces), width),
+        out_shape=outs,
+        in_specs=[SMEM, SMEM] + [VMEM] * (4 + len(pieces)),
+        out_specs=(VMEM,) * len(outs),
+        scratch_shapes=[
+            pltpu.VMEM((rows, model), bf16),
+            pltpu.VMEM((rows, 256), bf16),
+            pltpu.VMEM((model, 256), f32),
+        ],
+        compiler_params=params(40),
+        cost_estimate=cost(2 * rows * model * 384, 6 * 2**20),
+        name="output_grads",
+    )(scalars, offsets, hidden, grad_logits, *packed, *pieces)
+
+
+def projection_grad_kernel(scalars, hidden_ref, dq_ref, dkv_ref, gain_ref, *rest):
+    outs, whole = rest[:-1], rest[-1]
+    hidden = hidden_ref[...]
+    whole[:, 0:256] = dot_tn(hidden, dq_ref[...])
+    whole[:, 256:640] = dot_tn(hidden, dkv_ref[...])
+    lane = lax.broadcasted_iota(jnp.int32, (whole.shape[0], 128), 1)
+    column = jnp.broadcast_to(gain_ref[0:1, :], (128, whole.shape[0])).T
+    whole[:, 128:256] = jnp.where(lane < 64, whole[:, 128:256], column)
+    if len(outs) == 2:
+        split_by_side(scalars, whole, *outs)
+    else:
+        outs[0][...] = whole[...]
+
+
+def projection_grads(scalars, hidden, dq, dkv, gain_grad, small):
+    rows, model = hidden.shape
+    outs = (shape((model // 2, 640), f32),) * 2 if small else (shape((model, 640), f32),)
+    return pl.pallas_call(
+        projection_grad_kernel,
+        out_shape=outs,
+        in_specs=[SMEM] + [VMEM] * 4,
+        out_specs=(VMEM,) * len(outs),
+        scratch_shapes=[pltpu.VMEM((model, 640), f32)],
+        compiler_params=params(40),
+        cost_estimate=cost(2 * rows * model * 640, 6 * 2**20),
+        name="projection_grads",
+    )(scalars, hidden, dq, dkv, gain_grad)
+
+
+def share_kernel(scalars, mine, other, *outs):
+    size = outs[0].shape[0]
+    context = scalars[0]
+    for mask, out in enumerate(outs):
+        span = pl.ds(aligned((context ^ mask) * size, 16), size)
+        out[...] = mine[span, :] + other[span, :]
+
+
+def share(scalars, mine, other):
+    rows, width = mine.shape
+    return pl.pallas_call(
+        share_kernel,
+        out_shape=(shape((rows // 4, width), f32),) * 4,
+        in_specs=[SMEM, VMEM, VMEM],
+        out_specs=(VMEM,) * 4,
+        compiler_params=params(40),
+        cost_estimate=cost(rows * width, 12 * rows * width),
+        name="share",
+    )(scalars, mine, other)
+
+
 def shift(value, amount):
     size = lax.axis_size("tensor")
     return lax.ppermute(value, "tensor", [(i, (i + amount) % size) for i in range(size)])
@@ -1122,12 +1184,20 @@
     return (first.astype(f32) + second.astype(f32)).astype(bf16)
 
 
-def ring_reduce(own, next_one, next_two, last_one, last_two, far_one, far_two):
-    arrived_one, arrived_two = shift(far_one, 1), shift(far_two, -1)
+def ring_start(far_one, far_two):
+    return shift(far_one, 1), shift(far_two, -1)
+
+
+def ring_finish(next_one, next_two, last_one, last_two, arrived_one, arrived_two):
     from_last_two, from_next_one = shift(next_two, 1), shift(last_one, -1)
     from_last_one = shift(added(next_one, arrived_one), 1)
     from_next_two = shift(added(last_two, arrived_two), -1)
-    return (own, from_last_one, from_last_two, from_next_one, from_next_two)
+    return (from_last_one, from_last_two, from_next_one, from_next_two)
+
+
+def ring_reduce(own, next_one, next_two, last_one, last_two, far_one, far_two):
+    arrived = ring_start(far_one, far_two)
+    return (own,) + ring_finish(next_one, next_two, last_one, last_two, *arrived)
 
 
 def square_gather(one, two):
@@ -1145,46 +1215,45 @@
     return (from_beside_one, from_beside_two), (from_across_one, from_across_two)
 
 
+def doubled(value, axis, masks):
+    for mask in masks:
+        size = lax.axis_size(axis)
+        value = value + lax.ppermute(value, axis, [(i, i ^ mask) for i in range(size)])
+    return value
+
+
+def sum_rows(value, small):
+    if not small:
+        return lax.psum(value, ALL_ROWS)
+    return doubled(doubled(value, "dp", (1,)), "context", (1, 2))
+
+
 ALL_ROWS = ("dp", "context")
 
 
-def exchange(chunks):
-    count = lax.axis_size("dp") * lax.axis_size("context")
-    if len(chunks) == 1:
-        return [lax.all_to_all(chunks[0], ALL_ROWS, split_axis=0, concat_axis=0, tiled=True)]
-    return [
-        chunk if j == 0 else lax.ppermute(chunk, ALL_ROWS, [(d, d ^ j) for d in range(count)])
-        for j, chunk in enumerate(chunks)
-    ]
-
-
-def gather_weights(block, here, small):
-    count = lax.axis_size("dp") * lax.axis_size("context")
-    size = block.shape[0]
+def exchange(rows_out):
+    return lax.all_to_all(rows_out, ALL_ROWS, split_axis=0, concat_axis=0, tiled=True)
+
+
+def gather_weights(block, small, axis):
+    size = block.shape[axis]
     if not small:
-        whole = lax.all_gather(block, ALL_ROWS, axis=0, tiled=True)
+        whole = lax.all_gather(block, ALL_ROWS, axis=axis, tiled=True)
         return [whole], jnp.zeros((1,), jnp.int32)
-    pieces = [
-        block if j == 0 else lax.ppermute(block, ALL_ROWS, [(d, d ^ j) for d in range(count)])
-        for j in range(count)
-    ]
-    return pieces, jnp.stack([(here ^ j) * size for j in range(count)])
-
-
-def scatter_weights(whole, small):
-    if not small:
-        return lax.psum_scatter(whole, ALL_ROWS, scatter_dimension=0, tiled=True)
-    side, context = lax.axis_index("dp"), lax.axis_index("context")
-    halves = whole.reshape((2, whole.shape[0] // 2) + whole.shape[1:])
-    mine = lax.dynamic_index_in_dim(halves, side, 0, keepdims=False)
-    other = lax.dynamic_index_in_dim(halves, 1 - side, 0, keepdims=False)
-    mine = mine + lax.ppermute(other, "dp", [(0, 1), (1, 0)])
-    blocks = mine.reshape((4, mine.shape[0] // 4) + mine.shape[1:])
-    total = lax.dynamic_index_in_dim(blocks, context, 0, keepdims=False)
-    for mask in (1, 2, 3):
-        part = lax.dynamic_index_in_dim(blocks, context ^ mask, 0, keepdims=False)
-        total = total + cross(part, mask)
-    return total
+    context, side = lax.axis_index("context"), lax.axis_index("dp")
+    pieces = [block] + [cross(block, mask) for mask in (1, 2, 3)]
+    pieces = pieces + [lax.ppermute(piece, "dp", [(0, 1), (1, 0)]) for piece in pieces]
+    return pieces, jnp.stack(
+        [((side ^ far) * 4 + (context ^ mask)) * size for far in range(2) for mask in range(4)]
+    )
+
+
+def scatter_weights(scalars, parts):
+    if len(parts) == 1:
+        return lax.psum_scatter(parts[0], ALL_ROWS, scatter_dimension=0, tiled=True)
+    mine, other = parts
+    blocks = share(scalars, mine, lax.ppermute(other, "dp", [(0, 1), (1, 0)]))
+    return blocks[0] + cross(blocks[1], 1) + cross(blocks[2], 2) + cross(blocks[3], 3)
 
 
 def on_device(
@@ -1203,10 +1272,10 @@
     here = lax.axis_index("dp") * lax.axis_size("context") + context
     first_end = seq_lengths[0, 0]
     second_end = first_end + seq_lengths[0, 1]
-    scalars = jnp.stack([context, first_end, second_end, rank]).astype(jnp.int32)
-    chunk_shapes = [1] * count if small else [expert_count]
-    starts = jnp.stack([here ^ j for j in range(count)]) if small else jnp.zeros((1,), jnp.int32)
-    starts = starts.astype(jnp.int32)
+    side = lax.axis_index("dp")
+    scalars = jnp.stack([context, first_end, second_end, rank, here, side]).astype(jnp.int32)
+    padded = (capacity + 15) // 16 * 16 + 16
+    slots = expert_count * padded
     shard = query_weight.shape[0]
     first_block = jnp.concatenate(
         [
@@ -1223,114 +1292,124 @@
     second_block = jnp.concatenate(
         [output_weight.T, router_weight, jnp.zeros((shard, 64 - expert_count), bf16)], axis=1
     )
-    first_pieces, first_offsets = gather_weights(first_block, here, small)
-    buckets = jnp.asarray(bucket_tiles())
-    bias_tiles = bias_of(bias_table, buckets)
+    tie = lax.optimization_barrier
+    half, quarter, eighth = rows // 2, rows // 4, rows // 8
+    kv_offsets = jnp.stack(
+        [(context ^ mask) * rows + part * half for mask in range(4) for part in range(2)]
+    )
+    token_offsets = jnp.stack(
+        [which * quarter + part * eighth for which in ring_ranks(rank) for part in range(2)]
+    )
     far_bias = bias_table[-1]
     order_row = (pair_order & 1) * rows + (pair_order >> 1)
-    row_place, column_place = find_places(scalars, routes.T, order_row, expert_count, capacity)
+    first_pieces, first_offsets = gather_weights(first_block, small, 0)
+    second_block = jnp.stack([second_block] + [shift(second_block, step) for step in (1, -1, 2)])
     hidden_one, queries, kv_one, kv_two, weights, gains = project(
         first_offsets, tokens_in, first_pieces
     )
     kv_pieces = square_gather(kv_one, kv_two)
-    second_pieces, second_offsets = gather_weights(second_block, here, small)
-    output_own = assemble(second_offsets, second_pieces, bf16)
-    output_parts = [output_own] + [shift(output_own, step) for step in (1, -1, 2)]
-    cotangent_chunks = exchange(
-        scatter_rows(starts, cotangent, row_place, chunk_shapes, capacity)
-    )
-    half = rows // 2
-    kv_offsets = jnp.stack(
-        [(context ^ mask) * rows + part * half for mask in range(4) for part in range(2)]
-    )
+    order_row, queries = tie((order_row, queries))
+    row_place, column_place, bias_tiles = prepare(
+        scalars, bias_table, routes.T, order_row, expert_count, capacity, padded
+    )
+    cotangent_rows = scatter_rows(cotangent, row_place, slots)
+    queries, kv_pieces, second_block, cotangent_rows = tie(
+        (queries, kv_pieces, second_block, cotangent_rows)
+    )
+    second_pieces, second_offsets = gather_weights(second_block, small, 1)
+    cotangent_rows = exchange(cotangent_rows)
     packed_one, packed_two, lse, keys_values = attention_forward(
         scalars, far_bias, kv_offsets, queries, bias_tiles, kv_pieces, group_rows, heads, width
     )
     attended = ring_gather(packed_one, packed_two)
-    residual, hidden_two, info, *row_chunks = dispatch(
-        scalars, starts, tokens_in, gains, routes, row_place, attended, output_parts, chunk_shapes,
-        heads, width, capacity, expert_count,
-    )
-    row_chunks = exchange(row_chunks)
-    rows_all, grads_all, acted_all, pre_all, *returns = expert_step(
-        expert_in, expert_out, row_chunks, cotangent_chunks
-    )
-    returns = exchange(returns)
+    residual, hidden_two, info, output_own, output_all, rows_out = dispatch(
+        scalars, second_offsets, tokens_in, gains, routes, row_place, attended, second_pieces,
+        heads, width, expert_count, padded,
+    )
+    rows_out, cotangent_rows = tie((rows_out, cotangent_rows))
+    expert_rows = exchange(rows_out)
+    acted, grad_pre, gates, back = expert_step(
+        expert_in, expert_out, expert_rows, cotangent_rows, padded
+    )
+    back = exchange(back)
+    gate_column = gates[:, 0:1]
+    outs = dot_nn(acted, expert_out[0]).astype(bf16)
+    expert_out_grad = dot_tn((acted.astype(f32) * gate_column).astype(bf16), cotangent_rows)
+    expert_in_grad = dot_tn(expert_rows, (grad_pre.astype(f32) * gate_column).astype(bf16))
+    back, outs, expert_out_grad, expert_in_grad = tie(
+        (back, outs, expert_out_grad, expert_in_grad)
+    )
     grad_logits, *ring = combine_grads(
-        scalars, starts, column_place, info, routes, output_own, returns, capacity, expert_count
-    )
-    grad_one, branch_one, branch_two, gain_two_grad = norm_back(
-        1, True, scalars, residual, gains, cotangent, ring_reduce(*ring)
-    )
+        scalars, column_place, info, routes, output_own, back, expert_count, padded
+    )
+    ring, outs = ring_reduce(*ring), exchange(outs)
+    ring, outs = tie((ring, outs))
+    grad_one, branch_one, branch_two, gain_two_grad, *grad_heads = norm_back(
+        1, True, scalars, residual, gains, cotangent, ring, output_all
+    )
+    head_pieces = (
+        grad_heads[0], shift(grad_heads[2], 1), shift(grad_heads[1], -1), shift(grad_heads[3], 2)
+    )
+    mixed = combine_outs(column_place, info, outs)
+    head_pieces, branch_one, branch_two, mixed = tie((head_pieces, branch_one, branch_two, mixed))
+    mixed = lax.all_to_all(mixed, "tensor", split_axis=0, concat_axis=0, tiled=True)
     branch_pieces = ring_gather(branch_one, branch_two)
-    eighth = rows // 8
-    token_offsets = jnp.stack(
-        [which * 2 * eighth + part * eighth for which in ring_ranks(rank) for part in range(2)]
-    )
     dq, own, *sent, fold = attention_backward(
-        scalars, far_bias, token_offsets, queries, keys_values, bias_tiles, lse,
-        (packed_one, packed_two), output_own, branch_pieces, heads, width,
-    )
-    dkv, *ring = hidden_grad(scalars, dq, weights, own, *square_reduce(*sent))
-    input_full, input_one, input_two, gain_one_grad = norm_back(
-        0, False, scalars, tokens_in, gains, grad_one, ring_reduce(*ring)
-    )
-    input_grad = assemble(token_offsets, ring_gather(input_one, input_two), f32)
-    out_chunks = exchange(expert_outputs(acted_all, expert_out, chunk_shapes))
-    ring = combine_outs(scalars, starts, column_place, info, out_chunks, capacity)
-    layer_one, layer_two = finish(residual, ring_reduce(*ring))
-    layer_out = assemble(token_offsets, ring_gather(layer_one, layer_two), bf16)
-    gate_rows = jnp.concatenate([chunk[:, 0:16, 0:capacity] for chunk in row_chunks], axis=0)
-    gates = jnp.sum(gate_rows.astype(f32), axis=1).reshape(-1, 1)
-    total_rows = gates.shape[0]
-    acted_flat = acted_all.reshape(total_rows, -1)
-    pre_flat = pre_all.reshape(total_rows, -1)
-    expert_out_grad = dot_tn(
-        (acted_flat.astype(f32) * gates).astype(bf16), grads_all.reshape(total_rows, -1)
-    )[None]
-    expert_in_grad = dot_tn(
-        rows_all.reshape(total_rows, -1), (pre_flat.astype(f32) * gates).astype(bf16)
-    )[None]
-    grad_branch = assemble(token_offsets, branch_pieces, bf16)
-    quarter = rows // 4
-    attended_own = jnp.concatenate(
-        [
-            jnp.concatenate([packed_one[:, :192], packed_two[:, :192]], axis=0),
-            jnp.concatenate(
-                [
-                    jnp.concatenate([packed_one[:, 256:], packed_one[:, 192:256]], axis=1),
-                    jnp.concatenate([packed_two[:, 256:], packed_two[:, 192:256]], axis=1),
-                ],
-                axis=0,
-            ),
-        ],
-        axis=0,
-    )
-    output_grad = scatter_weights(dot_tn(grad_branch, attended_own), small).T
-    projected = jnp.concatenate([dot_tn(hidden_one, dq), dot_tn(hidden_one, dkv)], axis=1)
-    projected = scatter_weights(projected, small)
-    router_grad = dot_tn(hidden_two, grad_logits)[:, 64 : 64 + expert_count]
-    vectors = jnp.concatenate([router_grad, gain_two_grad[0][:, None]], axis=1)
-    vectors = lax.psum(vectors, ("dp", "context", "tensor"))
-    vectors = lax.dynamic_slice_in_dim(vectors, here * shard, shard, 0)
-    gain_one_grad = lax.psum(gain_one_grad[0], ("dp", "context", "tensor"))
-    gain_one_grad = lax.dynamic_slice_in_dim(gain_one_grad, here * shard, shard, 0)
+        scalars, far_bias, token_offsets[::2], queries, keys_values, bias_tiles, lse,
+        (packed_one, packed_two), head_pieces, heads, width,
+    )
+    mixed, sent, branch_pieces = tie((mixed, sent, branch_pieces))
+    from_square = square_reduce(*sent)
+    layer_out = lax.all_to_all(
+        finish(residual, mixed), "tensor", split_axis=0, concat_axis=0, tiled=True
+    )
+    outer_parts = output_grads(
+        scalars, token_offsets, hidden_two, grad_logits, (packed_one, packed_two), branch_pieces,
+        width, small,
+    )
+    dq, from_square, layer_out, outer_parts = tie((dq, from_square, layer_out, outer_parts))
+    dkv, *ring = hidden_grad(scalars, dq, weights, own, *from_square)
+    ring = ring_reduce(*ring)
+    input_full, input_one, input_two, _ = norm_back(
+        0, False, scalars, tokens_in, gains, grad_one, ring
+    )
+    input_pieces = ring_gather(input_one, input_two)
+    input_grad = assemble(token_offsets, input_pieces, f32)
+    dkv, input_one = tie((dkv, input_one))
+    expert_out_grad, expert_in_grad = expert_out_grad[None], expert_in_grad[None]
+    outer_grads = scatter_weights(scalars, outer_parts)
+    output_grad = outer_grads[:, :192].T
+    router_grad = doubled(outer_grads[:, 192 : 192 + expert_count], "tensor", (1, 2))
+    projected = scatter_weights(
+        scalars, projection_grads(scalars, hidden_one, dq, dkv, gain_two_grad, small)
+    )
+    query_grad, key_grad = projected[:, :192], projected[:, 256:448]
+    value_grad = jnp.concatenate([projected[:, 512:], projected[:, 448:512]], axis=1)
+    gain_one_grad = jnp.sum(
+        query_weight.astype(f32) * query_grad
+        + key_weight.astype(f32) * key_grad
+        + value_weight.astype(f32) * value_grad,
+        axis=1,
+        keepdims=True,
+    )
+    gain_grads = doubled(
+        jnp.concatenate([gain_one_grad, projected[:, 192:193]], axis=1), "tensor", (1, 2)
+    )
     bucket_row = jnp.asarray(bucket_tiles()[0, 0])
     bucket_hot = (bucket_row[None, :] == jnp.arange(bias_table.shape[0] - 1)[:, None]).astype(f32)
-    near_grad = jnp.sum(bucket_hot[:, None, :] * fold[None, :heads, :], axis=-1)
+    near_grad = jnp.sum(bucket_hot[:, None, :] * sum_rows(fold, small)[None, :heads, :], axis=-1)
     table_grad = jnp.concatenate([near_grad, -jnp.sum(near_grad, axis=0, keepdims=True)], axis=0)
-    table_grad = lax.psum(table_grad, ALL_ROWS)
     return (
         layer_out,
         input_grad,
-        projected[:, :192],
-        projected[:, 256:448],
-        jnp.concatenate([projected[:, 512:], projected[:, 448:512]], axis=1),
+        query_grad,
+        key_grad,
+        value_grad,
         output_grad,
         table_grad,
-        gain_one_grad,
-        vectors[:, :expert_count],
-        vectors[:, expert_count],
+        gain_grads[:, 0] / attention_gain.astype(f32),
+        router_grad,
+        gain_grads[:, 1],
         expert_in_grad,
         expert_out_grad,
     )

time: 730 us -> 571 us (0.78); the launches traced: 716 us -> 566 us
  waiting for transfers between devices: 190 us -> 109 us
  local copies, waits for them, and re-layouts: 91.5 us -> 58.7 us
  other arithmetic: 28 us -> 8.68 us
  blocking collectives: 62.5 us -> 49.6 us
  starting transfers between devices: 194 us -> 183 us
    ppermute x44 -> x17, waiting for transfers between devices: 119 us -> 11.1 us  [the longest x7 11.1 us: doubled(): lax.ppermute(value, axis, [(i, i ^ mask) for i in range(size)])]
    psum x2 -> x0, blocking collectives: 62.5 us -> none  [the longest x1 43.4 us: on_device(): gain_one_grad = lax.psum(gain_one_grad[0], ('dp', 'context', 'tensor'))]
    all_to_all x0 -> x1, blocking collectives: none -> 49.6 us  [exchange(): lax.all_to_all(rows_out, ALL_ROWS, split_axis=0, concat_axis=0, tiled=True)]
    ppermute x44 -> x17, starting transfers between devices: 58.2 us -> 20.6 us  [the longest x7 11.2 us: doubled(): lax.ppermute(value, axis, [(i, i ^ mask) for i in range(size)])]
    all_to_all x0 -> x5, waiting for transfers between devices: none -> 29 us  [the longest x3 23.7 us: exchange(): lax.all_to_all(rows_out, ALL_ROWS, split_axis=0, concat_axis=0, tiled=True)]
    all_to_all x0 -> x5, starting transfers between devices: none -> 24.5 us  [the longest x3 14.1 us: exchange(): lax.all_to_all(rows_out, ALL_ROWS, split_axis=0, concat_axis=0, tiled=True)]
    unnamed x354 -> x193, local copies, waits for them, and re-layouts: 66.9 us -> 49.3 us
    ppermute x45 -> x36, waiting for transfers between devices: 71.7 us -> 55.6 us  [shift(): lax.ppermute(value, 'tensor', [(i, (i + amount) % size) for i in range(si...]
  transfers between devices with their start and end apart: 107 -> 82, of which waited for: 27 -> 29; matrix products, arithmetic and copies ran while one was open for 14% -> 7% of each run, Pallas kernels for 12% -> 19%
where the time goes in v1:
time: 571 us; the launch traced here: 566 us
  starting transfers between devices  183 us (32%)
  Pallas kernels  134 us (23%)
  waiting for transfers between devices  109 us (19%)
  local copies, waits for them, and re-layouts  58.7 us (10%)
  blocking collectives  49.6 us (9%)
  matrix products  19.5 us (3%)
  other arithmetic  8.68 us (2%)
    ppermute x36, starting transfers between devices, shift(): lax.ppermute(value, 'tensor', [(i, (i + amount) % size) for i in range(si...  71.6 us
    ppermute x24, starting transfers between devices, cross(): return lax.ppermute(value, 'context', [(i, i ^ mask) for i in range(size)])  65.8 us
    ppermute x36, waiting for transfers between devices, shift(): lax.ppermute(value, 'tensor', [(i, (i + amount) % size) for i in range(si...  55.6 us
    all_to_all x1, blocking collectives, exchange(): lax.all_to_all(rows_out, ALL_ROWS, split_axis=0, concat_axis=0, tiled=True)  49.6 us
    unnamed x193, local copies, waits for them, and re-layouts  49.3 us
    all_to_all x3, waiting for transfers between devices, exchange(): lax.all_to_all(rows_out, ALL_ROWS, split_axis=0, concat_axis=0, tiled=True)  23.7 us
    pallas_call x1, Pallas kernels, attention_backward(): pl.pallas_call(functools.partial(attention_backward_kernel, heads, width,...  20.7 us
    pallas_call x1, Pallas kernels, expert_step(): pl.pallas_call(functools.partial(expert_kernel, padded), out_shape=(shape...  20.3 us
  transfers between devices with their start and end apart: 82, of which 29 were waited for; matrix products, arithmetic and copies ran while one was open for 7% of the time, Pallas kernels for 19%

profile of v1, /device:TPU:0, one launch (start us, length us, event | category | flops | bytes accessed | tf_op | source)
XLA Modules:
  0.0 565.7 jit_solution(7279423613299131333)
XLA Ops:
  34.5 5.0 collective-permute-done.7.rest_2_
  41.7 12.4 %prepare.1 = (s32[8,1024]{1,0:T(8,128)S(1)}, s32[1024,128]{1,0:T(8,128)S(1)}, f32[3,3,256,256]{3,2,1,0:T(8,128)S(1)}) custom-call(s32[6]{0:T(128)S(1)} %stack.128.scalars.scal, f32[32,3]{1,0:T(8,128)S(1)} %copy.65.table, s32[2,1024]{1,0:T(2,128)S(1)} %bitcast.70, s32[1,2048]{1,0:T(1,128)S(1)} %shift-right-arithmetic_add_fusion.order_ref), custom_call_target="tpu_custom_call" | custom-call | flops 10000000000 | bytes 3145728 | tf_op jit(solution)/shard_map/prepare/pallas_call | solution.py:516
  56.4 7.5 %scatter_rows.1 = bf16[2432,768]{1,0:T(8,128)(2,1)S(1)} custom-call(bf16[1024,768]{1,0:T(8,128)(2,1)S(1)} %copy-done.5, s32[8,1024]{1,0:T(8,128)S(1)} %get-tuple-element.143.row_place), custom_call_target="tpu_custom_call" | custom-call | flops 3825205248 | bytes 6291456 | tf_op jit(solution)/shard_map/scatter_rows/pallas_call | solution.py:760
  68.1 4.5 all-to-all-start
  73.9 11.6 %attention_forward.1 = (bf16[256,384]{1,0:T(8,128)(2,1)}, bf16[256,384]{1,0:T(8,128)(2,1)}, f32[8,1024]{1,0:T(8,128)}, bf16[4096,384]{1,0:T(8,128)(2,1)}) custom-call(s32[6]{0:T(128)} %copy-done.45, f32[3]{0:T(128)} %slice_reduce_fusion.1.far_bias, s32[8]{0:T(128)} %stack.160.offsets, bf16[1024,256]{1,0:T(8,128)(2,1)} %copy-done.60, ...), custom_call_target="tpu_custom_call" | custom-call | flops 12884901888 | bytes 10485760 | tf_op jit(solution)/shard_map/attention_forward/pallas_call | solution.py:161
  93.2 11.2 %collective-permute-start.22 = (bf16[4,96,256]{2,1,0:T(8,128)(2,1)S(1)}, bf16[4,96,256]{2,1,0:T(8,128)(2,1)S(1)}, u32[]{:S(2)}, u32[]{:S(2)}) collective-permute-start(bf16[4,96,256]{2,1,0:T(8,128)(2,1)S(1)} %pad_maximum_fusion.rest_8_), channel_id=1, source_target_pairs={{0,4},{4,0},{8,12},{12,8},{1,5},{5,1},{9,13},{13,9},{2,6},{6,2},{1... | collective-permute-start | bytes 589832 | tf_op jit(solution)/shard_map/ppermute | solution.py:1169
  104.4 12.4 %collective-permute-start.23 = (bf16[4,96,256]{2,1,0:T(8,128)(2,1)S(1)}, bf16[4,96,256]{2,1,0:T(8,128)(2,1)S(1)}, u32[]{:S(2)}, u32[]{:S(2)}) collective-permute-start(bf16[4,96,256]{2,1,0:T(8,128)(2,1)S(1)} %pad_maximum_fusion.rest_8_), channel_id=1, source_target_pairs={{0,8},{4,12},{8,0},{12,4},{1,9},{5,13},{9,1},{13,5},{2,10},{6,14},... | collective-permute-start | bytes 589832 | tf_op jit(solution)/shard_map/ppermute | solution.py:1169
  118.0 8.0 %collective-permute-start.25 = (bf16[4,96,256]{2,1,0:T(8,128)(2,1)S(1)}, bf16[4,96,256]{2,1,0:T(8,128)(2,1)S(1)}, u32[]{:S(2)}, u32[]{:S(2)}) collective-permute-start(bf16[4,96,256]{2,1,0:T(8,128)(2,1)S(1)} %pad_maximum_fusion.rest_8_), channel_id=1, source_target_pairs={{0,16},{16,0},{1,17},{17,1},{2,18},{18,2},{3,19},{19,3},{4,20},{20... | collective-permute-start | bytes 589832 | tf_op jit(solution)/shard_map/ppermute | solution.py:1245
  127.0 13.3 %collective-permute-start.21 = (bf16[256,384]{1,0:T(8,128)(2,1)S(1)}, bf16[256,384]{1,0:T(8,128)(2,1)}, u32[]{:S(2)}, u32[]{:S(2)}) collective-permute-start(bf16[256,384]{1,0:T(8,128)(2,1)S(1)} %collective-permute-done.19.rest_5_), channel_id=1, source_target_pairs={{0,3},{1,0},{2,1},{3,2},{4,7},{5,4},{6,5},{7,6},{8,11},{9,8},{10,9... | collective-permute-start | bytes 589832 | tf_op jit(solution)/shard_map/ppermute | solution.py:1164
  145.1 18.1 %dispatch.1 = (f32[256,768]{1,0:T(8,128)}, bf16[1024,768]{1,0:T(8,128)(2,1)}, f32[1024,128]{1,0:T(8,128)}, bf16[768,256]{1,0:T(8,128)(2,1)}, bf16[4,768,256]{2,1,0:T(8,128)(2,1)}, /*index=5*/bf16[2432,768]{1,0:T(8,128)(2,1)}) custom-call(s32[6]{0:T(128)} %copy-done.45, s32[8]{0:T(128)} %copy-done.49, bf16[1024,768]{1,0:T(8,128)(2,1)} %value_ref.3, ...), custom_call_target="tpu_custom_call" | custom-call | flops 5435817984 | bytes 16777216 | tf_op jit(solution)/shard_map/dispatch/pallas_call | solution.py:719
  163.2 49.6 %all_to_all.71 = bf16[8,304,768]{2,1,0:T(8,128)(2,1)} all-to-all(bf16[8,304,768]{2,1,0:T(8,128)(2,1)} %bitcast.72), channel_id=1, replica_groups=mesh['dp'=2,'context'=4,'tensor'=4] {'dp','context'}, dimensions={0} | all-to-all | bytes 7471104 | tf_op jit(solution)/shard_map/all_to_all | solution.py:1235
  212.8 20.3 %expert_step.1 = (bf16[2432,768]{1,0:T(8,128)(2,1)}, bf16[2432,768]{1,0:T(8,128)(2,1)}, f32[2432,128]{1,0:T(8,128)}, bf16[2432,768]{1,0:T(8,128)(2,1)}) custom-call(bf16[1,768,768]{2,1,0:T(8,128)(2,1)} %in_ref.1, bf16[1,768,768]{2,1,0:T(8,128)(2,1)} %out_ref.1, bf16[2432,768]{1,0:T(8,128)(2,1)} %bitcast.73, bf16[2432,768]{1,0:T(8,128)(2,1)} %bitcast.39.grads_ref), custom_call_target="tpu_custom_call" | custom-call | flops 8606711808 | bytes 25165824 | tf_op jit(solution)/shard_map/expert_step/pallas_call | solution.py:811
  233.1 4.7 all-to-all-start.2
  238.2 7.5 %convolution_convert_fusion = bf16[2432,768]{1,0:T(8,128)(2,1)} fusion(bf16[2432,768]{1,0:T(8,128)(2,1)} %get-tuple-element.169, bf16[1,768,768]{2,1,0:T(8,128)(2,1)} %out_ref.1), kind=kOutput, calls=%fused_computation.2 | convolution fusion | flops 2870771712 | bytes 8650752 | tf_op jit(solution)/shard_map/dot_general | solution.py:20
  245.7 7.1 %fusion = f32[768,768]{1,0:T(8,128)} fusion(bf16[2432,768]{1,0:T(8,128)(2,1)} %bitcast.39.grads_ref, bf16[2432,768]{1,0:T(8,128)(2,1)S(1)} %copy-done.91, f32[2432]{0:T(1024)S(1)} %slice_reduce_fusion), kind=kOutput, calls=%fused_computation.3 | convolution fusion | flops 2874507264 | bytes 9840128 | tf_op jit(solution)/shard_map/dot_general | solution.py:28
  252.9 4.9 fusion.1
  257.8 23.7 %all-to-all-done.2 = bf16[8,304,768]{2,1,0:T(8,128)(2,1)} async-done(((bf16[8,304,768]{2,1,0:T(8,128)(2,1)}), bf16[8,304,768]{2,1,0:T(8,128)(2,1)}, u32[]{:S(2)}, u32[]{:S(2)}) %all-to-all-start.2) | async-done | bytes 3735584 | tf_op jit(solution)/shard_map/all_to_all | solution.py:1235
  281.4 4.9 all-to-all-start.3
  286.4 16.9 %combine_grads.1 = (bf16[1024,128]{1,0:T(8,128)(2,1)}, f32[256,768]{1,0:T(8,128)}, bf16[128,768]{1,0:T(8,128)(2,1)}, bf16[128,768]{1,0:T(8,128)(2,1)}, bf16[128,...) custom-call(s32[6]{0:T(128)} %copy-done.45, ...), custom_call_target="tpu_custom_call" | custom-call | flops 3825205248 | bytes 8388608 | tf_op jit(solution)/shard_map/combine_grads/pallas_call | solution.py:910
  313.9 4.2 collective-permute-start.34
  329.7 4.5 collective-permute-done.30.rest_1_
  345.0 9.3 %combine_outs.1 = bf16[1024,768]{1,0:T(8,128)(2,1)} custom-call(s32[1024,128]{1,0:T(8,128)} %copy-done.61, f32[1024,128]{1,0:T(8,128)} %get-tuple-element.162.info_ref, bf16[2432,768]{1,0:T(8,128)(2,1)} %bitcast.46.rows_ref), custom_call_target="tpu_custom_call" | custom-call | flops 3825205248 | bytes 8388608 | tf_op jit(solution)/shard_map/combine_outs/pallas_call | solution.py:937
  371.8 20.7 %attention_backward.1 = (bf16[1024,256]{1,0:T(8,128)(2,1)}, bf16[1024,384]{1,0:T(8,128)(2,1)}, bf16[512,384]{1,0:T(8,128)(2,1)}, bf16[512,384]{1,0:T(8,128)(2,1)...) custom-call(s32[6]{0:T(128)} %copy-done.45, ...), custom_call_target="tpu_custom_call" | custom-call | flops 32212254720 | bytes 16777216 | tf_op jit(solution)/shard_map/attention_backward/pallas_call | solution.py:375
  392.5 15.3 %collective-permute-done.42.rest_6_ = bf16[128,768]{1,0:T(8,128)(2,1)S(1)} collective-permute-done((bf16[128,768]{1,0:T(8,128)(2,1)S(1)}, bf16[128,768]{1,0:T(8,128)(2,1)S(1)}, u32[]{:S(2)}, u32[]{:S(2)}) %collective-permute-start.42) | collective-permute-done | bytes 196640 | tf_op jit(solution)/shard_map/ppermute | solution.py:1164
  409.1 5.3 all-to-all-done.4
  415.8 6.9 %all-to-all-start.5 = ((bf16[4,256,768]{2,1,0:T(8,128)(2,1)}), bf16[4,256,768]{2,1,0:T(8,128)(2,1)}, u32[]{:S(2)}, u32[]{:S(2)}) async-start(bf16[4,256,768]{2,1,0:T(8,128)(2,1)} %bitcast.49), calls=%async_computation.5 | async-start | bytes 3145728 | tf_op jit(solution)/shard_map/all_to_all | solution.py:1363
  424.1 8.7 %collective-permute-start.45 = (bf16[512,384]{1,0:T(8,128)(2,1)}, bf16[512,384]{1,0:T(8,128)(2,1)S(1)}, u32[]{:S(2)}, u32[]{:S(2)}) collective-permute-start(bf16[512,384]{1,0:T(8,128)(2,1)} %get-tuple-element.210), channel_id=1, source_target_pairs={{0,8},{4,12},{8,0},{12,4},{1,9},{5,13},{9,1},{13,5},{2,10},{6,14},... | collective-permute-start | bytes 1179656 | tf_op jit(solution)/shard_map/ppermute | solution.py:1169
  434.1 10.1 %collective-permute-start.48 = (bf16[512,384]{1,0:T(8,128)(2,1)S(1)}, bf16[512,384]{1,0:T(8,128)(2,1)S(1)}, u32[]{:S(2)}, u32[]{:S(2)}) collective-permute-start(bf16[512,384]{1,0:T(8,128)(2,1)S(1)} %add_convert_fusion), channel_id=1, source_target_pairs={{0,8},{4,12},{8,0},{12,4},{1,9},{5,13},{9,1},{13,5},{2,10},{6,14},... | collective-permute-start | bytes 1179656 | tf_op jit(solution)/shard_map/ppermute | solution.py:1169
  478.6 6.1 %collective-permute-done.54 = bf16[128,768]{1,0:T(8,128)(2,1)S(1)} collective-permute-done((bf16[128,768]{1,0:T(8,128)(2,1)S(1)}, bf16[128,768]{1,0:T(8,128)(2,1)S(1)}, u32[]{:S(2)}, u32[]{:S(2)}) %collective-permute-start.54) | collective-permute-done | bytes 196640 | tf_op jit(solution)/shard_map/ppermute | solution.py:1164
  509.7 4.6 collective-permute-start.72
  534.1 4.5 collective-permute-done.64
  542.7 4.7 collective-permute-done.75
  (397 shorter events, 214.2 us)
Async XLA Ops:
  11.1 21.2 %collective-permute-start.13 = (bf16[96,256]{1,0:T(8,128)(2,1)S(1)}, bf16[96,256]{1,0:T(8,128)(2,1)S(1)}, u32[]{:S(2)}, u32[]{:S(2)}) collective-permute-start(bf16[96,256]{1,0:T(8,128)(2,1)S(1)} %maximum_maximum_fusion), channel_id=1, source_target_pairs={{0,1},{1,2},{2,3},{3,0},{4,5},{5,6},{6,7},{7,4},{8,9},{9,10},{10,1... | collective-permute-start | bytes 147464 | tf_op jit(solution)/shard_map/ppermute | solution.py:1164
  32.3 33.5 %collective-permute-start.8 = (bf16[512,384]{1,0:T(8,128)(2,1)S(1)}, bf16[512,384]{1,0:T(8,128)(2,1)S(1)}, u32[]{:S(2)}, u32[]{:S(2)}) collective-permute-start(bf16[512,384]{1,0:T(8,128)(2,1)S(1)} %get-tuple-element.147.rest_1_), channel_id=1, source_target_pairs={{0,4},{4,0},{8,12},{12,8},{1,5},{5,1},{9,13},{13,9},{2,6},{6,2},{1... | collective-permute-start | bytes 1179656 | tf_op jit(solution)/shard_map/ppermute | solution.py:1169
  33.8 31.9 %collective-permute-start.9 = (bf16[512,384]{1,0:T(8,128)(2,1)S(1)}, bf16[512,384]{1,0:T(8,128)(2,1)S(1)}, u32[]{:S(2)}, u32[]{:S(2)}) collective-permute-start(bf16[512,384]{1,0:T(8,128)(2,1)S(1)} %get-tuple-element.146.rest_0_), channel_id=1, source_target_pairs={{0,8},{4,12},{8,0},{12,4},{1,9},{5,13},{9,1},{13,5},{2,10},{6,14},... | collective-permute-start | bytes 1179656 | tf_op jit(solution)/shard_map/ppermute | solution.py:1169
  39.5 26.3 %collective-permute-start.11 = (bf16[512,384]{1,0:T(8,128)(2,1)S(1)}, bf16[512,384]{1,0:T(8,128)(2,1)S(1)}, u32[]{:S(2)}, u32[]{:S(2)}) collective-permute-start(bf16[512,384]{1,0:T(8,128)(2,1)S(1)} %collective-permute-done.7.rest_2_), channel_id=1, source_target_pairs={{0,8},{4,12},{8,0},{12,4},{1,9},{5,13},{9,1},{13,5},{2,10},{6,14},... | collective-permute-start | bytes 1179656 | tf_op jit(solution)/shard_map/ppermute | solution.py:1169
  40.9 25.6 %collective-permute-start.12 = (bf16[512,384]{1,0:T(8,128)(2,1)}, bf16[512,384]{1,0:T(8,128)(2,1)S(1)}, u32[]{:S(2)}, u32[]{:S(2)}) collective-permute-start(bf16[512,384]{1,0:T(8,128)(2,1)} %collective-permute-done.10.rest_5_), channel_id=1, source_target_pairs={{0,4},{4,0},{8,12},{12,8},{1,5},{5,1},{9,13},{13,9},{2,6},{6,2},{1... | collective-permute-start | bytes 1179656 | tf_op jit(solution)/shard_map/ppermute | solution.py:1169
  68.1 95.1 %all-to-all-start = ((bf16[8,304,768]{2,1,0:T(8,128)(2,1)}), bf16[8,304,768]{2,1,0:T(8,128)(2,1)}, u32[]{:S(2)}, u32[]{:S(2)}) async-start(bf16[8,304,768]{2,1,0:T(8,128)(2,1)} %bitcast.69), calls=%async_computation | async-start | bytes 7471104 | tf_op jit(solution)/shard_map/all_to_all | solution.py:1235
  85.5 18.9 %collective-permute-start.16 = (bf16[256,384]{1,0:T(8,128)(2,1)}, bf16[256,384]{1,0:T(8,128)(2,1)S(1)}, u32[]{:S(2)}, u32[]{:S(2)}) collective-permute-start(bf16[256,384]{1,0:T(8,128)(2,1)} %get-tuple-element.156.rest_0_.packed_one), channel_id=1, source_target_pairs={{0,1},{1,2},{2,3},{3,0},{4,5},{5,6},{6,7},{7,4},{8,9},{9,10},{10,1... | collective-permute-start | bytes 589832 | tf_op jit(solution)/shard_map/ppermute | solution.py:1164
  86.6 30.3 %collective-permute-start.19 = (bf16[256,384]{1,0:T(8,128)(2,1)}, bf16[256,384]{1,0:T(8,128)(2,1)S(1)}, u32[]{:S(2)}, u32[]{:S(2)}) collective-permute-start(bf16[256,384]{1,0:T(8,128)(2,1)} %get-tuple-element.157.rest_1_.packed_two), channel_id=1, source_target_pairs={{0,3},{1,0},{2,1},{3,2},{4,7},{5,4},{6,5},{7,6},{8,11},{9,8},{10,9... | collective-permute-start | bytes 589832 | tf_op jit(solution)/shard_map/ppermute | solution.py:1164
  89.4 28.7 %collective-permute-start.17 = (bf16[256,384]{1,0:T(8,128)(2,1)}, bf16[256,384]{1,0:T(8,128)(2,1)S(1)}, u32[]{:S(2)}, u32[]{:S(2)}) collective-permute-start(bf16[256,384]{1,0:T(8,128)(2,1)} %get-tuple-element.157.rest_1_.packed_two), channel_id=1, source_target_pairs={{0,1},{1,2},{2,3},{3,0},{4,5},{5,6},{6,7},{7,4},{8,9},{9,10},{10,1... | collective-permute-start | bytes 589832 | tf_op jit(solution)/shard_map/ppermute | solution.py:1164
  89.4 36.7 %collective-permute-start.18 = (bf16[256,384]{1,0:T(8,128)(2,1)}, bf16[256,384]{1,0:T(8,128)(2,1)S(1)}, u32[]{:S(2)}, u32[]{:S(2)}) collective-permute-start(bf16[256,384]{1,0:T(8,128)(2,1)} %get-tuple-element.156.rest_0_.packed_one), channel_id=1, source_target_pairs={{0,3},{1,0},{2,1},{3,2},{4,7},{5,4},{6,5},{7,6},{8,11},{9,8},{10,9... | collective-permute-start | bytes 589832 | tf_op jit(solution)/shard_map/ppermute | solution.py:1164
  93.2 33.8 %collective-permute-start.22 = (bf16[4,96,256]{2,1,0:T(8,128)(2,1)S(1)}, bf16[4,96,256]{2,1,0:T(8,128)(2,1)S(1)}, u32[]{:S(2)}, u32[]{:S(2)}) collective-permute-start(bf16[4,96,256]{2,1,0:T(8,128)(2,1)S(1)} %pad_maximum_fusion.rest_8_), channel_id=1, source_target_pairs={{0,4},{4,0},{8,12},{12,8},{1,5},{5,1},{9,13},{13,9},{2,6},{6,2},{1... | collective-permute-start | bytes 589832 | tf_op jit(solution)/shard_map/ppermute | solution.py:1169
  104.4 35.9 %collective-permute-start.23 = (bf16[4,96,256]{2,1,0:T(8,128)(2,1)S(1)}, bf16[4,96,256]{2,1,0:T(8,128)(2,1)S(1)}, u32[]{:S(2)}, u32[]{:S(2)}) collective-permute-start(bf16[4,96,256]{2,1,0:T(8,128)(2,1)S(1)} %pad_maximum_fusion.rest_8_), channel_id=1, source_target_pairs={{0,8},{4,12},{8,0},{12,4},{1,9},{5,13},{9,1},{13,5},{2,10},{6,14},... | collective-permute-start | bytes 589832 | tf_op jit(solution)/shard_map/ppermute | solution.py:1169
  116.8 23.5 %collective-permute-start.24 = (bf16[4,96,256]{2,1,0:T(8,128)(2,1)S(1)}, bf16[4,96,256]{2,1,0:T(8,128)(2,1)S(1)}, u32[]{:S(2)}, u32[]{:S(2)}) collective-permute-start(bf16[4,96,256]{2,1,0:T(8,128)(2,1)S(1)} %pad_maximum_fusion.rest_8_), channel_id=1, source_target_pairs={{0,12},{4,8},{8,4},{12,0},{1,13},{5,9},{9,5},{13,1},{2,14},{6,10},... | collective-permute-start | bytes 589832 | tf_op jit(solution)/shard_map/ppermute | solution.py:1169
  118.0 22.8 %collective-permute-start.25 = (bf16[4,96,256]{2,1,0:T(8,128)(2,1)S(1)}, bf16[4,96,256]{2,1,0:T(8,128)(2,1)S(1)}, u32[]{:S(2)}, u32[]{:S(2)}) collective-permute-start(bf16[4,96,256]{2,1,0:T(8,128)(2,1)S(1)} %pad_maximum_fusion.rest_8_), channel_id=1, source_target_pairs={{0,16},{16,0},{1,17},{17,1},{2,18},{18,2},{3,19},{19,3},{4,20},{20... | collective-permute-start | bytes 589832 | tf_op jit(solution)/shard_map/ppermute | solution.py:1245
  233.1 48.4 %all-to-all-start.2 = ((bf16[8,304,768]{2,1,0:T(8,128)(2,1)}), bf16[8,304,768]{2,1,0:T(8,128)(2,1)}, u32[]{:S(2)}, u32[]{:S(2)}) async-start(bf16[8,304,768]{2,1,0:T(8,128)(2,1)} %bitcast.75), calls=%async_computation.2 | async-start | bytes 7471104 | tf_op jit(solution)/shard_map/all_to_all | solution.py:1235
  281.4 52.8 %all-to-all-start.3 = ((bf16[8,304,768]{2,1,0:T(8,128)(2,1)}), bf16[8,304,768]{2,1,0:T(8,128)(2,1)}, u32[]{:S(2)}, u32[]{:S(2)}) async-start(bf16[8,304,768]{2,1,0:T(8,128)(2,1)} %bitcast.71), calls=%async_computation.3 | async-start | bytes 7471104 | tf_op jit(solution)/shard_map/all_to_all | solution.py:1235
  307.4 18.3 %collective-permute-start.32 = (bf16[128,768]{1,0:T(8,128)(2,1)}, bf16[128,768]{1,0:T(8,128)(2,1)S(1)}, u32[]{:S(2)}, u32[]{:S(2)}) collective-permute-start(bf16[128,768]{1,0:T(8,128)(2,1)} %get-tuple-element.177), channel_id=1, source_target_pairs={{0,3},{1,0},{2,1},{3,2},{4,7},{5,4},{6,5},{7,6},{8,11},{9,8},{10,9... | collective-permute-start | bytes 589832 | tf_op jit(solution)/shard_map/ppermute | solution.py:1164
  360.5 32.0 %collective-permute-start.39 = (bf16[128,768]{1,0:T(8,128)(2,1)S(1)}, bf16[128,768]{1,0:T(8,128)(2,1)S(1)}, u32[]{:S(2)}, u32[]{:S(2)}) collective-permute-start(bf16[128,768]{1,0:T(8,128)(2,1)S(1)} %get-tuple-element.218.rest_1_), channel_id=1, source_target_pairs={{0,1},{1,2},{2,3},{3,0},{4,5},{5,6},{6,7},{7,4},{8,9},{9,10},{10,1... | collective-permute-start | bytes 589832 | tf_op jit(solution)/shard_map/ppermute | solution.py:1164
  360.5 32.0 %collective-permute-start.40 = (bf16[128,768]{1,0:T(8,128)(2,1)S(1)}, bf16[128,768]{1,0:T(8,128)(2,1)S(1)}, u32[]{:S(2)}, u32[]{:S(2)}) collective-permute-start(bf16[128,768]{1,0:T(8,128)(2,1)S(1)} %get-tuple-element.217.rest_0_), channel_id=1, source_target_pairs={{0,3},{1,0},{2,1},{3,2},{4,7},{5,4},{6,5},{7,6},{8,11},{9,8},{10,9... | collective-permute-start | bytes 589832 | tf_op jit(solution)/shard_map/ppermute | solution.py:1164
  364.3 50.1 %all-to-all-start.4 = ((bf16[4,256,768]{2,1,0:T(8,128)(2,1)}), bf16[4,256,768]{2,1,0:T(8,128)(2,1)S(1)}, u32[]{:S(2)}, u32[]{:S(2)}) async-start(bf16[4,256,768]{2,1,0:T(8,128)(2,1)} %bitcast.76), calls=%async_computation.4 | async-start | bytes 3145728 | tf_op jit(solution)/shard_map/all_to_all | solution.py:1355
  367.9 39.9 %collective-permute-start.42 = (bf16[128,768]{1,0:T(8,128)(2,1)S(1)}, bf16[128,768]{1,0:T(8,128)(2,1)S(1)}, u32[]{:S(2)}, u32[]{:S(2)}) collective-permute-start(bf16[128,768]{1,0:T(8,128)(2,1)S(1)} %collective-permute-done.38.rest_2_), channel_id=1, source_target_pairs={{0,1},{1,2},{2,3},{3,0},{4,5},{5,6},{6,7},{7,4},{8,9},{9,10},{10,1... | collective-permute-start | bytes 589832 | tf_op jit(solution)/shard_map/ppermute | solution.py:1164
  370.7 37.7 %collective-permute-start.43 = (bf16[128,768]{1,0:T(8,128)(2,1)S(1)}, bf16[128,768]{1,0:T(8,128)(2,1)S(1)}, u32[]{:S(2)}, u32[]{:S(2)}) collective-permute-start(bf16[128,768]{1,0:T(8,128)(2,1)S(1)} %collective-permute-done.41.rest_5_), channel_id=1, source_target_pairs={{0,3},{1,0},{2,1},{3,2},{4,7},{5,4},{6,5},{7,6},{8,11},{9,8},{10,9... | collective-permute-start | bytes 589832 | tf_op jit(solution)/shard_map/ppermute | solution.py:1164
  415.8 46.6 %all-to-all-start.5 = ((bf16[4,256,768]{2,1,0:T(8,128)(2,1)}), bf16[4,256,768]{2,1,0:T(8,128)(2,1)}, u32[]{:S(2)}, u32[]{:S(2)}) async-start(bf16[4,256,768]{2,1,0:T(8,128)(2,1)} %bitcast.49), calls=%async_computation.5 | async-start | bytes 3145728 | tf_op jit(solution)/shard_map/all_to_all | solution.py:1363
  424.1 20.1 %collective-permute-start.45 = (bf16[512,384]{1,0:T(8,128)(2,1)}, bf16[512,384]{1,0:T(8,128)(2,1)S(1)}, u32[]{:S(2)}, u32[]{:S(2)}) collective-permute-start(bf16[512,384]{1,0:T(8,128)(2,1)} %get-tuple-element.210), channel_id=1, source_target_pairs={{0,8},{4,12},{8,0},{12,4},{1,9},{5,13},{9,1},{13,5},{2,10},{6,14},... | collective-permute-start | bytes 1179656 | tf_op jit(solution)/shard_map/ppermute | solution.py:1169
  432.9 27.2 %collective-permute-start.44 = (bf16[512,384]{1,0:T(8,128)(2,1)}, bf16[512,384]{1,0:T(8,128)(2,1)S(1)}, u32[]{:S(2)}, u32[]{:S(2)}) collective-permute-start(bf16[512,384]{1,0:T(8,128)(2,1)} %get-tuple-element.208), channel_id=1, source_target_pairs={{0,4},{4,0},{8,12},{12,8},{1,5},{5,1},{9,13},{13,9},{2,6},{6,2},{1... | collective-permute-start | bytes 1179656 | tf_op jit(solution)/shard_map/ppermute | solution.py:1169
  433.0 27.1 %collective-permute-start.49 = (bf16[512,384]{1,0:T(8,128)(2,1)}, bf16[512,384]{1,0:T(8,128)(2,1)S(1)}, u32[]{:S(2)}, u32[]{:S(2)}) collective-permute-start(bf16[512,384]{1,0:T(8,128)(2,1)} %get-tuple-element.213), channel_id=1, source_target_pairs={{0,8},{4,12},{8,0},{12,4},{1,9},{5,13},{9,1},{13,5},{2,10},{6,14},... | collective-permute-start | bytes 1179656 | tf_op jit(solution)/shard_map/ppermute | solution.py:1169
  434.1 26.7 %collective-permute-start.48 = (bf16[512,384]{1,0:T(8,128)(2,1)S(1)}, bf16[512,384]{1,0:T(8,128)(2,1)S(1)}, u32[]{:S(2)}, u32[]{:S(2)}) collective-permute-start(bf16[512,384]{1,0:T(8,128)(2,1)S(1)} %add_convert_fusion), channel_id=1, source_target_pairs={{0,8},{4,12},{8,0},{12,4},{1,9},{5,13},{9,1},{13,5},{2,10},{6,14},... | collective-permute-start | bytes 1179656 | tf_op jit(solution)/shard_map/ppermute | solution.py:1169
  503.4 19.9 %collective-permute-start.62 = (f32[384,640]{1,0:T(8,128)S(1)}, f32[384,640]{1,0:T(8,128)S(1)}, u32[]{:S(2)}, u32[]{:S(2)}) collective-permute-start(f32[384,640]{1,0:T(8,128)S(1)} %get-tuple-element.250), channel_id=1, source_target_pairs={{0,16},{16,0},{1,17},{17,1},{2,18},{18,2},{3,19},{19,3},{4,20},{20... | collective-permute-start | bytes 2949128 | tf_op jit(solution)/shard_map/ppermute | solution.py:1255
  528.2 19.8 %collective-permute-start.56 = (bf16[128,768]{1,0:T(8,128)(2,1)S(1)}, bf16[128,768]{1,0:T(8,128)(2,1)S(1)}, u32[]{:S(2)}, u32[]{:S(2)}) collective-permute-start(bf16[128,768]{1,0:T(8,128)(2,1)S(1)} %get-tuple-element.243.rest_0_), channel_id=1, source_target_pairs={{0,1},{1,2},{2,3},{3,0},{4,5},{5,6},{6,7},{7,4},{8,9},{9,10},{10,1... | collective-permute-start | bytes 589832 | tf_op jit(solution)/shard_map/ppermute | solution.py:1164
  530.1 19.5 %collective-permute-start.59 = (bf16[128,768]{1,0:T(8,128)(2,1)S(1)}, bf16[128,768]{1,0:T(8,128)(2,1)S(1)}, u32[]{:S(2)}, u32[]{:S(2)}) collective-permute-start(bf16[128,768]{1,0:T(8,128)(2,1)S(1)} %get-tuple-element.244.rest_1_), channel_id=1, source_target_pairs={{0,3},{1,0},{2,1},{3,2},{4,7},{5,4},{6,5},{7,6},{8,11},{9,8},{10,9... | collective-permute-start | bytes 589832 | tf_op jit(solution)/shard_map/ppermute | solution.py:1164
  533.8 22.8 %collective-permute-start.57 = (bf16[128,768]{1,0:T(8,128)(2,1)S(1)}, bf16[128,768]{1,0:T(8,128)(2,1)S(1)}, u32[]{:S(2)}, u32[]{:S(2)}) collective-permute-start(bf16[128,768]{1,0:T(8,128)(2,1)S(1)} %get-tuple-element.244.rest_1_), channel_id=1, source_target_pairs={{0,1},{1,2},{2,3},{3,0},{4,5},{5,6},{6,7},{7,4},{8,9},{9,10},{10,1... | collective-permute-start | bytes 589832 | tf_op jit(solution)/shard_map/ppermute | solution.py:1164
  538.7 17.9 %collective-permute-start.58 = (bf16[128,768]{1,0:T(8,128)(2,1)S(1)}, bf16[128,768]{1,0:T(8,128)(2,1)S(1)}, u32[]{:S(2)}, u32[]{:S(2)}) collective-permute-start(bf16[128,768]{1,0:T(8,128)(2,1)S(1)} %get-tuple-element.243.rest_0_), channel_id=1, source_target_pairs={{0,3},{1,0},{2,1},{3,2},{4,7},{5,4},{6,5},{7,6},{8,11},{9,8},{10,9... | collective-permute-start | bytes 589832 | tf_op jit(solution)/shard_map/ppermute | solution.py:1164
  (143 other events, 1601.6 us)

commit v2 on v1

v2 whole, which is shorter than its diff:
```python
import functools
import jax
import jax.numpy as jnp
import numpy as np
from jax import lax
from jax.experimental import pallas as pl
from jax.experimental.pallas import tpu as pltpu
from jax.sharding import PartitionSpec as P

bf16 = jnp.bfloat16
f32 = jnp.float32
epsilon = 1e-06
masked_value = -1e30
tile = 256
VMEM = pl.BlockSpec(memory_space=pltpu.VMEM)
SMEM = pl.BlockSpec(memory_space=pltpu.SMEM)


def dot_nn(a, b):
    return lax.dot_general(a, b, (((1,), (0,)), ((), ())), preferred_element_type=f32)


def dot_nt(a, b):
    return lax.dot_general(a, b, (((1,), (1,)), ((), ())), preferred_element_type=f32)


def dot_tn(a, b):
    return lax.dot_general(a, b, (((0,), (0,)), ((), ())), preferred_element_type=f32)


def start_of(position, first_end, second_end):
    return jnp.where(
        position >= second_end, second_end, jnp.where(position >= first_end, first_end, 0)
    )


def aligned(value, size):
    return pl.multiple_of(value, size)


def transpose_values(source, source_start, values_t, start, width):
    span, target = pl.ds(source_start, tile), pl.ds(start, tile)
    upper = source[span, 256:384].astype(f32).T.astype(bf16)
    lower = source[span, 128:256].astype(f32).T.astype(bf16)
    for head, part in enumerate((upper[0:width], upper[width:], lower[width:])):
        values_t[head, 0:width, target] = part
        values_t[head, width:, target] = jnp.ones((16, tile), bf16)


def masked_heads(queries, heads, width):
    lane = lax.broadcasted_iota(jnp.int32, queries.shape, 1) // width
    return [jnp.where(lane == head, queries, jnp.zeros_like(queries)) for head in range(heads)]


def absorb(
    keys_values, values_t, bias_ref, far_bias, best, running, index, masked_queries, heads,
    key_start, size, key_first, positions, row_start, bias_index, masked, first_time,
):
    keys = keys_values[pl.ds(key_start, size), 0:256]
    if masked:
        key_positions = (
            key_first + key_start + lax.broadcasted_iota(jnp.int32, (size, tile), 0)
        )
        seen = key_positions >= row_start
        if bias_index == 0:
            seen = seen & (key_positions <= positions)
    for head in range(heads):
        scores = dot_nt(keys, masked_queries[head])
        shift_by = 0.0
        if bias_index is None:
            shift_by = far_bias[head]
        else:
            scores = scores + bias_ref[bias_index, head]
        if masked:
            scores = jnp.where(seen, scores, masked_value)
        top = jnp.max(scores, axis=0, keepdims=True) + shift_by
        values = values_t[head, :, pl.ds(key_start, size)]
        if first_time:
            weights = jnp.exp(scores - top).astype(bf16)
            running[index, head] = dot_nn(values, weights)
            best[index, head] = jnp.broadcast_to(top, (8, tile))
        else:
            old = best[index, head, 0:1]
            new = jnp.maximum(old, top)
            weights = jnp.exp(scores - (new - shift_by)).astype(bf16)
            running[index, head] = running[index, head] * jnp.exp(old - new) + dot_nn(
                values, weights
            )
            best[index, head] = jnp.broadcast_to(new, (8, tile))


def attention_near_kernel(
    heads, width, scalars, far_bias, query_ref, bias_ref, kv_one, kv_two, running, best,
    keys_values, values_t,
):
    rows = query_ref.shape[0]
    half = rows // 2
    context, first_end, second_end = scalars[0], scalars[1], scalars[2]
    keys_values[0:half, :] = kv_one[...]
    keys_values[half:, :] = kv_two[...]
    base = context * rows

    def values_step(index, carry):
        start = aligned(index * tile, tile)
        transpose_values(keys_values, start, values_t, start, width)
        return carry

    lax.fori_loop(0, rows // tile, values_step, 0)

    def query_tile(index, carry):
        local = aligned(index * tile, tile)
        positions = base + local + lax.broadcasted_iota(jnp.int32, (1, tile), 1)
        row_start = start_of(positions, first_end, second_end)
        masked_queries = masked_heads(query_ref[pl.ds(local, tile), :], heads, width)

        def take(key_start, bias_index, first_time):
            absorb(
                keys_values, values_t, bias_ref, far_bias, best, running, index,
                masked_queries, heads, key_start, tile, base, positions, row_start, bias_index,
                True, first_time,
            )

        take(local, 0, True)

        @pl.when(index > 0)
        def _():
            take(aligned(local - tile, tile), 1, False)

        def far_step(step, inner):
            take(aligned(step * tile, tile), None, False)
            return inner

        lax.fori_loop(0, jnp.maximum(index - 1, 0), far_step, 0)
        return carry

    lax.fori_loop(0, rows // tile, query_tile, 0)


def attention_near(scalars, far_bias, queries, bias_tiles, kv_one, kv_two, heads, width):
    rows = queries.shape[0]
    tiles = rows // tile
    return pl.pallas_call(
        functools.partial(attention_near_kernel, heads, width),
        out_shape=(
            jax.ShapeDtypeStruct((tiles, heads, width + 16, tile), f32),
            jax.ShapeDtypeStruct((tiles, heads, 8, tile), f32),
        ),
        in_specs=[SMEM, SMEM] + [VMEM] * 4,
        out_specs=(VMEM,) * 2,
        scratch_shapes=[
            pltpu.VMEM((rows, 384), bf16),
            pltpu.VMEM((heads, width + 16, rows), bf16),
        ],
        compiler_params=pltpu.CompilerParams(vmem_limit_bytes=40 * 2**20),
        cost_estimate=pl.CostEstimate(
            flops=2 * rows * rows * 256 * heads,
            bytes_accessed=4 * 2**20,
            transcendentals=rows * rows * heads // 2,
        ),
        name="attention_near",
    )(scalars, far_bias, queries, bias_tiles, kv_one, kv_two)


def attention_far_kernel(
    heads, width, part, piece_count, scalars, far_bias, offsets, query_ref, bias_ref,
    running_in, best_in, *rest
):
    pieces = rest[:piece_count]
    if part == 0:
        packed, lse_ref, keys_values, values_t, running, best, side_one, side_two = rest[
            piece_count:
        ]
    else:
        keys_values, values_t, packed, lse_ref, running, best, side_one, side_two = rest
    rows = query_ref.shape[0]
    half, quarter = rows // 2, rows // 4
    context, first_end, second_end = scalars[0], scalars[1], scalars[2]
    base = context * rows
    if part == 0:
        for index, piece in enumerate(pieces):
            size = piece.shape[0]
            keys_values[pl.ds(aligned(offsets[index], 128), size), :] = piece[...]

        def values_step(index, carry):
            start = aligned(index * tile, tile)
            transpose_values(keys_values, start, values_t, start, width)
            return carry

        lax.fori_loop(0, context * (rows // tile), values_step, 0)
    running[...] = running_in[2 * part : 2 * part + 2]
    best[...] = best_in[2 * part : 2 * part + 2]

    def query_tile(index, carry):
        local = aligned(part * half + index * tile, tile)
        first = base + local
        positions = first + lax.broadcasted_iota(jnp.int32, (1, tile), 1)
        row_start = start_of(positions, first_end, second_end)
        start_first = start_of(first, first_end, second_end)
        start_last = start_of(first + tile - 1, first_end, second_end)
        masked_queries = masked_heads(query_ref[pl.ds(local, tile), :], heads, width)

        def take(key_start, size, bias_index, masked):
            absorb(
                keys_values, values_t, bias_ref, far_bias, best, running, index,
                masked_queries, heads, key_start, size, 0, positions, row_start, bias_index,
                masked, False,
            )

        far_rows = base
        if part == 0:
            far_rows = jnp.where(index == 0, jnp.maximum(base - tile, 0), base)

            @pl.when((index == 0) & (context > 0))
            def _():
                take(aligned(base - tile, tile), tile, 1, True)

        big = 2 * tile
        big_count = far_rows // big
        low = jnp.minimum(start_first // big, big_count)
        middle = jnp.clip((start_last + big - 1) // big, low, big_count)

        def masked_step(step, inner):
            take(aligned(step * big, big), big, None, True)
            return inner

        def plain_step(step, inner):
            take(aligned(step * big, big), big, None, False)
            return inner

        lax.fori_loop(low, middle, masked_step, 0)
        lax.fori_loop(middle, big_count, plain_step, 0)
        if part == 0:

            @pl.when(far_rows > big_count * big)
            def _():
                take(aligned(big_count * big, tile), tile, None, True)

        outs = []
        for head in range(heads):
            total = running[index, head, width : width + 1]
            outs.append(running[index, head, 0:width] / total)
            lse_ref[pl.ds(head, 1), pl.ds(aligned(index * tile, tile), tile)] = best[
                index, head, 0:1
            ] + jnp.log(total)
        span = pl.ds(aligned(index * tile, tile), tile)
        side_one[span, :] = jnp.concatenate([outs[0], outs[1]], axis=0).T
        side_two[span, :] = jnp.concatenate([outs[2], outs[2]], axis=0).T
        return carry

    lax.fori_loop(0, half // tile, query_tile, 0)
    lane = lax.broadcasted_iota(jnp.int32, (quarter, 128), 1)
    packed[:, 0:128] = side_one[0:quarter, :].astype(bf16)
    packed[:, 128:256] = jnp.where(
        lane < width, side_two[0:quarter, :], side_two[quarter:, :]
    ).astype(bf16)
    packed[:, 256:384] = side_one[quarter:, :].astype(bf16)


def attention_far(
    part, scalars, far_bias, offsets, queries, bias_tiles, states, kv, group_rows, heads, width
):
    rows = queries.shape[0]
    half = rows // 2
    shape = jax.ShapeDtypeStruct
    made = (
        shape((group_rows, 384), bf16),
        shape((heads, width + 16, group_rows), bf16),
    )
    outs = (shape((rows // 4, 384), bf16), shape((8, half), f32)) + (made if part == 0 else ())
    return pl.pallas_call(
        functools.partial(attention_far_kernel, heads, width, part, len(kv) if part == 0 else 0),
        out_shape=outs,
        in_specs=[SMEM, SMEM, SMEM] + [VMEM] * (4 + len(kv)),
        out_specs=(VMEM,) * len(outs),
        scratch_shapes=[
            pltpu.VMEM((2, heads, width + 16, tile), f32),
            pltpu.VMEM((2, heads, 8, tile), f32),
            pltpu.VMEM((half, 128), f32),
            pltpu.VMEM((half, 128), f32),
        ],
        compiler_params=pltpu.CompilerParams(vmem_limit_bytes=60 * 2**20),
        cost_estimate=pl.CostEstimate(
            flops=2 * rows * group_rows * 256 * heads,
            bytes_accessed=8 * 2**20,
            transcendentals=rows * group_rows * heads // 2,
        ),
        name="attention_far",
    )(scalars, far_bias, offsets, queries, bias_tiles, *states, *kv)


def attention_backward_kernel(heads, width, masks, piece_count, scalars, far_bias, offsets, *rest):
    query_ref, keys_values, bias_ref, lse_one, lse_two = rest[0:5]
    rest = rest[5:]
    first_call, last_call = masks[0] == 3, masks[0] == 0
    if first_call:
        packed_one, packed_two = rest[0:2]
        pieces = rest[2 : 2 + piece_count]
        rest = rest[2 + piece_count :]
        dout, deltas, dq_t = rest[0:3]
        rest = rest[3:]
    else:
        dout, deltas, dq_in, fold_in = rest[0:4]
        dq_t = rest[4]
        rest = rest[5:]
    out_count = 1 if last_call else 2 * len(masks)
    outs, rest = rest[:out_count], rest[out_count:]
    if last_call:
        dq_ref, rest = rest[0], rest[1:]
    fold_ref, masked_q, masked_o, keys_t, dkv, band_ref = rest
    rows = query_ref.shape[0]
    half, quarter = rows // 2, rows // 4
    context, first_end, second_end = scalars[0], scalars[1], scalars[2]
    tiles_here = rows // tile
    if first_call:
        for index, piece in enumerate(pieces):
            span = pl.ds(aligned(offsets[index], 128), piece.shape[0])
            dout[span, 0:128] = pltpu.roll(piece[:, 128:256].astype(f32), width, 1).astype(bf16)
            dout[span, 128:256] = piece[:, 0:128]
        head_row = lax.broadcasted_iota(jnp.int32, (16, 256), 0)
        head_lane = lax.broadcasted_iota(jnp.int32, (16, 256), 1) // width
        head_hot = (head_row == jnp.where(head_lane == 1, 2, head_lane - 2)).astype(bf16)
        for part in range(4):
            span = slice(part * quarter, (part + 1) * quarter)
            packed = packed_one if part < 2 else packed_two
            lower = packed[:, 128:256].astype(f32)
            if part % 2 == 0:
                upper, lower = packed[:, 0:128], pltpu.roll(lower, width, 1)
            else:
                upper = packed[:, 256:384]
            product = dout[span, :].astype(f32) * jnp.concatenate(
                [lower, upper.astype(f32)], axis=1
            )
            high = product.astype(bf16)
            rest_part = (product - high.astype(f32)).astype(bf16)
            deltas[:, span] = dot_nt(head_hot, high) + dot_nt(head_hot, rest_part)
        dq_t[...] = jnp.zeros_like(dq_t)
        fold_ref[...] = jnp.zeros_like(fold_ref)
    else:
        dq_t[...] = dq_in[...]
        fold_ref[...] = fold_in[...]
    lane = lax.broadcasted_iota(jnp.int32, (rows, 256), 1) // width
    for head in range(heads):
        masked_q[head] = jnp.where(lane == head, query_ref[...], jnp.zeros((rows, 256), bf16))
        slot = 1 if head == 2 else head + 2
        masked_o[head] = jnp.where(lane == slot, dout[...], jnp.zeros((rows, 256), bf16))
    first = context * rows
    all_positions = first + lax.broadcasted_iota(jnp.int32, (1, rows), 1)
    all_starts = start_of(all_positions, first_end, second_end)
    start_first = start_of(first, first_end, second_end)
    start_last = start_of(first + rows - 1, first_end, second_end)

    lse_all = jnp.concatenate([lse_one[...], lse_two[...]], axis=1)

    def block(key_start, base, query_start, bands, masked):
        size = rows - query_start
        here = pl.ds(aligned(key_start - base, tile), tile)
        keys = keys_values[pl.ds(key_start, tile), 0:256]
        values = keys_values[pl.ds(key_start, tile), 128:384]
        key_sum, value_sum = None, None
        if masked:
            key_positions = key_start + lax.broadcasted_iota(jnp.int32, (tile, size), 0)
            seen = key_positions >= all_starts[:, query_start:]
            if 0 in bands:
                seen = seen & (key_positions <= all_positions[:, query_start:])
        span = slice(query_start, rows)
        for head in range(heads):
            queries = masked_q[head, span, :]
            grads = masked_o[head, span, :]
            scores = dot_nt(keys, queries)
            lse = lse_all[head : head + 1, span]
            if bands:
                parts = [
                    scores[:, place * tile : (place + 1) * tile] + bias_ref[band, head]
                    for place, band in enumerate(bands)
                ]
                if size > len(bands) * tile:
                    parts.append(scores[:, len(bands) * tile :] + far_bias[head])
                scores = jnp.concatenate(parts, axis=1)
            else:
                lse = lse - far_bias[head]
            probs = jnp.exp(scores - lse)
            if masked:
                probs = jnp.where(seen, probs, 0.0)
            grad_probs = dot_nt(values, grads)
            grad_scores = probs * (grad_probs - deltas[head : head + 1, span])
            for place, band in enumerate(bands):
                band_ref[band, head] += grad_scores[:, place * tile : (place + 1) * tile]
            low_scores = grad_scores.astype(bf16)
            value_part = dot_nn(probs.astype(bf16), grads)
            key_part = dot_nn(low_scores, queries)
            dq_t[head, :, span] += dot_nn(keys_t[head, :, here], low_scores)
            key_sum = key_part if key_sum is None else key_sum + key_part
            value_sum = value_part if value_sum is None else value_sum + value_part
        return key_sum, value_sum

    lane_tile = lax.broadcasted_iota(jnp.int32, (tile, 128), 1)

    def write(local, key_sum, value_sum):
        span = pl.ds(local, tile)
        dkv[span, 0:128] = key_sum[:, 0:128].astype(bf16)
        dkv[span, 128:256] = jnp.where(
            lane_tile < width, key_sum[:, 128:256], value_sum[:, 0:128]
        ).astype(bf16)
        dkv[span, 256:384] = value_sum[:, 128:256].astype(bf16)

    band_ref[...] = jnp.zeros_like(band_ref)
    for place, mask in enumerate(masks):
        which = context ^ mask
        base = aligned(which * rows, rows)
        dkv[...] = jnp.zeros_like(dkv)

        @pl.when(which <= context)
        def _():
            def transpose_keys(index, carry):
                source = pl.ds(aligned(base + index * tile, tile), tile)
                target = pl.ds(aligned(index * tile, tile), tile)
                lower = keys_values[source, 0:128].astype(f32).T.astype(bf16)
                upper = keys_values[source, 128:256].astype(f32).T.astype(bf16)
                keys_t[0, :, target] = lower[0:width]
                keys_t[1, :, target] = lower[width:]
                keys_t[2, :, target] = upper[0:width]
                return carry

            lax.fori_loop(0, tiles_here, transpose_keys, 0)
            low_tile = which * tiles_here
            high_tile = low_tile + tiles_here
            if mask:
                far_end = jnp.minimum(high_tile, context * tiles_here - 1)
                low = jnp.clip(start_first // tile, low_tile, far_end)
                middle = jnp.clip((start_last + tile - 1) // tile, low, far_end)

                def masked_step(index, carry):
                    start = aligned(index * tile, tile)
                    found = block(start, base, 0, (), True)
                    write(aligned(start - base, tile), *found)
                    return carry

                def plain_step(index, carry):
                    start = aligned(index * tile, tile)
                    found = block(start, base, 0, (), False)
                    write(aligned(start - base, tile), *found)
                    return carry

                lax.fori_loop(low, middle, masked_step, 0)
                lax.fori_loop(middle, far_end, plain_step, 0)

                @pl.when(far_end < high_tile)
                def _():
                    start = aligned(far_end * tile, tile)
                    write(aligned(start - base, tile), *block(start, base, 0, (1,), True))

            else:
                for index in range(tiles_here):
                    start = aligned(base + index * tile, tile)
                    bands = (0, 1) if index + 1 < tiles_here else (0,)
                    write(index * tile, *block(start, base, index * tile, bands, True))

        if mask:
            outs[2 * place][...] = dkv[0:half, :]
            outs[2 * place + 1][...] = dkv[half:, :]
        else:
            outs[0][...] = dkv[...]
    key_index = lax.broadcasted_iota(jnp.int32, (tile, tile), 0)
    query_index = lax.broadcasted_iota(jnp.int32, (tile, tile), 1)
    for head in range(heads):
        both = jnp.where(key_index > query_index, band_ref[1, head], band_ref[0, head])
        by_row = both[0:8]
        for first_row in range(8, tile, 8):
            by_row = by_row + pltpu.roll(both[first_row : first_row + 8], tile - first_row, 1)
        folded = by_row[0:1]
        for row in range(1, 8):
            folded = folded + pltpu.roll(by_row, tile - row, 1)[row : row + 1]
        fold_ref[head : head + 1, :] += folded
    if last_call:
        scale = width ** (-0.5)
        upper = jnp.concatenate([dq_t[0], dq_t[1]], axis=0)
        lower = jnp.concatenate([dq_t[2], jnp.zeros((width, rows), f32)], axis=0)
        dq_ref[:, 0:128] = (upper.T * scale).astype(bf16)
        dq_ref[:, 128:256] = (lower.T * scale).astype(bf16)


def attention_backward(
    masks, scalars, far_bias, offsets, queries, keys_values, bias_tiles, lse, given, piece_count,
    heads, width,
):
    rows = queries.shape[0]
    half = rows // 2
    shape = jax.ShapeDtypeStruct
    first_call, last_call = masks[0] == 3, masks[0] == 0
    outs = (shape((heads, width, rows), f32),)
    if first_call:
        outs = (shape((rows, 256), bf16), shape((16, rows), f32)) + outs
    if last_call:
        outs = outs + (shape((rows, 384), bf16),)
    else:
        outs = outs + (shape((half, 384), bf16),) * (2 * len(masks))
    if last_call:
        outs = outs + (shape((rows, 256), bf16),)
    outs = outs + (shape((8, tile), f32),)

    return pl.pallas_call(
        functools.partial(attention_backward_kernel, heads, width, masks, piece_count),
        out_shape=outs,
        in_specs=[SMEM, SMEM, SMEM] + [VMEM] * (5 + len(given)),
        out_specs=(VMEM,) * len(outs),
        scratch_shapes=[
            pltpu.VMEM((heads, rows, 256), bf16),
            pltpu.VMEM((heads, rows, 256), bf16),
            pltpu.VMEM((heads, width, rows), bf16),
            pltpu.VMEM((rows, 384), bf16),
            pltpu.VMEM((2, heads, tile, tile), f32),
        ],
        compiler_params=pltpu.CompilerParams(vmem_limit_bytes=60 * 2**20),
        cost_estimate=pl.CostEstimate(
            flops=10 * rows * rows * 256 * heads if first_call else 0,
            bytes_accessed=10 * 2**20 if first_call else 2**10,
            transcendentals=0,
        ),
        name="attention_backward",
    )(scalars, far_bias, offsets, queries, keys_values, bias_tiles, *lse, *given)


bucket_edges = np.array(
    [19, 21, 24, 27, 31, 35, 40, 46, 52, 59, 67, 77, 87, 99, 113], dtype=np.int32
)


def bucket_tiles():
    key = np.arange(tile)[None, :, None]
    query = np.arange(tile)[None, None, :]
    lag = np.arange(3)[:, None, None] * tile + query - key
    clipped = np.maximum(lag, 0)
    counted = (clipped[..., None] >= bucket_edges).sum(-1)
    return np.where(clipped < 16, clipped, 16 + counted).astype(np.int32)


def shape(dims, dtype):
    return jax.ShapeDtypeStruct(dims, dtype)


def params(mebibytes):
    return pltpu.CompilerParams(vmem_limit_bytes=mebibytes * 2**20)


def cost(flops, bytes_accessed):
    return pl.CostEstimate(flops=flops, bytes_accessed=bytes_accessed, transcendentals=0)


def gelu_constants():
    return 0.7978845608028654, 0.044715


def prepare_kernel(
    part, padded, scalars, table, route_ref, order_ref, rows_ref, columns_ref,
    bias_ref, ranks, hot_ref, tall,
):
    pair_count = order_ref.shape[1]
    rows = pair_count // 2
    expert_pad = hot_ref.shape[0]
    step = 256
    live_end = scalars[2] - scalars[0] * rows
    order = order_ref[...]
    index_row = lax.broadcasted_iota(jnp.int32, (pair_count, 128), 0)
    index_lane = lax.broadcasted_iota(jnp.int32, (pair_count, 128), 1)
    digits = jnp.where(
        index_lane == 0, index_row // 64, jnp.where(index_lane == 1, index_row % 64, 0)
    ).astype(f32).astype(bf16)

    def rank_step(index, carry):
        start = aligned(index * step, step)
        pair = start + lax.broadcasted_iota(jnp.int32, (step, pair_count), 0)
        hit = (pair == order).astype(f32).astype(bf16)
        found = dot_nn(hit, digits)
        position = found[:, 0:1] * 64.0 + found[:, 1:2]
        ranks[pl.ds(start, step), :] = jnp.broadcast_to(position, (step, 128))
        return carry

    lax.fori_loop(0, pair_count // step, rank_step, 0)
    rank_row = ranks[...].T[0:1, :]
    position = lax.broadcasted_iota(jnp.int32, (1, rows), 1)
    live = position < live_end
    expert_row = jnp.concatenate([route_ref[0:1, :], route_ref[1:2, :]], axis=1)
    live_row = jnp.concatenate([live, live], axis=1)
    expert_index = lax.broadcasted_iota(jnp.int32, (expert_pad, pair_count), 0)
    hot = ((expert_index == expert_row) & live_row).astype(f32)
    hot_ref[...] = hot.astype(bf16)

    def count_step(index, counts):
        start = aligned(index * step, step)
        earlier = (ranks[pl.ds(start, step), 0:1] < rank_row).astype(f32).astype(bf16)
        return counts + dot_nn(hot_ref[:, pl.ds(start, step)], earlier)

    counts = lax.fori_loop(
        0, pair_count // step, count_step, jnp.zeros((expert_pad, pair_count), f32)
    )
    slot = jnp.sum(counts * hot, axis=0, keepdims=True).astype(jnp.int32)
    own = slot - (scalars[3] & 1) * part
    place = jnp.where(live_row & (own >= 0) & (own < part), expert_row * padded + own, -1)
    rows_ref[...] = jnp.full_like(rows_ref, -1)
    rows_ref[0:1, :] = place[:, 0:rows]
    rows_ref[1:2, :] = place[:, rows:]
    tall[...] = jnp.full_like(tall, -1.0)
    tall[0:1, :] = place[:, 0:rows].astype(f32)
    tall[1:2, :] = place[:, rows:].astype(f32)
    columns_ref[...] = tall[...].T.astype(jnp.int32)
    key = lax.broadcasted_iota(jnp.int32, (8, tile), 0)
    query = lax.broadcasted_iota(jnp.int32, (8, tile), 1)
    heads = bias_ref.shape[1]
    for head in range(heads):
        bias_ref[2, head] = jnp.full((tile, tile), table[31, head], f32)

    def bias_step(index, carry):
        start = aligned(index * 8, 8)
        for band in range(2):
            lag = band * tile + query - key - start
            found = [jnp.full((8, tile), table[0, head], f32) for head in range(heads)]
            for bucket, edge in enumerate(list(range(1, 17)) + list(bucket_edges), start=1):
                beyond = lag >= int(edge)
                found = [
                    jnp.where(beyond, table[bucket, head], found[head]) for head in range(heads)
                ]
            for head in range(heads):
                bias_ref[band, head, pl.ds(start, 8), :] = found[head]
        return carry

    lax.fori_loop(0, tile // 8, bias_step, 0)


def prepare(scalars, table, route_rows, order_row, expert_count, part, padded):
    rows = route_rows.shape[1]
    heads = table.shape[1]
    expert_pad = max(16, expert_count)
    return pl.pallas_call(
        functools.partial(prepare_kernel, part, padded),
        out_shape=(
            shape((8, rows), jnp.int32),
            shape((rows, 128), jnp.int32),
            shape((3, heads, tile, tile), f32),
        ),
        in_specs=[SMEM, SMEM, VMEM, VMEM],
        out_specs=(VMEM,) * 3,
        scratch_shapes=[
            pltpu.VMEM((2 * rows, 128), f32),
            pltpu.VMEM((expert_pad, 2 * rows), bf16),
            pltpu.VMEM((128, rows), f32),
        ],
        compiler_params=params(40),
        cost_estimate=cost(10 * 10**9, 3 * 2**20),
        name="prepare",
    )(scalars, table, route_rows, order_row)


def pack_kernel(query, key, value, output, gain_one, gain_two, router, block):
    size = query.shape[0]
    experts = router.shape[1]
    block[...] = jnp.zeros_like(block)
    block[:, 0:192] = query[...]
    gains = jnp.concatenate([gain_one[...], gain_two[...]], axis=0).astype(f32)
    block[:, 192:194] = gains.T.astype(bf16)
    block[:, 256:448] = key[...]
    block[:, 448:512] = value[:, 128:192]
    block[:, 512:640] = value[:, 0:128]
    block[:, 640:832] = output[...].astype(f32).T.astype(bf16)
    block[:, 832 : 832 + experts] = router[...]


def pack_weights(query, key, value, output, gain_one, gain_two, router):
    size = query.shape[0]
    return pl.pallas_call(
        pack_kernel,
        out_shape=shape((size, 896), bf16),
        in_specs=[VMEM] * 7,
        out_specs=VMEM,
        compiler_params=params(60),
        cost_estimate=cost(0, 2**19),
        name="pack_weights",
    )(query, key, value, output, gain_one[None], gain_two[None], router)


def project_kernel(piece_count, offsets, token_ref, *rest):
    pieces = rest[:piece_count]
    hidden_ref, query_ref, kv_one, kv_two, weight_ref, output_ref, gain_ref = rest[piece_count:]
    for index, piece in enumerate(pieces):
        span = pl.ds(aligned(offsets[index], 16), piece.shape[0])
        weight_ref[span, :] = piece[:, 0:640]
        output_ref[span, :] = piece[:, 640:896]
    rows = token_ref.shape[0]
    half = rows // 2
    gains = weight_ref[:, 128:256].astype(f32).T
    gain_ref[0:1, :] = gains[64:65, :]
    gain_ref[1:2, :] = gains[65:66, :]
    step = 256
    lane = lax.broadcasted_iota(jnp.int32, (step, 256), 1)
    for start in range(0, rows, step):
        inputs = token_ref[start : start + step, :].astype(f32)
        scale = lax.rsqrt(jnp.mean(inputs * inputs, axis=-1, keepdims=True) + epsilon)
        hidden = (inputs * scale * gain_ref[0:1, :]).astype(bf16)
        hidden_ref[start : start + step, :] = hidden
        queries = dot_nn(hidden, weight_ref[:, 0:256]).astype(bf16)
        query_ref[start : start + step, :] = jnp.where(
            lane < 192, queries * bf16(0.125), jnp.zeros_like(queries)
        )
        target, base = (kv_one, 0) if start < half else (kv_two, half)
        target[start - base : start - base + step, :] = dot_nn(
            hidden, weight_ref[:, 256:640]
        ).astype(bf16)


def project(offsets, tokens, pieces):
    rows, model = tokens.shape
    return pl.pallas_call(
        functools.partial(project_kernel, len(pieces)),
        out_shape=(
            shape((rows, model), bf16),
            shape((rows, 256), bf16),
            shape((rows // 2, 384), bf16),
            shape((rows // 2, 384), bf16),
            shape((model, 640), bf16),
            shape((model, 256), bf16),
            shape((8, model), f32),
        ),
        in_specs=[SMEM, VMEM] + [VMEM] * len(pieces),
        out_specs=(VMEM,) * 7,
        compiler_params=params(40),
        cost_estimate=cost(2 * rows * model * 640, 6 * 2**20),
        name="project",
    )(offsets, tokens, *pieces)


def assemble_kernel(piece_count, offsets, *rest):
    pieces = rest[:piece_count]
    out_ref = rest[piece_count]
    for index, piece in enumerate(pieces):
        size = piece.shape[0]
        out_ref[pl.ds(aligned(offsets[index], 16), size), :] = piece[...].astype(out_ref.dtype)


def assemble(offsets, pieces, dtype):
    total = sum(piece.shape[0] for piece in pieces)
    width = pieces[0].shape[1]
    return pl.pallas_call(
        functools.partial(assemble_kernel, len(pieces)),
        out_shape=shape((total, width), dtype),
        in_specs=[SMEM] + [VMEM] * len(pieces),
        out_specs=VMEM,
        compiler_params=params(40),
        cost_estimate=cost(0, 6 * total * width),
        name="assemble",
    )(offsets, *pieces)


def dispatch_kernel(
    width, expert_count, padded, scalars, token_ref, gain_ref, route_ref, row_place, *rest
):
    attended = rest[0:8]
    weights = rest[8:12]
    residual_ref, hidden_ref, info_ref, attended_ref, sent = rest[12:17]
    packed, joined, column = rest[17:]
    rows, model = token_ref.shape
    half, quarter = rows // 2, rows // 4
    lane_low = lax.broadcasted_iota(jnp.int32, (quarter, 128), 1)
    for source in range(4):
        for part in range(2):
            piece = attended[2 * source + part]
            middle = piece[:, 128:256].astype(f32)
            span = slice(part * half, part * half + quarter)
            packed[source, span, 0:128] = piece[:, 0:128]
            packed[source, span, 128:256] = jnp.where(lane_low < width, middle, 0.0).astype(bf16)
            span = slice(part * half + quarter, (part + 1) * half)
            packed[source, span, 0:128] = piece[:, 256:384]
            packed[source, span, 128:256] = jnp.where(
                lane_low < width, pltpu.roll(middle, 64, 1), 0.0
            ).astype(bf16)
    step = 256
    lane = lax.broadcasted_iota(jnp.int32, (step, 128), 1)
    valid = (lane >= 64) & (lane < 64 + expert_count)

    def token_step(index, carry):
        start = aligned(index * step, step)
        span = pl.ds(start, step)
        residual = token_ref[span, :].astype(f32)
        for source in range(4):
            residual = residual + dot_nt(packed[source, span, :], weights[source][...])
        joined[span, :] = residual
        scale = lax.rsqrt(jnp.mean(residual * residual, axis=-1, keepdims=True) + epsilon)
        hidden = (residual * scale * gain_ref[1:2, :]).astype(bf16)
        hidden_ref[span, :] = hidden
        logits = dot_nn(hidden, weights[0][:, 128:256])
        logits = jnp.where(valid, logits, masked_value)
        powers = jnp.where(valid, jnp.exp(logits - jnp.max(logits, axis=-1, keepdims=True)), 0.0)
        probs = powers / jnp.sum(powers, axis=-1, keepdims=True)
        first = jnp.sum(
            jnp.where(lane == route_ref[span, 0:1] + 64, probs, 0.0), axis=-1, keepdims=True
        )
        second = jnp.sum(
            jnp.where(lane == route_ref[span, 1:2] + 64, probs, 0.0), axis=-1, keepdims=True
        )
        total = first + second
        info_ref[span, :] = jnp.where(
            lane == 0,
            first / total,
            jnp.where(lane == 1, second / total, jnp.where(lane == 2, total, probs)),
        )
        return carry

    lax.fori_loop(0, rows // step, token_step, 0)
    here = pl.ds(aligned(scalars[3] * quarter, quarter), quarter)
    residual_ref[...] = joined[here, :]
    for source in range(4):
        attended_ref[:, source * 256 : (source + 1) * 256] = packed[source, here, :]
    gates = info_ref[...].T
    gate_one, gate_two = gates[0:1, :], gates[1:2, :]
    place_one, place_two = row_place[0:1, :], row_place[1:2, :]
    column[...] = jnp.zeros_like(column)

    taken = 4 * padded

    def expert_rows(index, carry):
        start = aligned(index * taken, 64)
        slot = start + lax.broadcasted_iota(jnp.int32, (taken, rows), 0)
        hit_one, hit_two = slot == place_one, slot == place_two
        picked = jnp.where(hit_one | hit_two, 1.0, 0.0).astype(bf16)
        sent[pl.ds(start, taken), :] = dot_nn(picked, hidden_ref[...]).astype(bf16)
        gate = jnp.where(hit_one, gate_one, jnp.where(hit_two, gate_two, 0.0))
        gate = jnp.sum(gate, axis=-1, keepdims=True)
        for chunk in range(4):
            write_digits(
                sent, column, start + chunk * padded, padded,
                gate[chunk * padded : (chunk + 1) * padded],
            )
        return carry

    lax.fori_loop(0, expert_count // 4, expert_rows, 0)


def write_digits(rows_ref, column, start, padded, values):
    column[0:padded, :] = jnp.broadcast_to(values, (padded, 128))
    row = column[...].T[0:1, :]
    high = row.astype(bf16).astype(f32)
    middle = (row - high).astype(bf16).astype(f32)
    low = row - high - middle
    size = row.shape[1]
    index = lax.broadcasted_iota(jnp.int32, (16, size), 0)
    block = jnp.where(
        index == 0, high, jnp.where(index == 1, middle, jnp.where(index == 2, low, 0.0))
    )
    span = pl.ds(aligned(start + padded - 16, 16), 16)
    rows_ref[span, 0:size] = block.astype(bf16)
    rows_ref[span, size:] = jnp.zeros((16, rows_ref.shape[1] - size), bf16)


def read_digits(rows_ref, start, padded):
    wide = (padded + 127) // 128 * 128
    span = pl.ds(aligned(start + padded - 16, 16), 16)
    return jnp.sum(rows_ref[span, 0:wide].astype(f32), axis=0, keepdims=True)


def dispatch(
    scalars, tokens, gains, routes, row_place, attended, weights, width, expert_count, padded
):
    rows, model = tokens.shape
    slots = expert_count * padded
    wide = (padded + 127) // 128 * 128
    return pl.pallas_call(
        functools.partial(dispatch_kernel, width, expert_count, padded),
        out_shape=(
            shape((rows // 4, model), f32),
            shape((rows, model), bf16),
            shape((rows, 128), f32),
            shape((rows // 4, 1024), bf16),
            shape((slots, model), bf16),
        ),
        in_specs=[SMEM] + [VMEM] * 16,
        out_specs=(VMEM,) * 5,
        scratch_shapes=[
            pltpu.VMEM((4, rows, 256), bf16),
            pltpu.VMEM((rows, model), f32),
            pltpu.VMEM((wide, 128), f32),
        ],
        compiler_params=params(60),
        cost_estimate=cost(2 * rows * model * (1024 + slots), 16 * 2**20),
        name="dispatch",
    )(scalars, tokens, gains, routes, row_place, *attended, *weights)


def scatter_kernel(value_ref, row_place, sent):
    rows = value_ref.shape[0]
    place_one, place_two = row_place[0:1, :], row_place[1:2, :]
    fill = sent.shape[0] // 2

    def slot_step(index, carry):
        start = aligned(index * fill, fill)
        slot = start + lax.broadcasted_iota(jnp.int32, (fill, rows), 0)
        picked = jnp.where((slot == place_one) | (slot == place_two), 1.0, 0.0).astype(bf16)
        sent[pl.ds(start, fill), :] = dot_nn(picked, value_ref[...]).astype(bf16)
        return carry

    lax.fori_loop(0, sent.shape[0] // fill, slot_step, 0)


def scatter_rows(values, row_place, slots):
    rows, model = values.shape
    return pl.pallas_call(
        scatter_kernel,
        out_shape=shape((slots, model), bf16),
        in_specs=[VMEM, VMEM],
        out_specs=VMEM,
        compiler_params=params(40),
        cost_estimate=cost(2 * rows * model * slots, 6 * 2**20),
        name="scatter_rows",
    )(values, row_place)


def expert_kernel(
    padded, in_own, in_partner, out_own, out_partner, rows_ref, grads_ref, acted_ref, pre_ref,
    back_ref, column, gate_ref,
):
    hidden = in_own.shape[1]
    root, cubic = gelu_constants()
    wide = column.shape[0]
    column[...] = jnp.zeros_like(column)
    slots = rows_ref.shape[0]
    taken = 4 * padded

    def one(index, carry):
        start = aligned(index * taken, 64)
        span = pl.ds(start, taken)
        for chunk in range(4):
            gates = read_digits(rows_ref, start + chunk * padded, padded)
            gates = jnp.broadcast_to(gates, (128, wide)).T[0:padded, :]
            gate_ref[chunk * padded : (chunk + 1) * padded, :] = gates
        gate = jnp.concatenate([gate_ref[...], gate_ref[...]], axis=1)
        gate_part = None
        for side, (in_ref, out_ref) in enumerate(((in_own, out_own), (in_partner, out_partner))):
            for first in range(0, hidden, 256):
                part = slice(first, first + 256)
                pre = dot_nn(rows_ref[span, :], in_ref[:, part])
                grad_acted = dot_nt(grads_ref[span, :], out_ref[part, :])
                square = pre * pre
                bent = jnp.tanh(root * pre * (1.0 + cubic * square))
                acted = 0.5 * pre * (1.0 + bent)
                slope = 0.5 * (1.0 + bent) + 0.5 * pre * (1.0 - bent * bent) * root * (
                    1.0 + 3.0 * cubic * square
                )
                acted_ref[side, span, part] = (acted * gate).astype(bf16)
                product = grad_acted * acted
                folded = product[:, 0:128] + product[:, 128:256]
                gate_part = folded if gate_part is None else gate_part + folded
                pre_ref[side, span, part] = (grad_acted * slope * gate).astype(bf16)
        back = dot_nt(pre_ref[0, span, :], in_own[...])
        back = back + dot_nt(pre_ref[1, span, :], in_partner[...])
        back_ref[span, :] = back.astype(bf16)
        gate_part = jnp.sum(gate_part, axis=-1, keepdims=True)
        for chunk in range(4):
            write_digits(
                back_ref, column, start + chunk * padded, padded,
                gate_part[chunk * padded : (chunk + 1) * padded],
            )
        return carry

    lax.fori_loop(0, slots // taken, one, 0)


def expert_step(in_parts, out_parts, rows_in, grads_in, padded):
    slots, model = rows_in.shape
    hidden = in_parts[0].shape[1]
    wide = (padded + 127) // 128 * 128
    return pl.pallas_call(
        functools.partial(expert_kernel, padded),
        out_shape=(
            shape((2, slots, hidden), bf16),
            shape((2, slots, hidden), bf16),
            shape((slots, model), bf16),
        ),
        in_specs=[VMEM] * 6,
        out_specs=(VMEM,) * 3,
        scratch_shapes=[pltpu.VMEM((wide, 128), f32), pltpu.VMEM((4 * padded, 128), f32)],
        compiler_params=params(60),
        cost_estimate=cost(12 * slots * model * hidden, 24 * 2**20),
        name="expert_step",
    )(*in_parts, *out_parts, rows_in, grads_in)


def expert_out_kernel(acted_ref, out_own, out_partner, out_ref):
    step = out_ref.shape[0] // 4

    def one(index, carry):
        span = pl.ds(aligned(index * step, 16), step)
        total = dot_nn(acted_ref[0, span, :], out_own[...])
        total = total + dot_nn(acted_ref[1, span, :], out_partner[...])
        out_ref[span, :] = total.astype(bf16)
        return carry

    lax.fori_loop(0, 4, one, 0)


def expert_outputs(acted, out_parts):
    _, slots, hidden = acted.shape
    model = out_parts[0].shape[1]
    return pl.pallas_call(
        expert_out_kernel,
        out_shape=shape((slots, model), bf16),
        in_specs=[VMEM] * 3,
        out_specs=VMEM,
        compiler_params=params(60),
        cost_estimate=cost(4 * slots * model * hidden, 10 * 2**20),
        name="expert_outputs",
    )(acted, *out_parts)


def write_ring(scalars, joined, own, next_ref, last_ref, far_one, far_two):
    quarter = own.shape[0]
    eighth = quarter // 2
    rank = scalars[3]

    def rows_of(which):
        return aligned(lax.rem(rank + which, 4) * quarter, quarter)

    own[...] = joined[pl.ds(rows_of(0), quarter), :]
    next_ref[...] = joined[pl.ds(rows_of(1), quarter), :].astype(bf16)
    last_ref[...] = joined[pl.ds(rows_of(3), quarter), :].astype(bf16)
    far = rows_of(2)
    far_one[...] = joined[pl.ds(far, eighth), :].astype(bf16)
    far_two[...] = joined[pl.ds(aligned(far + eighth, eighth), eighth), :].astype(bf16)


def ring_shapes(rows, model):
    quarter, eighth = shape((rows // 4, model), bf16), shape((rows // 8, model), bf16)
    return (shape((rows // 4, model), f32), quarter, quarter, eighth, eighth)


def combine_grads_kernel(
    expert_count, padded, far, scalars, place_ref, info_ref, route_ref, router_ref, back_ref, *rest
):
    if far:
        logit_ref, far_one, far_two, digits = rest
    else:
        far_logits, logit_ref, own, next_ref, last_ref, digits = rest
    rows = place_ref.shape[0]
    quarter, eighth = rows // 4, rows // 8
    slots = back_ref.shape[0]
    rank = scalars[3]
    wide = (padded + 127) // 128 * 128
    lane_digit = lax.broadcasted_iota(jnp.int32, (padded, 128), 1)

    def column_step(expert, carry):
        start = aligned(expert * padded, 16)
        row = jnp.broadcast_to(read_digits(back_ref, start, padded), (128, wide))
        column = row.T[0:padded, :]
        high = column.astype(bf16).astype(f32)
        middle = (column - high).astype(bf16).astype(f32)
        digits[pl.ds(start, padded), :] = jnp.where(
            lane_digit == 0,
            high,
            jnp.where(lane_digit == 1, middle, jnp.where(lane_digit == 2, column - high - middle, 0.0)),
        ).astype(bf16)
        return carry

    lax.fori_loop(0, expert_count, column_step, 0)
    lane = lax.broadcasted_iota(jnp.int32, (quarter, 128), 1)
    slot = lax.broadcasted_iota(jnp.int32, (quarter, slots), 1)

    def rows_of(which):
        return pl.ds(aligned(lax.rem(rank + which, 4) * quarter, quarter), quarter)

    def tokens(which):
        span = rows_of(which)
        info, place = info_ref[span, :], place_ref[span, :]
        hit_one, hit_two = slot == place[:, 0:1], slot == place[:, 1:2]
        ones = jnp.where(hit_one | hit_two, 1.0, 0.0).astype(bf16)
        total = dot_nn(ones, back_ref[...])
        signs = jnp.where(hit_one, 1.0, jnp.where(hit_two, -1.0, 0.0)).astype(bf16)
        difference = jnp.sum(dot_nn(signs, digits[...]), axis=-1, keepdims=True) / info[:, 2:3]
        picked = jnp.where(
            lane == route_ref[span, 0:1] + 64,
            info[:, 1:2] * difference,
            jnp.where(lane == route_ref[span, 1:2] + 64, -info[:, 0:1] * difference, 0.0),
        )
        probs = jnp.where((lane >= 64) & (lane < 64 + expert_count), info, 0.0)
        grads = probs * (picked - jnp.sum(probs * picked, axis=-1, keepdims=True))
        grads = grads.astype(bf16)
        return grads, total + dot_nt(grads, router_ref[:, 128:256])

    if far:
        grads, total = tokens(2)
        logit_ref[...] = grads
        far_one[...] = total[0:eighth].astype(bf16)
        far_two[...] = total[eighth:].astype(bf16)
    else:
        logit_ref[rows_of(2), :] = far_logits[...]
        for which, target in ((1, next_ref), (3, last_ref)):
            grads, total = tokens(which)
            logit_ref[rows_of(which), :] = grads
            target[...] = total.astype(bf16)
        grads, total = tokens(0)
        logit_ref[rows_of(0), :] = grads
        own[...] = total


def combine_grads(far, scalars, place, info, routes, router, back, given, expert_count, padded):
    rows = place.shape[0]
    model = router.shape[0]
    slots = back.shape[0]
    half = shape((rows // 8, model), bf16)
    if far:
        outs = (shape((rows // 4, 128), bf16), half, half)
    else:
        outs = (shape((rows, 128), bf16), shape((rows // 4, model), f32))
        outs = outs + (shape((rows // 4, model), bf16),) * 2
    return pl.pallas_call(
        functools.partial(combine_grads_kernel, expert_count, padded, far),
        out_shape=outs,
        in_specs=[SMEM] + [VMEM] * (5 + len(given)),
        out_specs=(VMEM,) * len(outs),
        scratch_shapes=[pltpu.VMEM((slots, 128), bf16)],
        compiler_params=params(60),
        cost_estimate=cost(2 * rows * model * slots, 8 * 2**20),
        name="combine_grads",
    )(scalars, place, info, routes, router, back, *given)


def combine_outs_kernel(place_ref, rows_ref, out_ref):
    step = 256
    slot = lax.broadcasted_iota(jnp.int32, (step, rows_ref.shape[0]), 1)

    def token_step(index, carry):
        span = pl.ds(aligned(index * step, step), step)
        place = place_ref[span, :]
        hit = (slot == place[:, 0:1]) | (slot == place[:, 1:2])
        out_ref[span, :] = dot_nn(jnp.where(hit, 1.0, 0.0).astype(bf16), rows_ref[...]).astype(bf16)
        return carry

    lax.fori_loop(0, out_ref.shape[0] // step, token_step, 0)


def combine_outs(place, rows_in):
    rows = place.shape[0]
    slots, model = rows_in.shape
    return pl.pallas_call(
        combine_outs_kernel,
        out_shape=shape((rows, model), bf16),
        in_specs=[VMEM] * 2,
        out_specs=VMEM,
        compiler_params=params(60),
        cost_estimate=cost(2 * rows * model * slots, 8 * 2**20),
        name="combine_outs",
    )(place, rows_in)


def received(own, from_last, from_next):
    return own[...] + from_last[...].astype(f32) + from_next[...].astype(f32)


def norm_back_kernel(gain_index, has_bypass_rows, scalars, value_ref, gain_ref, bypass_ref, *rest):
    grads = received(*rest[:3])
    rest = rest[3:]
    weights = ()
    if gain_index == 1:
        weights, rest = rest[0:4], rest[4:]
    else:
        blocks_ref, rest = rest[0], rest[1:]
    full_ref, low_ref, gain_grad = rest[0:3]
    quarter = grads.shape[0]
    here = pl.ds(aligned(scalars[3] * quarter, quarter), quarter)
    values = (value_ref[here, :] if gain_index == 0 else value_ref[...]).astype(f32)
    bypass = (bypass_ref[here, :] if has_bypass_rows else bypass_ref[...]).astype(f32)
    scale = lax.rsqrt(jnp.mean(values * values, axis=-1, keepdims=True) + epsilon)
    normed = values * scale
    scaled = grads * gain_ref[gain_index : gain_index + 1, :]
    gain_grad[...] = jnp.broadcast_to(
        jnp.sum(grads * normed, axis=0, keepdims=True), gain_grad.shape
    )
    out = bypass + scale * (scaled - normed * jnp.mean(scaled * normed, axis=-1, keepdims=True))
    full_ref[...] = out
    low = out.astype(bf16)
    if weights:
        low_ref[...] = low
    else:
        block = blocks_ref.shape[0] // 3
        for place, step in enumerate((0, 3, 1, 2)):
            target = lax.rem(scalars[3] + step, 4)
            low_ref[target, 0:quarter, :] = low
            columns = slice(place * 256, (place + 1) * 256)
            for third in range(3):
                low_ref[target, quarter:, third * 256 : (third + 1) * 256] = blocks_ref[
                    third * block : (third + 1) * block, columns
                ].astype(bf16)
    lane = lax.broadcasted_iota(jnp.int32, (quarter, 256), 1)
    for weight, target in zip(weights, rest[3:]):
        target[...] = jnp.where(lane < 192, dot_nn(low, weight[...]), 0.0).astype(bf16)


def norm_back(gain_index, has_bypass_rows, scalars, values, gains, bypass, parts, weights=(), blocks=None):
    quarter, model = parts[0].shape
    low = shape((quarter, model), bf16)
    if blocks is not None:
        low = shape((4, quarter + blocks.shape[0] // 3, model), bf16)
    extra = tuple(weights) if blocks is None else (blocks,)
    return pl.pallas_call(
        functools.partial(norm_back_kernel, gain_index, has_bypass_rows),
        out_shape=(shape((quarter, model), f32), low, shape((8, model), f32))
        + (shape((quarter, 256), bf16),) * len(weights),
        in_specs=[SMEM] + [VMEM] * (6 + len(extra)),
        out_specs=(VMEM,) * (3 + len(weights)),
        compiler_params=params(60),
        cost_estimate=cost(quarter * model * 16, 6 * 2**20),
        name="norm_back",
    )(scalars, values, gains, bypass, *parts, *extra)


def unpack_kernel(arrived, input_ref, outer_ref):
    quarter = input_ref.shape[0] // 4
    block = outer_ref.shape[0] // 3
    for source in range(4):
        input_ref[source * quarter : (source + 1) * quarter, :] = arrived[
            source, 0:quarter, :
        ].astype(f32)
    total = arrived[0, quarter:, :].astype(f32)
    for source in range(1, 4):
        total = total + arrived[source, quarter:, :].astype(f32)
    for third in range(3):
        outer_ref[third * block : (third + 1) * block, :] = total[:, third * 256 : third * 256 + 256]


def unpack(arrived, rows, shard):
    return pl.pallas_call(
        unpack_kernel,
        out_shape=(shape((rows, arrived.shape[2]), f32), shape((shard, 256), f32)),
        in_specs=[VMEM],
        out_specs=(VMEM,) * 2,
        compiler_params=params(40),
        cost_estimate=cost(0, 5 * 2**20),
        name="unpack",
    )(arrived)


def finish_kernel(residual_ref, part_ref, out_ref):
    total = residual_ref[...]
    quarter = total.shape[0]
    for source in range(4):
        total = total + part_ref[source * quarter : (source + 1) * quarter, :].astype(f32)
    low = total.astype(bf16)
    for target in range(4):
        out_ref[target * quarter : (target + 1) * quarter, :] = low


def finish(residual, parts):
    quarter, model = residual.shape
    return pl.pallas_call(
        finish_kernel,
        out_shape=shape((4 * quarter, model), bf16),
        in_specs=[VMEM] * 2,
        out_specs=VMEM,
        compiler_params=params(40),
        cost_estimate=cost(quarter * model * 4, 4 * 2**20),
        name="finish",
    )(residual, parts)


def hidden_grad_kernel(
    scalars, dq_ref, weight_ref, own, beside_one, beside_two, across_one, across_two, dkv_ref, *rest
):
    ring, joined = rest[:5], rest[5]
    half = own.shape[0] // 2
    for part, (beside, across) in enumerate(
        ((beside_one, across_one), (beside_two, across_two))
    ):
        span = slice(part * half, (part + 1) * half)
        total = own[span, :].astype(f32) + beside[...].astype(f32) + across[...].astype(f32)
        total = total.astype(bf16)
        dkv_ref[span, :] = total
        joined[span, :] = dot_nt(dq_ref[span, :], weight_ref[:, 0:256]) + dot_nt(
            total, weight_ref[:, 256:640]
        )
    write_ring(scalars, joined, *ring)


def hidden_grad(scalars, dq, weights, own, beside, across):
    rows = dq.shape[0]
    model = weights.shape[0]
    return pl.pallas_call(
        hidden_grad_kernel,
        out_shape=(shape((rows, 384), bf16),) + ring_shapes(rows, model),
        in_specs=[SMEM] + [VMEM] * 7,
        out_specs=(VMEM,) * 6,
        scratch_shapes=[pltpu.VMEM((rows, model), f32)],
        compiler_params=params(40),
        cost_estimate=cost(2 * rows * model * 640, 8 * 2**20),
        name="hidden_grad",
    )(scalars, dq, weights, own, *beside, *across)


def split_by_side(scalars, whole, mine, other):
    half = mine.shape[0]
    side = scalars[5]
    mine[...] = whole[pl.ds(aligned(side * half, 16), half), :]
    other[...] = whole[pl.ds(aligned((1 - side) * half, 16), half), :].astype(other.dtype)


def output_grad_kernel(scalars, branch_ref, attended_ref, hidden_ref, logit_ref, *rest):
    outs, whole = rest[:-1], rest[-1]
    whole[...] = dot_tn(branch_ref[...], attended_ref[...])
    router = dot_tn(hidden_ref[...], logit_ref[...])
    for source in range(4):
        whole[:, source * 256 + 128 : source * 256 + 256] += router
    if len(outs) == 1:
        outs[0][...] = whole[...]
    else:
        size = outs[0].shape[0] // 4
        context, side = scalars[0], scalars[5]
        for out, masks in zip(outs, ((0, 2), (1, 3))):
            for place, mask in enumerate(masks):
                for far in range(2):
                    start = aligned((4 * (side ^ far) + (context ^ mask)) * size, 16)
                    target = slice((2 * place + far) * size, (2 * place + far + 1) * size)
                    out[target, :] = whole[pl.ds(start, size), :].astype(out.dtype)


def output_grads(scalars, branch, attended, hidden, grad_logits, small):
    rows, model = hidden.shape
    outs = (shape((model, 1024), f32),)
    if small:
        outs = (shape((model // 2, 1024), f32), shape((model // 2, 1024), bf16))
    return pl.pallas_call(
        output_grad_kernel,
        out_shape=outs,
        in_specs=[SMEM] + [VMEM] * 4,
        out_specs=(VMEM,) * len(outs),
        scratch_shapes=[pltpu.VMEM((model, 1024), f32)],
        compiler_params=params(60),
        cost_estimate=cost(2 * rows * model * 384, 6 * 2**20),
        name="output_grads",
    )(scalars, branch, attended, hidden, grad_logits)


def projection_grad_kernel(scalars, hidden_ref, dq_ref, dkv_ref, gain_ref, fold_ref, *rest):
    outs, whole = rest[:-1], rest[-1]
    hidden = hidden_ref[...]
    whole[:, 0:256] = dot_tn(hidden, dq_ref[...])
    whole[:, 256:640] = dot_tn(hidden, dkv_ref[...])
    lane = lax.broadcasted_iota(jnp.int32, (whole.shape[0], 128), 1)
    column = jnp.broadcast_to(gain_ref[0:1, :], (128, whole.shape[0])).T
    whole[:, 128:256] = jnp.where(lane < 64, whole[:, 128:256], column)
    if len(outs) == 2:
        side = scalars[5]
        block = outs[0].shape[0] // 4
        size = block - 8
        for which, out in ((side, outs[0]), (1 - side, outs[1])):
            for context in range(4):
                start = aligned((which * 4 + context) * size, 8)
                out[context * block : context * block + size, :] = whole[pl.ds(start, size), :]
                tail = slice(context * block + size, (context + 1) * block)
                out[tail, 0:256] = fold_ref[...]
                out[tail, 256:640] = jnp.zeros((8, 384), f32)
    else:
        outs[0][...] = whole[...]


def projection_grads(scalars, hidden, dq, dkv, gain_grad, fold, small):
    rows, model = hidden.shape
    outs = (shape((model // 2 + 32, 640), f32),) * 2 if small else (shape((model, 640), f32),)
    return pl.pallas_call(
        projection_grad_kernel,
        out_shape=outs,
        in_specs=[SMEM] + [VMEM] * 5,
        out_specs=(VMEM,) * len(outs),
        scratch_shapes=[pltpu.VMEM((model, 640), f32)],
        compiler_params=params(40),
        cost_estimate=cost(2 * rows * model * 640, 6 * 2**20),
        name="projection_grads",
    )(scalars, hidden, dq, dkv, gain_grad, fold)


def share_kernel(scalars, mine, other, *outs):
    size = outs[0].shape[0]
    context = scalars[0]
    for mask, out in enumerate(outs):
        span = pl.ds(aligned((context ^ mask) * size, 8), size)
        total = mine[span, :] + other[span, :].astype(f32)
        out[...] = total.astype(out.dtype)


def share(scalars, mine, other):
    rows, width = mine.shape
    return pl.pallas_call(
        share_kernel,
        out_shape=(shape((rows // 4, width), f32),) + (shape((rows // 4, width), other.dtype),) * 3,
        in_specs=[SMEM, VMEM, VMEM],
        out_specs=(VMEM,) * 4,
        compiler_params=params(40),
        cost_estimate=cost(rows * width, 12 * rows * width),
        name="share",
    )(scalars, mine, other)


def shift(value, amount):
    size = lax.axis_size("tensor")
    return lax.ppermute(value, "tensor", [(i, (i + amount) % size) for i in range(size)])


def cross(value, mask):
    size = lax.axis_size("context")
    return lax.ppermute(value, "context", [(i, i ^ mask) for i in range(size)])


def partner(value):
    return lax.ppermute(value, "tensor", [(i, i ^ 1) for i in range(lax.axis_size("tensor"))])


def spread(value):
    return [value] + [shift(value, step) for step in (1, -1, 2)]


def sum_ranks(value):
    total = value
    for step in (1, 2, 3):
        total = total + shift(value, step)
    return total


def ring_gather(one, two):
    last_one, next_two = shift(one, 1), shift(two, -1)
    last_two, next_one = shift(two, 1), shift(one, -1)
    far_one, far_two = shift(last_one, 1), shift(next_two, -1)
    return (one, two, last_one, last_two, next_one, next_two, far_one, far_two)


def ring_ranks(rank):
    return [lax.rem(rank + step, 4) for step in (0, 3, 1, 2)]


def added(first, second):
    return (first.astype(f32) + second.astype(f32)).astype(bf16)


def ring_start(far_one, far_two):
    return shift(far_one, 1), shift(far_two, -1)


def with_first(whole, arrived):
    half = arrived.shape[0]
    return jnp.concatenate([added(whole[:half], arrived), whole[half:]], axis=0)


def with_second(whole, arrived):
    half = arrived.shape[0]
    return jnp.concatenate([whole[:half], added(whole[half:], arrived)], axis=0)


def ring_finish(next_block, last_block, arrived_one, arrived_two):
    from_last = shift(with_first(next_block, arrived_one), 1)
    from_next = shift(with_second(last_block, arrived_two), -1)
    return from_last, from_next


ALL_ROWS = ("dp", "context")


def exchange(rows_out):
    return lax.all_to_all(rows_out, ALL_ROWS, split_axis=0, concat_axis=0, tiled=True)


def gather_weights(block, small, axis):
    size = block.shape[axis]
    if not small:
        whole = lax.all_gather(block, ALL_ROWS, axis=axis, tiled=True)
        return [whole], jnp.zeros((1,), jnp.int32)
    context, side = lax.axis_index("context"), lax.axis_index("dp")
    pieces = [block] + [cross(block, mask) for mask in (1, 2, 3)]
    pieces = pieces + [lax.ppermute(piece, "dp", [(0, 1), (1, 0)]) for piece in pieces]
    return pieces, jnp.stack(
        [((side ^ far) * 4 + (context ^ mask)) * size for far in range(2) for mask in range(4)]
    )


def swap_sides(parts):
    if len(parts) == 1:
        return parts
    return parts[0], lax.ppermute(parts[1], "dp", [(0, 1), (1, 0)])


def share_blocks(scalars, parts):
    return parts if len(parts) == 1 else share(scalars, *parts)


def halve(mine, arrived):
    total = mine + arrived.astype(f32)
    half = total.shape[0] // 2
    return total[:half], total[half:].astype(bf16)


def scatter_blocks(blocks):
    if len(blocks) == 1:
        return lax.psum_scatter(blocks[0], ALL_ROWS, scatter_dimension=0, tiled=True)
    total = blocks[0]
    for mask in (1, 2, 3):
        total = total + cross(blocks[mask], mask).astype(f32)
    return total


def on_device(
    tokens_in, query_weight, key_weight, value_weight, output_weight, bias_table, attention_gain,
    router_weight, expert_gain, expert_in, expert_out, routes, pair_order, seq_lengths, cotangent,
):
    rows, model = tokens_in.shape
    heads = bias_table.shape[1]
    width = query_weight.shape[1] // heads
    group_rows = rows * lax.axis_size("context")
    expert_count = router_weight.shape[1]
    capacity = (9 * rows + 4 * expert_count - 1) // (4 * expert_count)
    count = lax.axis_size("dp") * lax.axis_size("context")
    small = count == 8
    context, rank = lax.axis_index("context"), lax.axis_index("tensor")
    here = lax.axis_index("dp") * lax.axis_size("context") + context
    first_end = seq_lengths[0, 0]
    second_end = first_end + seq_lengths[0, 1]
    side = lax.axis_index("dp")
    scalars = jnp.stack([context, first_end, second_end, rank, here, side]).astype(jnp.int32)
    part = capacity // 2
    padded = (part + 15) // 16 * 16 + 16
    slots = expert_count * padded
    shard = query_weight.shape[0]
    block = pack_weights(
        query_weight, key_weight, value_weight, output_weight, attention_gain, expert_gain, router_weight
    )
    tie = lax.optimization_barrier
    half, quarter = rows // 2, rows // 4
    kv_offsets = jnp.stack(
        [(context ^ mask) * rows + part * half for mask in range(4) for part in range(2)]
    )
    token_offsets = jnp.stack([which * quarter for which in ring_ranks(rank)])
    far_bias = bias_table[-1]
    order_row = (pair_order & 1) * rows + (pair_order >> 1)
    pieces, offsets = gather_weights(block, small, 0)
    in_parts = (expert_in[0], partner(expert_in[0]))
    out_parts = (expert_out[0], partner(expert_out[0]))
    hidden_one, queries, kv_one, kv_two, weights, output_own, gains = project(
        offsets, tokens_in, pieces
    )
    output_parts = [output_own] + [shift(output_own, step) for step in (1, -1, 2)]
    beside_one, across_two = cross(kv_one, 1), cross(kv_two, 2)
    beside_two, across_one = cross(kv_two, 1), cross(kv_one, 2)
    order_row, queries = tie((order_row, queries))
    row_place, column_place, bias_tiles = prepare(
        scalars, bias_table, routes.T, order_row, expert_count, part, padded
    )
    beside_one, across_two, row_place = tie((beside_one, across_two, row_place))
    kv_far = cross(beside_one, 2), cross(across_two, 1)
    kv_pieces = (kv_one, kv_two, beside_one, beside_two, across_one, across_two) + kv_far
    cotangent_rows = scatter_rows(cotangent, row_place, slots)
    states = attention_near(
        scalars, far_bias, queries, bias_tiles, kv_one, kv_two, heads, width
    )
    states, kv_pieces, cotangent_rows, in_parts, out_parts = tie(
        (states, kv_pieces, cotangent_rows, in_parts, out_parts)
    )
    packed_one, lse_one, *made = attention_far(
        0, scalars, far_bias, kv_offsets, queries, bias_tiles, states, kv_pieces, group_rows,
        heads, width,
    )
    attended_one = spread(packed_one)
    packed_two, lse_two = attention_far(
        1, scalars, far_bias, kv_offsets, queries, bias_tiles, states, made, group_rows,
        heads, width,
    )
    packed_two, attended_one, output_parts, cotangent_rows = tie(
        (packed_two, attended_one, output_parts, cotangent_rows)
    )
    attended_two = spread(packed_two)
    cotangent_rows = exchange(cotangent_rows)
    attended = [piece for pair in zip(attended_one, attended_two) for piece in pair]
    attended, cotangent_rows = tie((attended, cotangent_rows))
    residual, hidden_two, info, attended_here, rows_out = dispatch(
        scalars, tokens_in, gains, routes, row_place, attended, output_parts, width,
        expert_count, padded,
    )
    expert_rows = exchange(rows_out)
    acted, grad_pre, back = expert_step(
        in_parts, out_parts, expert_rows, cotangent_rows, padded
    )
    back = exchange(back)
    in_grad_partner = dot_tn(expert_rows, grad_pre[1]).astype(bf16)
    out_grad_partner = dot_tn(acted[1], cotangent_rows).astype(bf16)
    in_grad_partner, out_grad_partner, acted, grad_pre = tie(
        (in_grad_partner, out_grad_partner, acted, grad_pre)
    )
    in_grad_partner = partner(in_grad_partner)
    outs = expert_outputs(acted, out_parts)
    expert_out_grad = dot_tn(acted[0], cotangent_rows)
    expert_in_grad = dot_tn(expert_rows, grad_pre[0])
    back, outs, expert_out_grad, expert_in_grad = tie(
        (back, outs, expert_out_grad, expert_in_grad)
    )
    combine = (scalars, column_place, info, routes, output_own, back)
    far_logits, *far = combine_grads(True, *combine, (), expert_count, padded)
    arrived = ring_start(*far)
    grad_logits, own, *ring = combine_grads(False, *combine, (far_logits,), expert_count, padded)
    arrived, ring, outs, in_grad_partner = tie((arrived, ring, outs, in_grad_partner))
    ring, outs = (own,) + ring_finish(*ring, *arrived), exchange(outs)
    ring, outs = tie((ring, outs))
    grad_one, grad_branch, gain_two_grad, *grad_heads = norm_back(
        1, True, scalars, residual, gains, cotangent, ring, output_parts
    )
    head_pieces = (
        grad_heads[0], shift(grad_heads[2], 1), shift(grad_heads[1], -1), shift(grad_heads[3], 2)
    )
    outer = output_grads(scalars, grad_branch, attended_here, hidden_two, grad_logits, small)
    mixed = combine_outs(column_place, outs)
    head_pieces, mixed, out_grad_partner, outer = tie(
        (head_pieces, mixed, out_grad_partner, outer)
    )
    if small:
        outer = outer[0], cross(outer[1], 1)
    out_grad_partner = partner(out_grad_partner)
    mixed = lax.all_to_all(mixed, "tensor", split_axis=0, concat_axis=0, tiled=True)
    shared = (scalars, far_bias, token_offsets, queries, made[0], bias_tiles)
    lse = (lse_one, lse_two)
    dout, deltas, dq_t, far_one, far_two, fold = attention_backward(
        (3,), *shared, lse, (packed_one, packed_two, *head_pieces), 4, heads, width
    )
    arrived = cross(far_one, 1), cross(far_two, 2)
    dq_t, *beside_across, fold = attention_backward(
        (1, 2), *shared, lse, (dout, deltas, dq_t, fold), 0, heads, width
    )
    beside, across = beside_across[0:2], beside_across[2:4]
    beside_two, across_one = added(beside[1], arrived[1]), added(across[0], arrived[0])
    dq_t, mixed, beside_two, across_one, outer = tie(
        (dq_t, mixed, beside_two, across_one, outer)
    )
    from_square = (
        (cross(beside[0], 1), cross(beside_two, 1)), (cross(across_one, 2), cross(across[1], 2))
    )
    layer_out = finish(residual, mixed)
    dq_t, layer_out = tie((dq_t, layer_out))
    layer_out = lax.all_to_all(layer_out, "tensor", split_axis=0, concat_axis=0, tiled=True)
    dq_t, own, dq, fold = attention_backward(
        (0,), *shared, lse, (dout, deltas, dq_t, fold), 0, heads, width
    )
    dq, from_square, out_grad_partner = tie((dq, from_square, out_grad_partner))
    dkv, own, *ring = hidden_grad(scalars, dq, weights, own, *from_square)
    arrived = ring_start(*ring[2:4])
    inner_parts = projection_grads(scalars, hidden_one, dq, dkv, gain_two_grad, fold, small)
    if small:
        outer = halve(*outer)
    arrived, inner_parts, outer = tie((arrived, inner_parts, outer))
    inner_parts = swap_sides(inner_parts)
    ring = (own,) + ring_finish(*ring[0:2], *arrived)
    if small:
        outer = halve(outer[0], cross(outer[1], 2))
        outer_grads = outer[0] + swap_sides(outer)[1].astype(f32)
    else:
        outer_grads = lax.psum_scatter(outer[0], ALL_ROWS, scatter_dimension=0, tiled=True)
    ring, layer_out, outer_grads = tie((ring, layer_out, outer_grads))
    _, input_low, _ = norm_back(
        0, False, scalars, tokens_in, gains, grad_one, ring, blocks=outer_grads
    )
    arrived = lax.all_to_all(input_low, "tensor", split_axis=0, concat_axis=0, tiled=True)
    inner_parts, layer_out, input_low = tie((inner_parts, layer_out, input_low))
    layer_out = assemble(jnp.zeros((1,), jnp.int32), [layer_out], bf16)
    projected = scatter_blocks(share_blocks(scalars, inner_parts))
    expert_out_grad, expert_in_grad, projected = tie((expert_out_grad, expert_in_grad, projected))
    input_grad, outer_grads = unpack(arrived, rows, shard)
    expert_out_grad = (expert_out_grad + out_grad_partner.astype(f32))[None]
    expert_in_grad = (expert_in_grad + in_grad_partner.astype(f32))[None]
    output_grad = outer_grads[:, :192].T
    router_grad = outer_grads[:, 192 : 192 + expert_count]
    fold = projected[shard:, :256] if small else lax.psum(fold, ALL_ROWS)
    projected = projected[:shard]
    query_grad, key_grad = projected[:, :192], projected[:, 256:448]
    value_grad = jnp.concatenate([projected[:, 512:], projected[:, 448:512]], axis=1)
    gain_one_grad = jnp.sum(
        query_weight.astype(f32) * query_grad
        + key_weight.astype(f32) * key_grad
        + value_weight.astype(f32) * value_grad,
        axis=1,
        keepdims=True,
    )
    gain_grads = sum_ranks(jnp.concatenate([gain_one_grad, projected[:, 192:193]], axis=1))
    bucket_row = jnp.asarray(bucket_tiles()[0, 0])
    bucket_hot = (bucket_row[None, :] == jnp.arange(bias_table.shape[0] - 1)[:, None]).astype(f32)
    near_grad = jnp.sum(bucket_hot[:, None, :] * fold[None, :heads, :], axis=-1)
    table_grad = jnp.concatenate([near_grad, -jnp.sum(near_grad, axis=0, keepdims=True)], axis=0)
    return (
        layer_out,
        input_grad,
        query_grad,
        key_grad,
        value_grad,
        output_grad,
        table_grad,
        gain_grads[:, 0] / attention_gain.astype(f32),
        router_grad,
        gain_grads[:, 1],
        expert_in_grad,
        expert_out_grad,
    )


def solution(mesh):
    rows = P(("dp", "context"), None)
    return jax.shard_map(
        on_device,
        mesh=mesh,
        in_specs=(
            rows,
            P(("dp", "context"), "tensor"),
            P(("dp", "context"), "tensor"),
            P(("dp", "context"), "tensor"),
            P("tensor", ("dp", "context")),
            P(None, "tensor"),
            P(("dp", "context")),
            rows,
            P(("dp", "context")),
            P(("dp", "context"), None, "tensor"),
            P(("dp", "context"), "tensor", None),
            rows,
            rows,
            P("dp", None),
            rows,
        ),
        out_specs=(
            rows,
            rows,
            P(("dp", "context"), "tensor"),
            P(("dp", "context"), "tensor"),
            P(("dp", "context"), "tensor"),
            P("tensor", ("dp", "context")),
            P(None, "tensor"),
            P(("dp", "context")),
            rows,
            P(("dp", "context")),
            P(("dp", "context"), None, "tensor"),
            P(("dp", "context"), "tensor", None),
        ),
        check_vma=False,
    )
```

time: 571 us -> 497 us (0.87)
  the two profiles are of different devices: /device:TPU:0 before, /device:TPU:6 now
where the time goes in v2:
time: 497 us; the launch traced here: 488 us
  Pallas kernels  187 us (38%)
  starting transfers between devices  107 us (22%)
  waiting for transfers between devices  106 us (21%)
  blocking collectives  29 us (6%)
  local copies, waits for them, and re-layouts  24.9 us (5%)
  other arithmetic  16.5 us (3%)
  matrix products  15.3 us (3%)
    ppermute x23, waiting for transfers between devices, shift(): lax.ppermute(value, 'tensor', [(i, (i + amount) % size) for i in range(si...  78.4 us
    pallas_call x3, Pallas kernels, attention_backward(): pl.pallas_call(functools.partial(attention_backward_kernel, heads, width,...  53.8 us
    ppermute x23, starting transfers between devices, shift(): lax.ppermute(value, 'tensor', [(i, (i + amount) % size) for i in range(si...  53.2 us
    all_to_all x1, blocking collectives, exchange(): lax.all_to_all(rows_out, ALL_ROWS, split_axis=0, concat_axis=0, tiled=True)  29 us
    ppermute x20, waiting for transfers between devices, cross(): return lax.ppermute(value, 'context', [(i, i ^ mask) for i in range(size)])  23.7 us
    unnamed x149, local copies, waits for them, and re-layouts  20 us
    ppermute x20, starting transfers between devices, cross(): return lax.ppermute(value, 'context', [(i, i ^ mask) for i in range(size)])  19 us
    pallas_call x2, Pallas kernels, attention_far(): pl.pallas_call(functools.partial(attention_far_kernel, heads, width, part...  18.8 us
  transfers between devices with their start and end apart: 59, of which 22 were waited for; matrix products, arithmetic and copies ran while one was open for 8% of the time, Pallas kernels for 30%

profile of v2, /device:TPU:6, one launch (start us, length us, event | category | flops | bytes accessed | tf_op | source)
XLA Modules:
  0.0 488.3 jit_solution(10384338670444603000)
XLA Ops:
  31.3 12.4 %prepare.1 = (s32[8,1024]{1,0:T(8,128)S(1)}, s32[1024,128]{1,0:T(8,128)S(1)}, f32[3,3,256,256]{3,2,1,0:T(8,128)S(1)}) custom-call(s32[6]{0:T(128)S(1)} %stack.92.scalars, f32[32,3]{1,0:T(8,128)S(1)} %copy.56.table, s32[2,1024]{1,0:T(2,128)S(1)} %bitcast.78, s32[1,2048]{1,0:T(1,128)S(1)} %shift-right-arithmetic_add_fusion.order_ref), custom_call_target="tpu_custom_call" | custom-call | flops 10000000000 | bytes 3145728 | tf_op jit(solution)/shard_map/prepare/pallas_call | solution.py:633
  52.6 7.4 %attention_near.1 = (f32[4,3,80,256]{3,2,1,0:T(8,128)S(1)}, f32[4,3,8,256]{3,2,1,0:T(8,128)S(1)}) custom-call(s32[6]{0:T(128)S(1)} %stack.92.scalars, f32[3]{0:T(128)S(1)} %slice_reduce_fusion.far_bias, bf16[1024,256]{1,0:T(8,128)(2,1)S(1)} %get-tuple-element.181.query_ref.rest_0_, f32[3,3,256,256]{3,2,1,0:T(8,128)S(1)} %get-tuple-element.183.bias_ref.rest_2_, ...), custom_call_target="tpu_custom_call" | custom-call | flops 1610612736 | bytes 4194304 | tf_op jit(solution)/shard_map/attention_near/pallas_call | solution.py:142
  70.2 14.1 %attention_far.2 = (bf16[256,384]{1,0:T(8,128)(2,1)}, f32[8,512]{1,0:T(8,128)}, bf16[4096,384]{1,0:T(8,128)(2,1)}, bf16[3,80,4096]{2,1,0:T(8,128)(2,1)}) custom-call(s32[6]{0:T(128)} %copy-done.16, f32[3]{0:T(128)} %copy-done.20, s32[8]{0:T(128)} %stack.115.offsets, bf16[1024,256]{1,0:T(8,128)(2,1)} %copy-done.2, f32[3,3,256,256]{3,2,1,0:T(8,128)} %copy-done, ...), custom_call_target="tpu_custom_call" | custom-call | flops 6442450944 | bytes 8388608 | tf_op jit(solution)/shard_map/attention_far/pallas_call | solution.py:270
  88.4 8.8 %collective-permute-start.17 = (bf16[256,384]{1,0:T(8,128)(2,1)}, bf16[256,384]{1,0:T(8,128)(2,1)S(1)}, u32[]{:S(2)}, u32[]{:S(2)}) collective-permute-start(bf16[256,384]{1,0:T(8,128)(2,1)} %get-tuple-element.217.rest_0_.rest_5_), channel_id=1, source_target_pairs={{0,2},{1,3},{2,0},{3,1},{4,6},{5,7},{6,4},{7,5},{8,10},{9,11},{10,... | collective-permute-start | bytes 589832 | tf_op jit(solution)/shard_map/ppermute | solution.py:1398
  97.1 4.8 attention_far.3
  101.9 8.9 %collective-permute-done.20.rest_11_.rest_6_ = bf16[768,256]{1,0:T(8,128)(2,1)S(1)} collective-permute-done((bf16[768,256]{1,0:T(8,128)(2,1)S(1)}, bf16[768,256]{1,0:T(8,128)(2,1)S(1)}, u32[]{:S(2)}, u32[]{:S(2)}) %collective-permute-start.20) | collective-permute-done | bytes 393248 | tf_op jit(solution)/shard_map/ppermute | solution.py:1398
  110.8 8.3 %collective-permute-done.17.rest_6_ = bf16[256,384]{1,0:T(8,128)(2,1)S(1)} collective-permute-done((bf16[256,384]{1,0:T(8,128)(2,1)}, bf16[256,384]{1,0:T(8,128)(2,1)S(1)}, u32[]{:S(2)}, u32[]{:S(2)}) %collective-permute-start.17) | collective-permute-done | bytes 196640 | tf_op jit(solution)/shard_map/ppermute | solution.py:1398
  119.8 4.8 all-to-all-start
  129.5 4.7 collective-permute-done.21.rest_3_
  136.4 8.0 %collective-permute-done.23.rest_7_ = bf16[256,384]{1,0:T(8,128)(2,1)S(1)} collective-permute-done((bf16[256,384]{1,0:T(8,128)(2,1)S(1)}, bf16[256,384]{1,0:T(8,128)(2,1)S(1)}, u32[]{:S(2)}, u32[]{:S(2)}) %collective-permute-start.23) | collective-permute-done | bytes 196640 | tf_op jit(solution)/shard_map/ppermute | solution.py:1398
  147.5 13.6 %dispatch.1 = (f32[256,768]{1,0:T(8,128)}, bf16[1024,768]{1,0:T(8,128)(2,1)}, f32[1024,128]{1,0:T(8,128)}, bf16[256,1024]{1,0:T(8,128)(2,1)}, bf16[1280,768]{1,0:T(8,128)(2,1)}) custom-call(s32[6]{0:T(128)} %copy-done.16, bf16[1024,768]{1,0:T(8,128)(2,1)} %value_ref.3, f32[8,768]{1,0:T(8,128)} %copy-done.15, s32[1024,2]{1,0:T(8,128)} %copy.57.route_ref, ...), custom_call_target="tpu_custom_call" | custom-call | flops 3623878656 | bytes 16777216 | tf_op jit(solution)/shard_map/dispatch/pallas_call | solution.py:864
  161.1 29.0 %all_to_all.76 = bf16[8,160,768]{2,1,0:T(8,128)(2,1)} all-to-all(bf16[8,160,768]{2,1,0:T(8,128)(2,1)} %bitcast.87), channel_id=1, replica_groups=mesh['dp'=2,'context'=4,'tensor'=4] {'dp','context'}, dimensions={0} | all-to-all | bytes 3932160 | tf_op jit(solution)/shard_map/all_to_all | solution.py:1460
  190.1 18.0 %expert_step.1 = (bf16[2,1280,768]{2,1,0:T(8,128)(2,1)}, bf16[2,1280,768]{2,1,0:T(8,128)(2,1)}, bf16[1280,768]{1,0:T(8,128)(2,1)}) custom-call(bf16[768,768]{1,0:T(8,128)(2,1)} %bitcast.94, bf16[768,768]{1,0:T(8,128)(2,1)} %collective-permute-done.13.in_partner, bf16[768,768]{1,0:T(8,128)(2,1)} %bitcast.96, ...), custom_call_target="tpu_custom_call" | custom-call | flops 9059696640 | bytes 25165824 | tf_op jit(solution)/shard_map/expert_step/pallas_call | solution.py:968
  208.2 7.0 %all-to-all-start.2 = ((bf16[8,160,768]{2,1,0:T(8,128)(2,1)}), bf16[8,160,768]{2,1,0:T(8,128)(2,1)}, u32[]{:S(2)}, u32[]{:S(2)}) async-start(bf16[8,160,768]{2,1,0:T(8,128)(2,1)} %bitcast.86), calls=%async_computation.2 | async-start | bytes 3932160 | tf_op jit(solution)/shard_map/all_to_all | solution.py:1460
  215.2 4.5 fusion.15
  225.7 7.9 %expert_outputs.1 = bf16[1280,768]{1,0:T(8,128)(2,1)} custom-call(bf16[2,1280,768]{2,1,0:T(8,128)(2,1)} %get-tuple-element.241.acted_ref, bf16[768,768]{1,0:T(8,128)(2,1)} %bitcast.97, bf16[768,768]{1,0:T(8,128)(2,1)} %collective-permute-done.14.out_partner), custom_call_target="tpu_custom_call" | custom-call | flops 3019898880 | bytes 10485760 | tf_op jit(solution)/shard_map/expert_outputs/pallas_call | solution.py:1000
  233.7 4.7 fusion
  238.4 5.8 %combine_grads.2 = (bf16[256,128]{1,0:T(8,128)(2,1)}, bf16[128,768]{1,0:T(8,128)(2,1)}, bf16[128,768]{1,0:T(8,128)(2,1)}) custom-call(s32[6]{0:T(128)} %copy-done.16, s32[1024,128]{1,0:T(8,128)} %copy-done.28, f32[1024,128]{1,0:T(8,128)} %get-tuple-element.231.info_ref, s32[1024,2]{1,0:T(8,128)} %copy.57.route_ref, bf16[768,256]{1,0:T(8,128)(2,1)} %copy-done.13, ...), custom_call_target="tpu_custom_call" | custom-call | flops 2013265920 | bytes 8388608 | tf_op jit(solution)/shard_map/combine_grads/pallas_call | solution.py:1110
  248.2 8.8 %combine_grads.3 = (bf16[1024,128]{1,0:T(8,128)(2,1)}, f32[256,768]{1,0:T(8,128)}, bf16[256,768]{1,0:T(8,128)(2,1)}, bf16[256,768]{1,0:T(8,128)(2,1)}) custom-call(s32[6]{0:T(128)} %copy-done.16, s32[1024,128]{1,0:T(8,128)} %copy-done.28, f32[1024,128]{1,0:T(8,128)} %get-tuple-element.231.info_ref, s32[1024,2]{1,0:T(8,128)} %copy.57.route_ref, ...), custom_call_target="tpu_custom_call" | custom-call | flops 2013265920 | bytes 8388608 | tf_op jit(solution)/shard_map/combine_grads/pallas_call | solution.py:1110
  268.6 9.3 %collective-permute-done.28.rest_2_ = bf16[256,768]{1,0:T(8,128)(2,1)S(1)} collective-permute-done((bf16[256,768]{1,0:T(8,128)(2,1)S(1)}, bf16[256,768]{1,0:T(8,128)(2,1)S(1)}, u32[]{:S(2)}, u32[]{:S(2)}) %collective-permute-start.28) | collective-permute-done | bytes 393248 | tf_op jit(solution)/shard_map/ppermute | solution.py:1398
  278.0 8.3 %collective-permute-done.27.rest_1_ = bf16[256,768]{1,0:T(8,128)(2,1)S(1)} collective-permute-done((bf16[256,768]{1,0:T(8,128)(2,1)S(1)}, bf16[256,768]{1,0:T(8,128)(2,1)S(1)}, u32[]{:S(2)}, u32[]{:S(2)}) %collective-permute-start.27) | collective-permute-done | bytes 393248 | tf_op jit(solution)/shard_map/ppermute | solution.py:1398
  287.1 5.0 %norm_back.2 = (f32[256,768]{1,0:T(8,128)}, bf16[256,768]{1,0:T(8,128)(2,1)}, f32[8,768]{1,0:T(8,128)}, bf16[256,256]{1,0:T(8,128)(2,1)}, bf16[256,256]{1,0:T(8,...) custom-call(s32[6]{0:T(128)} %copy-done.16, f32[256,768]{1,0:T(8,128)} %get-tuple-element.229.value_ref.residual_ref, ...), custom_call_target="tpu_custom_call" | custom-call | flops 3145728 | bytes 6291456 | tf_op jit(solution)/shard_map/norm_back/pallas_call | solution.py:1199
  300.4 6.1 %combine_outs.1 = bf16[1024,768]{1,0:T(8,128)(2,1)} custom-call(s32[1024,128]{1,0:T(8,128)} %copy-done.28, bf16[1280,768]{1,0:T(8,128)(2,1)} %bitcast.79), custom_call_target="tpu_custom_call" | custom-call | flops 2013265920 | bytes 8388608 | tf_op jit(solution)/shard_map/combine_outs/pallas_call | solution.py:1139
  311.3 15.8 %attention_backward.3 = (bf16[1024,256]{1,0:T(8,128)(2,1)}, f32[16,1024]{1,0:T(8,128)}, f32[3,64,1024]{2,1,0:T(8,128)}, bf16[512,384]{1,0:T(8,128)(2,1)}, bf16[512,384]{1,0:T(8,128)(2,1)}, /*index=5*/f32[8,256]{1,0:T(8,128)}) custom-call(s32[6]{0:T(128)} %copy-done.16, f32[3]{0:T(128)} %copy-done.20, s32[4]{0:T(128)} %pad_add_fusion.offsets, ...), custom_call_target="tpu_custom_call" | custom-call | flops 8053063680 | bytes 10485760 | tf_op jit(solution)/shard_map/attention_backward/pallas_call | solution.py:501
  331.2 25.7 %attention_backward.4 = (f32[3,64,1024]{2,1,0:T(8,128)}, bf16[512,384]{1,0:T(8,128)(2,1)}, bf16[512,384]{1,0:T(8,128)(2,1)}, bf16[512,384]{1,0:T(8,128)(2,1)}, b...) custom-call(s32[6]{0:T(128)} %copy-done.16, f32[3]{0:T(128)} %copy-done.20, s32[4]{0:T(128)} %pad_add_fusion.offsets, ...), custom_call_target="tpu_custom_call" | custom-call | bytes 1024 | tf_op jit(solution)/shard_map/attention_backward/pallas_call | solution.py:501
  369.7 12.3 %attention_backward.5 = (f32[3,64,1024]{2,1,0:T(8,128)}, bf16[1024,384]{1,0:T(8,128)(2,1)}, bf16[1024,256]{1,0:T(8,128)(2,1)}, f32[8,256]{1,0:T(8,128)}) custom-call(s32[6]{0:T(128)} %copy-done.16, f32[3]{0:T(128)} %copy-done.20, s32[4]{0:T(128)} %pad_add_fusion.offsets, bf16[1024,256]{1,0:T(8,128)(2,1)} %copy-done.2, ...), custom_call_target="tpu_custom_call" | custom-call | bytes 1024 | tf_op jit(solution)/shard_map/attention_backward/pallas_call | solution.py:501
  403.0 7.3 %collective-permute-done.45 = bf16[192,1024]{1,0:T(8,128)(2,1)S(1)} collective-permute-done((bf16[192,1024]{1,0:T(8,128)(2,1)S(1)}, bf16[192,1024]{1,0:T(8,128)(2,1)S(1)}, u32[]{:S(2)}, u32[]{:S(2)}) %collective-permute-start.45) | collective-permute-done | bytes 393248 | tf_op jit(solution)/shard_map/ppermute | solution.py:1403
  410.6 12.1 %collective-permute-start.43 = (bf16[256,768]{1,0:T(8,128)(2,1)S(1)}, bf16[256,768]{1,0:T(8,128)(2,1)S(1)}, u32[]{:S(2)}, u32[]{:S(2)}) collective-permute-start(bf16[256,768]{1,0:T(8,128)(2,1)S(1)} %pad_maximum_fusion.2), channel_id=1, source_target_pairs={{0,1},{1,2},{2,3},{3,0},{4,5},{5,6},{6,7},{7,4},{8,9},{9,10},{10,1... | collective-permute-start | bytes 1179656 | tf_op jit(solution)/shard_map/ppermute | solution.py:1398
  423.5 9.0 %collective-permute-done.43.rest_1_ = bf16[256,768]{1,0:T(8,128)(2,1)S(1)} collective-permute-done((bf16[256,768]{1,0:T(8,128)(2,1)S(1)}, bf16[256,768]{1,0:T(8,128)(2,1)S(1)}, u32[]{:S(2)}, u32[]{:S(2)}) %collective-permute-start.43) | collective-permute-done | bytes 393248 | tf_op jit(solution)/shard_map/ppermute | solution.py:1398
  437.5 5.0 %all-to-all-start.6 = ((bf16[4,288,768]{2,1,0:T(8,128)(2,1)}), bf16[4,288,768]{2,1,0:T(8,128)(2,1)S(1)}, u32[]{:S(2)}, u32[]{:S(2)}) async-start(bf16[4,288,768]{2,1,0:T(8,128)(2,1)} %get-tuple-element.331), calls=%async_computation.6 | async-start | bytes 3538944 | tf_op jit(solution)/shard_map/all_to_all | solution.py:1657
  466.5 5.5 %add_bitcast_fusion = (f32[1,768,768]{2,1,0:T(8,128)}, f32[1,768,768]{2,1,0:T(8,128)}) fusion(f32[768,768]{1,0:T(8,128)} %fusion.2, bf16[768,768]{1,0:T(8,128)(2,1)} %collective-permute-done.39, f32[768,768]{1,0:T(8,128)} %fusion, bf16[768,768]{1,0:T(8,128)(2,1)S(1)} %copy-done.39), kind=kLoop, calls=%fused_computation | loop fusion | flops 2359296 | bytes 11796480 | tf_op jit(solution)/shard_map/broadcast_in_dim | solution.py:1663
  475.1 8.5 %collective-permute-done.51 = f32[96,2]{0,1:T(2,128)S(1)} collective-permute-done((f32[96,2]{0,1:T(2,128)S(1)}, f32[96,2]{0,1:T(2,128)S(1)}, u32[]{:S(2)}, u32[]{:S(2)}) %collective-permute-start.51) | collective-permute-done | bytes 800 | tf_op jit(solution)/shard_map/ppermute | solution.py:1398
  (312 shorter events, 173.9 us)
Async XLA Ops:
  7.3 62.9 %collective-permute-start.13 = (bf16[768,768]{1,0:T(8,128)(2,1)}, bf16[768,768]{1,0:T(8,128)(2,1)}, u32[]{:S(2)}, u32[]{:S(2)}) collective-permute-start(bf16[768,768]{1,0:T(8,128)(2,1)} %bitcast.93), channel_id=1, source_target_pairs={{0,1},{1,0},{2,3},{3,2},{4,5},{5,4},{6,7},{7,6},{8,9},{9,8},{10,11... | collective-permute-start | bytes 3538952 | tf_op jit(solution)/shard_map/ppermute | solution.py:1407
  19.5 50.7 %collective-permute-start.14 = (bf16[768,768]{1,0:T(8,128)(2,1)}, bf16[768,768]{1,0:T(8,128)(2,1)}, u32[]{:S(2)}, u32[]{:S(2)}) collective-permute-start(bf16[768,768]{1,0:T(8,128)(2,1)} %bitcast.95), channel_id=1, source_target_pairs={{0,1},{1,0},{2,3},{3,2},{4,5},{5,4},{6,7},{7,6},{8,9},{9,8},{10,11... | collective-permute-start | bytes 3538952 | tf_op jit(solution)/shard_map/ppermute | solution.py:1407
  27.7 16.9 %collective-permute-start.7 = (bf16[512,384]{1,0:T(8,128)(2,1)S(1)}, bf16[512,384]{1,0:T(8,128)(2,1)}, u32[]{:S(2)}, u32[]{:S(2)}) collective-permute-start(bf16[512,384]{1,0:T(8,128)(2,1)S(1)} %get-tuple-element.194.kv_one.rest_0_), channel_id=1, source_target_pairs={{0,4},{4,0},{8,12},{12,8},{1,5},{5,1},{9,13},{13,9},{2,6},{6,2},{1... | collective-permute-start | bytes 1179656 | tf_op jit(solution)/shard_map/ppermute | solution.py:1403
  29.3 19.5 %collective-permute-start.10 = (bf16[512,384]{1,0:T(8,128)(2,1)S(1)}, bf16[512,384]{1,0:T(8,128)(2,1)S(1)}, u32[]{:S(2)}, u32[]{:S(2)}) collective-permute-start(bf16[512,384]{1,0:T(8,128)(2,1)S(1)} %get-tuple-element.194.kv_one.rest_0_), channel_id=1, source_target_pairs={{0,8},{4,12},{8,0},{12,4},{1,9},{5,13},{9,1},{13,5},{2,10},{6,14},... | collective-permute-start | bytes 1179656 | tf_op jit(solution)/shard_map/ppermute | solution.py:1403
  29.8 18.5 %collective-permute-start.8 = (bf16[512,384]{1,0:T(8,128)(2,1)}, bf16[512,384]{1,0:T(8,128)(2,1)}, u32[]{:S(2)}, u32[]{:S(2)}) collective-permute-start(bf16[512,384]{1,0:T(8,128)(2,1)} %get-tuple-element.195.kv_two.rest_1_), channel_id=1, source_target_pairs={{0,8},{4,12},{8,0},{12,4},{1,9},{5,13},{9,1},{13,5},{2,10},{6,14},... | collective-permute-start | bytes 1179656 | tf_op jit(solution)/shard_map/ppermute | solution.py:1403
  44.6 21.0 %collective-permute-start.9 = (bf16[512,384]{1,0:T(8,128)(2,1)}, bf16[512,384]{1,0:T(8,128)(2,1)}, u32[]{:S(2)}, u32[]{:S(2)}) collective-permute-start(bf16[512,384]{1,0:T(8,128)(2,1)} %get-tuple-element.195.kv_two.rest_1_), channel_id=1, source_target_pairs={{0,4},{4,0},{8,12},{12,8},{1,5},{5,1},{9,13},{13,9},{2,6},{6,2},{1... | collective-permute-start | bytes 1179656 | tf_op jit(solution)/shard_map/ppermute | solution.py:1403
  48.3 17.8 %collective-permute-start.11 = (bf16[512,384]{1,0:T(8,128)(2,1)}, bf16[512,384]{1,0:T(8,128)(2,1)}, u32[]{:S(2)}, u32[]{:S(2)}) collective-permute-start(bf16[512,384]{1,0:T(8,128)(2,1)} %collective-permute-done.7.rest_2_), channel_id=1, source_target_pairs={{0,8},{4,12},{8,0},{12,4},{1,9},{5,13},{9,1},{13,5},{2,10},{6,14},... | collective-permute-start | bytes 1179656 | tf_op jit(solution)/shard_map/ppermute | solution.py:1403
  49.5 19.9 %collective-permute-start.12 = (bf16[512,384]{1,0:T(8,128)(2,1)}, bf16[512,384]{1,0:T(8,128)(2,1)}, u32[]{:S(2)}, u32[]{:S(2)}) collective-permute-start(bf16[512,384]{1,0:T(8,128)(2,1)} %collective-permute-done.8.rest_5_), channel_id=1, source_target_pairs={{0,4},{4,0},{8,12},{12,8},{1,5},{5,1},{9,13},{13,9},{2,6},{6,2},{1... | collective-permute-start | bytes 1179656 | tf_op jit(solution)/shard_map/ppermute | solution.py:1403
  65.6 22.8 %collective-permute-start.18 = (bf16[768,256]{1,0:T(8,128)(2,1)S(1)}, bf16[768,256]{1,0:T(8,128)(2,1)S(1)}, u32[]{:S(2)}, u32[]{:S(2)}) collective-permute-start(bf16[768,256]{1,0:T(8,128)(2,1)S(1)} %get-tuple-element.225.rest_8_.router_ref.rest_3_), channel_id=1, source_target_pairs={{0,1},{1,2},{2,3},{3,0},{4,5},{5,6},{6,7},{7,4},{8,9},{9,10},{10,1... | collective-permute-start | bytes 1179656 | tf_op jit(solution)/shard_map/ppermute | solution.py:1398
  66.0 35.8 %collective-permute-start.19 = (bf16[768,256]{1,0:T(8,128)(2,1)S(1)}, bf16[768,256]{1,0:T(8,128)(2,1)S(1)}, u32[]{:S(2)}, u32[]{:S(2)}) collective-permute-start(bf16[768,256]{1,0:T(8,128)(2,1)S(1)} %get-tuple-element.225.rest_8_.router_ref.rest_3_), channel_id=1, source_target_pairs={{0,3},{1,0},{2,1},{3,2},{4,7},{5,4},{6,5},{7,6},{8,11},{9,8},{10,9... | collective-permute-start | bytes 1179656 | tf_op jit(solution)/shard_map/ppermute | solution.py:1398
  69.4 41.4 %collective-permute-start.20 = (bf16[768,256]{1,0:T(8,128)(2,1)S(1)}, bf16[768,256]{1,0:T(8,128)(2,1)S(1)}, u32[]{:S(2)}, u32[]{:S(2)}) collective-permute-start(bf16[768,256]{1,0:T(8,128)(2,1)S(1)} %get-tuple-element.225.rest_8_.router_ref.rest_3_), channel_id=1, source_target_pairs={{0,2},{1,3},{2,0},{3,1},{4,6},{5,7},{6,4},{7,5},{8,10},{9,11},{10,... | collective-permute-start | bytes 1179656 | tf_op jit(solution)/shard_map/ppermute | solution.py:1398
  84.3 26.5 %collective-permute-start.15 = (bf16[256,384]{1,0:T(8,128)(2,1)}, bf16[256,384]{1,0:T(8,128)(2,1)S(1)}, u32[]{:S(2)}, u32[]{:S(2)}) collective-permute-start(bf16[256,384]{1,0:T(8,128)(2,1)} %get-tuple-element.217.rest_0_.rest_5_), channel_id=1, source_target_pairs={{0,1},{1,2},{2,3},{3,0},{4,5},{5,6},{6,7},{7,4},{8,9},{9,10},{10,1... | collective-permute-start | bytes 589832 | tf_op jit(solution)/shard_map/ppermute | solution.py:1398
  84.8 26.0 %collective-permute-start.16 = (bf16[256,384]{1,0:T(8,128)(2,1)}, bf16[256,384]{1,0:T(8,128)(2,1)S(1)}, u32[]{:S(2)}, u32[]{:S(2)}) collective-permute-start(bf16[256,384]{1,0:T(8,128)(2,1)} %get-tuple-element.217.rest_0_.rest_5_), channel_id=1, source_target_pairs={{0,3},{1,0},{2,1},{3,2},{4,7},{5,4},{6,5},{7,6},{8,11},{9,8},{10,9... | collective-permute-start | bytes 589832 | tf_op jit(solution)/shard_map/ppermute | solution.py:1398
  88.4 30.8 %collective-permute-start.17 = (bf16[256,384]{1,0:T(8,128)(2,1)}, bf16[256,384]{1,0:T(8,128)(2,1)S(1)}, u32[]{:S(2)}, u32[]{:S(2)}) collective-permute-start(bf16[256,384]{1,0:T(8,128)(2,1)} %get-tuple-element.217.rest_0_.rest_5_), channel_id=1, source_target_pairs={{0,2},{1,3},{2,0},{3,1},{4,6},{5,7},{6,4},{7,5},{8,10},{9,11},{10,... | collective-permute-start | bytes 589832 | tf_op jit(solution)/shard_map/ppermute | solution.py:1398
  119.8 27.7 %all-to-all-start = ((bf16[8,160,768]{2,1,0:T(8,128)(2,1)}), bf16[8,160,768]{2,1,0:T(8,128)(2,1)S(1)}, u32[]{:S(2)}, u32[]{:S(2)}) async-start(bf16[8,160,768]{2,1,0:T(8,128)(2,1)} %bitcast.31), calls=%async_computation | async-start | bytes 3932160 | tf_op jit(solution)/shard_map/all_to_all | solution.py:1460
  208.2 30.2 %all-to-all-start.2 = ((bf16[8,160,768]{2,1,0:T(8,128)(2,1)}), bf16[8,160,768]{2,1,0:T(8,128)(2,1)}, u32[]{:S(2)}, u32[]{:S(2)}) async-start(bf16[8,160,768]{2,1,0:T(8,128)(2,1)} %bitcast.86), calls=%async_computation.2 | async-start | bytes 3932160 | tf_op jit(solution)/shard_map/all_to_all | solution.py:1460
  222.5 34.4 %collective-permute-start.26 = (bf16[768,768]{1,0:T(8,128)(2,1)}, bf16[768,768]{1,0:T(8,128)(2,1)S(1)}, u32[]{:S(2)}, u32[]{:S(2)}) collective-permute-start(bf16[768,768]{1,0:T(8,128)(2,1)} %fusion.12), channel_id=1, source_target_pairs={{0,1},{1,0},{2,3},{3,2},{4,5},{5,4},{6,7},{7,6},{8,9},{9,8},{10,11... | collective-permute-start | bytes 3538952 | tf_op jit(solution)/shard_map/ppermute | solution.py:1407
  259.9 27.2 %all-to-all-start.3 = ((bf16[8,160,768]{2,1,0:T(8,128)(2,1)}), bf16[8,160,768]{2,1,0:T(8,128)(2,1)S(1)}, u32[]{:S(2)}, u32[]{:S(2)}) async-start(bf16[8,160,768]{2,1,0:T(8,128)(2,1)} %bitcast.41), calls=%async_computation.3 | async-start | bytes 3932160 | tf_op jit(solution)/shard_map/all_to_all | solution.py:1460
  268.6 17.7 %collective-permute-start.27 = (bf16[256,768]{1,0:T(8,128)(2,1)S(1)}, bf16[256,768]{1,0:T(8,128)(2,1)S(1)}, u32[]{:S(2)}, u32[]{:S(2)}) collective-permute-start(bf16[256,768]{1,0:T(8,128)(2,1)S(1)} %pad_maximum_fusion), channel_id=1, source_target_pairs={{0,1},{1,2},{2,3},{3,0},{4,5},{5,6},{6,7},{7,4},{8,9},{9,10},{10,1... | collective-permute-start | bytes 1179656 | tf_op jit(solution)/shard_map/ppermute | solution.py:1398
  306.7 53.9 %all-to-all-start.4 = ((bf16[4,256,768]{2,1,0:T(8,128)(2,1)}), bf16[4,256,768]{2,1,0:T(8,128)(2,1)S(1)}, u32[]{:S(2)}, u32[]{:S(2)}) async-start(bf16[4,256,768]{2,1,0:T(8,128)(2,1)} %bitcast.88), calls=%async_computation.4 | async-start | bytes 3145728 | tf_op jit(solution)/shard_map/all_to_all | solution.py:1615
  327.1 29.8 %collective-permute-start.33 = (bf16[512,384]{1,0:T(8,128)(2,1)}, bf16[512,384]{1,0:T(8,128)(2,1)S(1)}, u32[]{:S(2)}, u32[]{:S(2)}) collective-permute-start(bf16[512,384]{1,0:T(8,128)(2,1)} %get-tuple-element.285), channel_id=1, source_target_pairs={{0,4},{4,0},{8,12},{12,8},{1,5},{5,1},{9,13},{13,9},{2,6},{6,2},{1... | collective-permute-start | bytes 1179656 | tf_op jit(solution)/shard_map/ppermute | solution.py:1403
  328.2 32.4 %collective-permute-start.34 = (bf16[384,1024]{1,0:T(8,128)(2,1)}, bf16[384,1024]{1,0:T(8,128)(2,1)S(1)}, u32[]{:S(2)}, u32[]{:S(2)}) collective-permute-start(bf16[384,1024]{1,0:T(8,128)(2,1)} %get-tuple-element.287), channel_id=1, source_target_pairs={{0,4},{4,0},{8,12},{12,8},{1,5},{5,1},{9,13},{13,9},{2,6},{6,2},{1... | collective-permute-start | bytes 2359304 | tf_op jit(solution)/shard_map/ppermute | solution.py:1403
  329.1 52.9 %collective-permute-start.39 = (bf16[768,768]{1,0:T(8,128)(2,1)}, bf16[768,768]{1,0:T(8,128)(2,1)}, u32[]{:S(2)}, u32[]{:S(2)}) collective-permute-start(bf16[768,768]{1,0:T(8,128)(2,1)} %fusion.15), channel_id=1, source_target_pairs={{0,1},{1,0},{2,3},{3,2},{4,5},{5,4},{6,7},{7,6},{8,9},{9,8},{10,11... | collective-permute-start | bytes 3538952 | tf_op jit(solution)/shard_map/ppermute | solution.py:1407
  331.2 27.6 %collective-permute-start.32 = (bf16[512,384]{1,0:T(8,128)(2,1)}, bf16[512,384]{1,0:T(8,128)(2,1)S(1)}, u32[]{:S(2)}, u32[]{:S(2)}) collective-permute-start(bf16[512,384]{1,0:T(8,128)(2,1)} %get-tuple-element.283), channel_id=1, source_target_pairs={{0,8},{4,12},{8,0},{12,4},{1,9},{5,13},{9,1},{13,5},{2,10},{6,14},... | collective-permute-start | bytes 1179656 | tf_op jit(solution)/shard_map/ppermute | solution.py:1403
  362.0 70.5 %all-to-all-start.5 = ((bf16[4,256,768]{2,1,0:T(8,128)(2,1)}), bf16[4,256,768]{2,1,0:T(8,128)(2,1)S(1)}, u32[]{:S(2)}, u32[]{:S(2)}) async-start(bf16[4,256,768]{2,1,0:T(8,128)(2,1)} %bitcast.45), calls=%async_computation.5 | async-start | bytes 3145728 | tf_op jit(solution)/shard_map/all_to_all | solution.py:1635
  365.7 16.4 %collective-permute-start.35 = (bf16[512,384]{1,0:T(8,128)(2,1)}, bf16[512,384]{1,0:T(8,128)(2,1)S(1)}, u32[]{:S(2)}, u32[]{:S(2)}) collective-permute-start(bf16[512,384]{1,0:T(8,128)(2,1)} %get-tuple-element.293), channel_id=1, source_target_pairs={{0,4},{4,0},{8,12},{12,8},{1,5},{5,1},{9,13},{13,9},{2,6},{6,2},{1... | collective-permute-start | bytes 1179656 | tf_op jit(solution)/shard_map/ppermute | solution.py:1403
  402.6 20.9 %collective-permute-start.44 = (bf16[256,768]{1,0:T(8,128)(2,1)S(1)}, bf16[256,768]{1,0:T(8,128)(2,1)S(1)}, u32[]{:S(2)}, u32[]{:S(2)}) collective-permute-start(bf16[256,768]{1,0:T(8,128)(2,1)S(1)} %pad_maximum_fusion.3), channel_id=1, source_target_pairs={{0,3},{1,0},{2,1},{3,2},{4,7},{5,4},{6,5},{7,6},{8,11},{9,8},{10,9... | collective-permute-start | bytes 1179656 | tf_op jit(solution)/shard_map/ppermute | solution.py:1398
  402.9 39.6 %collective-permute-start.42 = (f32[416,640]{1,0:T(8,128)}, f32[416,640]{1,0:T(8,128)}, u32[]{:S(2)}, u32[]{:S(2)}) collective-permute-start(f32[416,640]{1,0:T(8,128)} %get-tuple-element.316), channel_id=1, source_target_pairs={{0,16},{16,0},{1,17},{17,1},{2,18},{18,2},{3,19},{19,3},{4,20},{20... | collective-permute-start | bytes 3194888 | tf_op jit(solution)/shard_map/ppermute | solution.py:1479
  410.6 21.9 %collective-permute-start.43 = (bf16[256,768]{1,0:T(8,128)(2,1)S(1)}, bf16[256,768]{1,0:T(8,128)(2,1)S(1)}, u32[]{:S(2)}, u32[]{:S(2)}) collective-permute-start(bf16[256,768]{1,0:T(8,128)(2,1)S(1)} %pad_maximum_fusion.2), channel_id=1, source_target_pairs={{0,1},{1,2},{2,3},{3,0},{4,5},{5,6},{6,7},{7,4},{8,9},{9,10},{10,1... | collective-permute-start | bytes 1179656 | tf_op jit(solution)/shard_map/ppermute | solution.py:1398
  437.5 47.2 %all-to-all-start.6 = ((bf16[4,288,768]{2,1,0:T(8,128)(2,1)}), bf16[4,288,768]{2,1,0:T(8,128)(2,1)S(1)}, u32[]{:S(2)}, u32[]{:S(2)}) async-start(bf16[4,288,768]{2,1,0:T(8,128)(2,1)} %get-tuple-element.331), calls=%async_computation.6 | async-start | bytes 3538944 | tf_op jit(solution)/shard_map/all_to_all | solution.py:1657
  461.6 22.0 %collective-permute-start.51 = (f32[96,2]{0,1:T(2,128)S(1)}, f32[96,2]{0,1:T(2,128)S(1)}, u32[]{:S(2)}, u32[]{:S(2)}) collective-permute-start(f32[96,2]{0,1:T(2,128)S(1)} %pad_maximum_fusion.6), channel_id=1, source_target_pairs={{0,2},{1,3},{2,0},{3,1},{4,6},{5,7},{6,4},{7,5},{8,10},{9,11},{10,... | collective-permute-start | bytes 2312 | tf_op jit(solution)/shard_map/ppermute | solution.py:1398
  464.0 19.6 %collective-permute-start.52 = (f32[96,2]{0,1:T(2,128)S(1)}, f32[96,2]{0,1:T(2,128)S(1)}, u32[]{:S(2)}, u32[]{:S(2)}) collective-permute-start(f32[96,2]{0,1:T(2,128)S(1)} %pad_maximum_fusion.6), channel_id=1, source_target_pairs={{0,3},{1,0},{2,1},{3,2},{4,7},{5,4},{6,5},{7,6},{8,11},{9,8},{10,9... | collective-permute-start | bytes 2312 | tf_op jit(solution)/shard_map/ppermute | solution.py:1398
  (100 other events, 924.7 us)
